TPU v7x, 32 devices: a whole 2x2x4 slice. The times are simulated.
32 devices in a mesh: dp: 8 (over z, x), tensor: 4 (over y, core).
Axes of the slice: x: 2, y: 2, z: 4, core: 2. Of those that a mesh axis runs over, the one named last changes fastest.
Arguments:
- tokens: bfloat16 [16384, 1024], P(('dp', 'tensor')), may hold values from -6 to 6
- ln1_gain: float32 [1024], replicated, may hold values from 0.1 to 1.9
- ln1_bias: float32 [1024], replicated, may hold values from -2 to 2
- ln2_gain: float32 [1024], replicated, may hold values from 0.1 to 1.9
- ln2_bias: float32 [1024], replicated, may hold values from -2 to 2
- w_qkv: bfloat16 [3, 1024, 1024], P(None, None, 'tensor'), may hold values from -0.1875 to 0.1875
- w_out: bfloat16 [1024, 1024], P('tensor'), may hold values from -1.5 to 1.5
- w_up: bfloat16 [1024, 4096], P(None, 'tensor'), may hold values from -0.1875 to 0.1875
- w_down: bfloat16 [4096, 1024], P('tensor'), may hold values from -0.09375 to 0.09375
- feature_scale: float32 [16, 64], P('tensor'), may hold values from 0.1 to 0.5
- feature_weight: float32 [16, 64], P('tensor'), may hold values from 0.5 to 2
- lengths: int32 [8, 3], P('dp'), may hold values from 1 to 20, 32 in all within a row
- cotangent: bfloat16 [16384, 1024], P(('dp', 'tensor')), may hold values from -6 to 6
Outputs:
- mixed_out: bfloat16 [16384, 1024], P(('dp', 'tensor'))
- input_grad: bfloat16 [16384, 1024], P(('dp', 'tensor'))
- grad_ln1_gain: float32 [1024], replicated
- grad_ln1_bias: float32 [1024], replicated
- grad_ln2_gain: float32 [1024], replicated
- grad_ln2_bias: float32 [1024], replicated
- grad_qkv: float32 [3, 1024, 1024], P(None, None, 'tensor')
- grad_out: float32 [1024, 1024], P('tensor')
- grad_up: float32 [1024, 4096], P(None, 'tensor')
- grad_down: float32 [4096, 1024], P('tensor')
- grad_scale: float32 [16, 64], P('tensor')
- grad_weight: float32 [16, 64], P('tensor')
Inputs may be any that keep to these rules, and one draw needn't show every extreme that they name: `lengths`: each row sums to 32, and its largest entry is exactly 20.
All inputs are finite; a program needn't handle non-finite values.
Results may differ from a plain program's by a relative error of at most 0.0035.
The roundings to bfloat16 on the way count: a program that leaves them out, or rounds other values in their place, can miss the bound.
Values may be sent and summed in bfloat16 or wider, within the bound.
A program may use at most 192 MiB of HBM per device.

v0:
```python
import math

import jax
import jax.numpy as jnp
from jax import lax
from jax.sharding import PartitionSpec as P

HEAD_DIM = 64
ROT = 16
BLOCK = 64


PRECISE_MODE = lax.Precision.HIGHEST


def bf_rounded(values_in):
    exact = lax.optimization_barrier(values_in.astype(jnp.bfloat16)).astype(jnp.float32)
    return values_in + lax.stop_gradient(exact - values_in)


def dct_table(order):
    freq_rows = jnp.arange(order, dtype=jnp.float32)[:, None]
    dim_cols = jnp.arange(order, dtype=jnp.float32)[None, :]
    cosines = jnp.cos(math.pi * (dim_cols + 0.5) * freq_rows / order) * math.sqrt(2.0 / order)
    return cosines * jnp.where(freq_rows == 0, math.sqrt(0.5), 1.0)


def rotate(field_rows, positions):
    half_rot = ROT // 2
    frequency = 10000.0 ** (-jnp.arange(half_rot, dtype=jnp.float32) * 2.0 / ROT)
    angles = positions.astype(jnp.float32)[:, None] * frequency[None, :]
    cosine = jnp.cos(angles)[:, None, :]
    sinusoid = jnp.sin(angles)[:, None, :]
    first_half = field_rows[..., :half_rot]
    second_half = field_rows[..., half_rot:ROT]
    passive = field_rows[..., ROT:]
    return jnp.concatenate(
        [
            first_half * cosine - second_half * sinusoid,
            second_half * cosine + first_half * sinusoid,
            passive,
        ],
        -1,
    )


def features(field_rows, table, scale_part, weight_part):
    spectrum = jnp.einsum("ghd,fd->ghf", field_rows, table, precision=PRECISE_MODE)
    return weight_part[None] * jnp.exp(scale_part[None] * spectrum)


def linear_mixer(projected, scale_part, weight_part, lengths_row):
    group_rows = projected.shape[0]
    head_count = projected.shape[2]
    head_width = projected.shape[3]
    blocks = group_rows // BLOCK
    starts = jnp.cumsum(lengths_row) - lengths_row
    block_ids = jnp.arange(blocks, dtype=jnp.int32)
    started = starts[None, :] <= block_ids[:, None]
    segment = jnp.sum(started.astype(jnp.int32), 1)
    seg_start = jnp.max(jnp.where(started, starts[None, :], 0), 1)
    positions = (
        jnp.arange(group_rows, dtype=jnp.int32)
        - jnp.repeat(seg_start, BLOCK, total_repeat_length=group_rows) * BLOCK
    )
    table = dct_table(head_width)
    queries = rotate(projected[:, 0], positions)
    keys_rot = rotate(projected[:, 1], positions)
    values = bf_rounded(projected[:, 2]).reshape(blocks, BLOCK, head_count, head_width)
    feat_q = bf_rounded(features(queries, table, scale_part, weight_part)).reshape(
        blocks, BLOCK, head_count, head_width
    )
    feat_k = bf_rounded(features(keys_rot, table, scale_part, weight_part)).reshape(
        blocks, BLOCK, head_count, head_width
    )
    causal = jnp.arange(BLOCK)[:, None] >= jnp.arange(BLOCK)[None, :]
    scores = jnp.einsum("bthf,bshf->bhts", feat_q, feat_k, precision=PRECISE_MODE)
    scores = jnp.where(causal[None, None], scores, 0.0)
    states = jnp.einsum("bshf,bshd->bhfd", feat_k, values, precision=PRECISE_MODE)
    totals = jnp.sum(feat_k, 1)
    earlier = jnp.where(
        (block_ids[None, :] < block_ids[:, None]) & (segment[None, :] == segment[:, None]), 1.0, 0.0
    ).astype(jnp.float32)
    carried = jnp.einsum("ac,chfd->ahfd", earlier, states, precision=PRECISE_MODE)
    carried_sum = jnp.einsum("ac,chf->ahf", earlier, totals, precision=PRECISE_MODE)
    numerator = jnp.einsum("bthf,bhfd->bthd", feat_q, bf_rounded(carried), precision=PRECISE_MODE)
    numerator = numerator + jnp.einsum(
        "bhts,bshd->bthd", bf_rounded(scores), values, precision=PRECISE_MODE
    )
    denominator = jnp.einsum("bthf,bhf->bth", feat_q, carried_sum, precision=PRECISE_MODE)
    denominator = denominator + jnp.swapaxes(jnp.sum(scores, -1), 1, 2)
    return (numerator / denominator[..., None]).reshape(group_rows, head_count * head_width)


def layer_norm(row_block, gain, bias):
    average = jnp.mean(row_block, -1, keepdims=True)
    centered = row_block - average
    variance = jnp.mean(centered * centered, -1, keepdims=True)
    return centered * lax.rsqrt(variance + 1e-05) * gain + bias


def exact_gelu(values_in):
    return jax.nn.gelu(values_in, approximate=False)


def shards(
    tokens,
    ln1_gain,
    ln1_bias,
    ln2_gain,
    ln2_bias,
    w_qkv,
    w_out,
    w_up,
    w_down,
    feature_scale,
    feature_weight,
    lengths,
    cotangent,
):
    token_rows = tokens.astype(jnp.float32)
    normed_one = layer_norm(token_rows, ln1_gain, ln1_bias).astype(jnp.bfloat16)
    normed_two = layer_norm(token_rows, ln2_gain, ln2_bias).astype(jnp.bfloat16)
    all_one, all_two = (
        lax.all_gather(normed_one, "tensor", axis=0, tiled=True),
        lax.all_gather(normed_two, "tensor", axis=0, tiled=True),
    )
    group_rows = all_one.shape[0]
    head_count = feature_scale.shape[0]
    projected = jnp.einsum("gd,sde->gse", all_one, w_qkv, preferred_element_type=jnp.float32)
    projected = projected.reshape(group_rows, 3, head_count, HEAD_DIM)
    lengths_row = lengths[0]

    def local_mixer(proj_field, scale_part, weight_part):
        return linear_mixer(proj_field, scale_part, weight_part, lengths_row)

    mixed_full, mixer_back = jax.vjp(local_mixer, projected, feature_scale, feature_weight)
    mixed = mixed_full.astype(jnp.bfloat16)
    up_proj = jnp.dot(all_two, w_up, preferred_element_type=jnp.float32)
    activated, gelu_back = jax.vjp(exact_gelu, up_proj)
    hidden = activated.astype(jnp.bfloat16)
    branches = lax.psum_scatter(
        jnp.dot(mixed, w_out, preferred_element_type=jnp.float32)
        + jnp.dot(hidden, w_down, preferred_element_type=jnp.float32),
        "tensor",
        scatter_dimension=0,
        tiled=True,
    )
    mixed_out = (token_rows + branches).astype(jnp.bfloat16)
    all_one, all_two, all_cot = (
        lax.all_gather(normed_one, "tensor", axis=0, tiled=True),
        lax.all_gather(normed_two, "tensor", axis=0, tiled=True),
        lax.all_gather(cotangent, "tensor", axis=0, tiled=True),
    )
    d_hidden = jnp.einsum("gd,fd->gf", all_cot, w_down, preferred_element_type=jnp.float32)
    grad_down = jnp.einsum("gf,gd->fd", hidden, all_cot, preferred_element_type=jnp.float32)
    (d_up,) = gelu_back(d_hidden)
    d_up_low = d_up.astype(jnp.bfloat16)
    grad_up = jnp.einsum("gd,gf->df", all_two, d_up_low, preferred_element_type=jnp.float32)
    d_second = jnp.einsum("gf,df->gd", d_up_low, w_up, preferred_element_type=jnp.float32)
    d_mixed = jnp.einsum("gd,id->gi", all_cot, w_out, preferred_element_type=jnp.float32)
    grad_out = jnp.einsum("gi,gd->id", mixed, all_cot, preferred_element_type=jnp.float32)
    d_proj, grad_scale, grad_weight = mixer_back(d_mixed)
    d_proj_low = d_proj.reshape(group_rows, 3, head_count * HEAD_DIM).astype(jnp.bfloat16)
    grad_qkv = jnp.einsum("gd,gse->sde", all_one, d_proj_low, preferred_element_type=jnp.float32)
    d_first = jnp.einsum("gse,sde->gd", d_proj_low, w_qkv, preferred_element_type=jnp.float32)
    d_one_rows, d_two_rows = (
        lax.psum_scatter(d_first, "tensor", scatter_dimension=0, tiled=True),
        lax.psum_scatter(d_second, "tensor", scatter_dimension=0, tiled=True),
    )
    unused_one, norm_back_one = jax.vjp(layer_norm, token_rows, ln1_gain, ln1_bias)
    unused_two, norm_back_two = jax.vjp(layer_norm, token_rows, ln2_gain, ln2_bias)
    d_rows_one, d_gain_one, d_bias_one = norm_back_one(d_one_rows)
    d_rows_two, d_gain_two, d_bias_two = norm_back_two(d_two_rows)
    input_grad = (cotangent.astype(jnp.float32) + d_rows_one + d_rows_two).astype(jnp.bfloat16)
    d_gain_one, d_bias_one, d_gain_two, d_bias_two = lax.psum(
        (d_gain_one, d_bias_one, d_gain_two, d_bias_two), "tensor"
    )
    (
        grad_qkv,
        grad_out,
        grad_up,
        grad_down,
        grad_scale,
        grad_weight,
        d_gain_one,
        d_bias_one,
        d_gain_two,
        d_bias_two,
    ) = lax.psum(
        (
            grad_qkv,
            grad_out,
            grad_up,
            grad_down,
            grad_scale,
            grad_weight,
            d_gain_one,
            d_bias_one,
            d_gain_two,
            d_bias_two,
        ),
        "dp",
    )
    return (
        mixed_out,
        input_grad,
        d_gain_one,
        d_bias_one,
        d_gain_two,
        d_bias_two,
        grad_qkv,
        grad_out,
        grad_up,
        grad_down,
        grad_scale,
        grad_weight,
    )


def solution(mesh):
    placed = (
        P(("dp", "tensor"), None),
        P(),
        P(),
        P(),
        P(),
        P(None, None, "tensor"),
        P("tensor", None),
        P(None, "tensor"),
        P("tensor", None),
        P("tensor", None),
        P("tensor", None),
        P("dp", None),
        P(("dp", "tensor"), None),
    )
    return jax.shard_map(
        shards,
        mesh=mesh,
        in_specs=placed,
        out_specs=(
            P(("dp", "tensor"), None),
            P(("dp", "tensor"), None),
            P(),
            P(),
            P(),
            P(),
            P(None, None, "tensor"),
            P("tensor", None),
            P(None, "tensor"),
            P("tensor", None),
            P("tensor", None),
            P("tensor", None),
        ),
        check_vma=False,
    )
```

profile of v0, /device:TPU:0, one launch (start us, length us, event | category | flops | bytes accessed | tf_op | source)
XLA Modules:
  0.0 1053.5 jit_solution(11502069826752679613)
XLA Ops:
  22.8 15.7 %fusion.129 = f32[2048]{0:T(1024)S(1)} fusion(pred[2048]{0:T(1024)(128)(4,1)S(1)} %get-tuple-element.110, pred[2048]{0:T(1024)(128)(4,1)S(1)} %get-tuple-element.109, pred[2048]{0:T(1024)(128)(4,1)S(1)} %get-tuple-element.108, pred[2048]{0:T(1024)(128)(4,1)S(1)} %get-tuple-element.107, pred[2048]{0:T(1024)(128)(4,1)S(1)} %get-tuple-element.106, ...), kind=kLoop, calls=%fused_computation.221 | loop fusion | flops 75776 | bytes 75940 | tf_op jit(solution)/shard_map/jvp()/convert_element_type | solution.py:31
  38.8 12.9 %all-gather.4.cloned.1.call-done = bf16[2048,1024]{1,0:T(8,128)(2,1)} async-done(((bf16[512,1024]{1,0:T(8,128)(2,1)}), bf16[2048,1024]{1,0:T(8,128)(2,1)}) %all-gather.4.cloned.1.call-update) | async-done | bytes 4194320 | tf_op jit(solution)/shard_map/all_gather | solution.py:125
  89.6 10.6 %select_reduce_fusion = (f32[32,4,64]{2,1,0:T(4,128)}, f32[32,4,64,64]{2,3,1,0:T(8,128)S(1)}) fusion(pred[64,64]{0,1:T(8,128)(4,1)S(1)} %iota_compare_fusion, f32[32,64,4,64]{3,1,2,0:T(8,128)} %copy.149, f32[32,64,4,64]{3,1,2,0:T(8,128)} %copy.151), kind=kOutput, calls=%fused_computation.59 | convolution fusion | flops 403693568 | bytes 6328320 | tf_op jit(solution)/shard_map/jvp(bthf,bshf->bhts)/dot_general | solution.py:77
  125.6 19.2 %fusion.10 = f32[32,4,64,64]{3,2,1,0:T(8,128)} fusion(f32[32,64,4,64]{1,0,3,2:T(8,128)} %reshape.310, f32[32,64,4,64]{1,0,3,2:T(8,128)} %reshape.311, f32[32,64,4]{1,2,0:T(4,128)S(1)} %get-tuple-element.130), kind=kOutput, calls=%fused_computation.27 | convolution fusion | flops 403177472 | bytes 6324224 | tf_op jit(solution)/shard_map/transpose(jvp(bthf,bhfd->bthd))/dot_general | solution.py:86
  144.8 11.7 %fusion.12 = f32[32,4,64,64]{3,2,1,0:T(8,128)} fusion(bf16[32,4,64,64]{2,3,1,0:T(8,128)(2,1)S(1)} %copy-done.24, f32[32,4,64,64]{2,3,1,0:T(8,128)S(1)} %copy-done.11, pred[64,64]{0,1:T(8,128)(4,1)S(1)} %iota_compare_fusion, f32[32,64,4,64]{1,0,3,2:T(8,128)S(1)} %copy-done.30, f32[32,64,4]{1,2,0:T(4,128)S(1)} %get-tuple-element.130), kind=kOutput, calls=%fused_computation.29 | convolution fusion | flops 405274624 | bytes 7376896 | tf_op jit(solution)/shard_map/transpose(jvp(bhts,bshd->bthd))/dot_general | solution.py:87
  165.0 15.7 %fusion.40 = f32[32,4,64,64]{3,2,1,0:T(8,128)} fusion(f32[32,64,4,64]{3,1,2,0:T(8,128)} %copy.151, f32[32,64,4,64]{1,0,3,2:T(8,128)} %reshape.309), kind=kOutput, calls=%fused_computation.65 | convolution fusion | flops 402653184 | bytes 6291456 | tf_op jit(solution)/shard_map/jvp(bshf,bshd->bhfd)/dot_general | solution.py:79
  180.8 9.4 fusion.36
  196.2 10.4 add_bitcast_fusion.1
  230.0 15.0 %fusion.15 = (f32[32,64,4]{1,2,0:T(4,128)S(1)}, bf16[32,64,4,64]{1,3,2,0:T(8,128)(2,1)}) fusion(f32[32,64,4,64]{1,0,3,2:T(8,128)S(1)} %copy-done.31, f32[32,64,4]{1,2,0:T(4,128)S(1)} %copy-done.46, f32[32,64,4]{1,2,0:T(4,128)S(1)} %copy-done.45, f32[32,4,64,64]{3,2,1,0:T(8,128)S(1)} %copy-done.29, f32[32,64,4,64]{3,1,2,0:T(8,128)S(1)} %copy-done.6, ...), kind=kOutput, calls=%fused_computation.34 | convolution fusion | flops 405790720 | bytes 9535488 | tf_op jit(solution)/shard_map/jvp(bthf,bhfd->bthd)/dot_general | solution.py:86
  245.0 10.9 %fusion.6 = f32[32,4,64,64]{2,3,1,0:T(8,128)} fusion(f32[32,4,64,64]{3,0,2,1:T(8,128)} %subtract_add_fusion.1, f32[32,64,4,64]{1,0,3,2:T(8,128)S(1)} %copy-done.31, f32[32,64,4]{1,2,0:T(4,128)S(1)} %copy-done.45), kind=kOutput, calls=%fused_computation.23 | convolution fusion | flops 403177472 | bytes 6324224 | tf_op jit(solution)/shard_map/transpose(jvp(bthf,bhfd->bthd))/dot_general | solution.py:86
  256.0 13.3 %fusion.8 = f32[32,4,64,64]{2,3,1,0:T(8,128)S(1)} fusion(f32[32,64,4,64]{1,0,3,2:T(8,128)S(1)} %copy-done.4, f32[32,64,4,64]{1,0,3,2:T(8,128)S(1)} %copy-done.31, f32[32,64,4]{1,2,0:T(4,128)S(1)} %copy-done.45), kind=kOutput, calls=%fused_computation.25 | convolution fusion | flops 403177472 | bytes 6324224 | tf_op jit(solution)/shard_map/transpose(jvp(bhts,bshd->bthd))/dot_general | solution.py:87
  269.3 11.2 %add_bitcast_fusion = f32[32,64,4,64]{1,3,2,0:T(8,128)S(1)} fusion(f32[32,4,64,64]{2,3,1,0:T(8,128)} %fusion.6, f32[32,64,4,64]{3,1,2,0:T(8,128)S(1)} %copy-done.2, f32[32,4,64,64]{2,3,1,0:T(8,128)S(1)} %fusion.8, f32[32,4,64]{2,1,0:T(4,128)S(1)} %copy.175, f32[32,4,64]{2,1,0:T(4,128)S(1)} %get-tuple-element.158, pred[64,64]{0,1:T(8,128)(4,1)S(1)} %iota_compare_fusion), kind=kOutput, calls=%fused_computation.43 | convolution fusion | flops 405274624 | bytes 8458240 | tf_op jit(solution)/shard_map/transpose(jvp(bthf,bshf->bhts))/dot_general | solution.py:77
  295.6 9.4 fusion.35
  305.0 12.7 %bitcast_add_fusion = f32[32,64,4,64]{1,3,2,0:T(8,128)S(1)} fusion(f32[32,4,64,64]{2,3,1,0:T(8,128)S(1)} %fusion.35, f32[32,64,4,64]{1,0,3,2:T(8,128)S(1)} %copy-done.5, f32[32,4,64,64]{3,0,2,1:T(8,128)S(1)} %copy-done.15, f32[32,4,64]{2,1,0:T(4,128)S(1)} %copy.166), kind=kOutput, calls=%fused_computation.22 | convolution fusion | flops 403701760 | bytes 8421376 | tf_op jit(solution)/shard_map/transpose(jvp(bshf,bshd->bhfd))/dot_general | solution.py:79
  351.9 24.4 %add_convert_fusion = (bf16[2048,1024]{1,0:T(8,128)(2,1)}, f32[2048,1024]{1,0:T(8,128)}) fusion(f32[2048,1024]{1,0:T(8,128)S(1)} %fusion.171, bf16[2048,1024]{1,0:T(8,128)(2,1)S(1)} %copy-done.59, bf16[1024,1024]{1,0:T(8,128)(2,1)S(1)} %copy-done), kind=kOutput, calls=%fused_computation.2 | convolution fusion | flops 4445962240 | bytes 27262976 | tf_op jit(solution)/shard_map/gd,fd->gf/dot_general | solution.py:155
  376.3 10.2 multiply_convert_fusion
  412.1 9.1 convolution_bitcast_fusion
  421.3 10.6 %fusion.175 = f32[2048,1024]{1,0:T(8,128)} fusion(bf16[2048,1024]{1,0:T(8,128)(2,1)} %get-tuple-element.131, bf16[1024,1024]{1,0:T(8,128)(2,1)} %param.22), kind=kOutput, calls=%fused_computation.278 | convolution fusion | flops 4294967296 | bytes 14680064 | tf_op jit(solution)/shard_map/gf,df->gd/dot_general | solution.py:160
  448.9 363.8 %all-reduce.14.cloned.1.call-done = (f32[3,1024,256]{1,2,0:T(8,128)}, f32[256,1024]{1,0:T(8,128)}, f32[1024,1024]{1,0:T(8,128)}, f32[1024,1024]{1,0:T(8,128)}) async-done(((f32[3,1024,256]{1,2,0:T(8,128)}, f32[256,1024]{1,0:T(8,128)}, f32[1024,1024]{1,0:T(8,128)}, f32[1024,1024]{1,0:T(8,128)}), (f32[3,1024,256]{1,2,0:T(8,128)}, f32[256,1024]{1,0:T(8,128)}, f32[1024,1024]{1,0:T(8,128)}, ...) | async-done | bytes 12582928 | tf_op jit(solution)/shard_map/psum | solution.py:190
  816.3 69.8 %reduce-scatter.6.cloned.1.call-done = f32[512,1024]{1,0:T(8,128)} async-done(((f32[2048,1024]{1,0:T(8,128)}), f32[512,1024]{1,0:T(8,128)}) %reduce-scatter.6.cloned.1.call-update) | async-done | bytes 2097168 | tf_op jit(solution)/shard_map/reduce_scatter | solution.py:168
  886.0 74.2 %reduce-scatter.8.cloned.1.call-done = f32[512,1024]{1,0:T(8,128)} async-done(((f32[2048,1024]{1,0:T(8,128)}), f32[512,1024]{1,0:T(8,128)}) %reduce-scatter.8.cloned.1.call-update) | async-done | bytes 2097168 | tf_op jit(solution)/shard_map/reduce_scatter | solution.py:169
  965.7 10.1 all-reduce.11
  975.8 37.7 %all-reduce.9 = (f32[1024]{0:T(1024)}, f32[1024]{0:T(1024)}, f32[1024]{0:T(1024)}, f32[1024]{0:T(1024)}, f32[4,64]{1,0:T(4,128)}, /*index=5*/f32[4,64]{1,0:T(4,128)}) all-reduce(f32[1024]{0:T(1024)S(1)} %get-tuple-element.125, f32[1024]{0:T(1024)S(1)} %get-tuple-element.126, ...), channel_id=1, replica_groups=mesh['dp'=8,'tensor'=4] {'dp'}, use_global_device_ids=true, to_apply=%region_17.18 | all-reduce | flops 4608 | bytes 36864 | tf_op jit(solution)/shard_map/psum | solution.py:190
  1013.6 21.2 %reduce-scatter.4.cloned.1.call-done = f32[512,1024]{1,0:T(8,128)} async-done(((f32[2048,1024]{1,0:T(8,128)}), f32[512,1024]{1,0:T(8,128)}) %reduce-scatter.4.cloned.1.call-update) | async-done | bytes 2097168 | tf_op jit(solution)/shard_map/reduce_scatter | solution.py:142
  (230 shorter events, 229.0 us)
Async XLA Ops:
  7.2 344.7 %copy-start = (bf16[1024,1024]{1,0:T(8,128)(2,1)S(1)}, bf16[1024,1024]{1,0:T(8,128)(2,1)}, u32[]{:S(2)}) copy-start(bf16[1024,1024]{1,0:T(8,128)(2,1)} %param.23) | copy-start | bytes 6291460
  7.2 44.4 %all-gather.4.cloned.1.call-start = ((), (), s32[]{:S(2)}) async-start(), calls=%async_computation.3 | async-start | bytes 5242880 | tf_op jit(solution)/shard_map/all_gather | solution.py:125
  14.3 100.6 %all-gather.8.cloned.1.call-start = ((), (), s32[]{:S(2)}) async-start(), calls=%async_computation.6 | async-start | bytes 5242880 | tf_op jit(solution)/shard_map/all_gather | solution.py:153
  15.1 329.3 %all-gather.6.cloned.1.call-start = ((), (), s32[]{:S(2)}) async-start(), calls=%async_computation.4 | async-start | bytes 5242880 | tf_op jit(solution)/shard_map/all_gather | solution.py:126
  15.8 796.9 %all-reduce.14.cloned.1.call-start = ((), (), s32[]{:S(2)}) async-start(), calls=%async_computation.9 | async-start | bytes 25165824 | tf_op jit(solution)/shard_map/psum | solution.py:190
  125.6 19.2 %copy-start.44 = (f32[32,64,4]{1,2,0:T(4,128)}, f32[32,64,4]{1,2,0:T(4,128)S(1)}, u32[]{:S(2)}) copy-start(f32[32,64,4]{1,2,0:T(4,128)S(1)} %get-tuple-element.130) | copy-start | bytes 98308
  125.6 19.2 %copy-start.11 = (f32[32,4,64,64]{2,3,1,0:T(8,128)S(1)}, f32[32,4,64,64]{2,3,1,0:T(8,128)}, u32[]{:S(2)}) copy-start(f32[32,4,64,64]{2,3,1,0:T(8,128)} %copy-done.10) | copy-start | bytes 6291460
  125.6 19.2 %copy-start.24 = (bf16[32,4,64,64]{2,3,1,0:T(8,128)(2,1)S(1)}, bf16[32,4,64,64]{2,3,1,0:T(8,128)(2,1)}, u32[]{:S(2)}) copy-start(bf16[32,4,64,64]{2,3,1,0:T(8,128)(2,1)} %select_convert_fusion) | copy-start | bytes 3145732
  125.6 19.2 %copy-start.30 = (f32[32,64,4,64]{1,0,3,2:T(8,128)S(1)}, f32[32,64,4,64]{1,0,3,2:T(8,128)}, u32[]{:S(2)}) copy-start(f32[32,64,4,64]{1,0,3,2:T(8,128)} %reshape.311) | copy-start | bytes 6291460
  165.0 15.7 %copy-start.3 = (f32[32,64,4,64]{1,0,3,2:T(8,128)S(1)}, f32[32,64,4,64]{1,0,3,2:T(8,128)}, u32[]{:S(2)}) copy-start(f32[32,64,4,64]{1,0,3,2:T(8,128)} %reshape.309) | copy-start | bytes 6291460
  165.0 15.7 %copy-start.12 = (f32[32,4,64,64]{2,3,1,0:T(8,128)S(1)}, f32[32,4,64,64]{2,3,1,0:T(8,128)}, u32[]{:S(2)}) copy-start(f32[32,4,64,64]{2,3,1,0:T(8,128)} %copy-done.10) | copy-start | bytes 6291460
  165.0 15.7 %copy-start.25 = (bf16[32,4,64,64]{2,3,1,0:T(8,128)(2,1)S(1)}, bf16[32,4,64,64]{2,3,1,0:T(8,128)(2,1)}, u32[]{:S(2)}) copy-start(bf16[32,4,64,64]{2,3,1,0:T(8,128)(2,1)} %select_convert_fusion) | copy-start | bytes 3145732
  216.0 11.9 %copy-start.31 = (f32[32,64,4,64]{1,0,3,2:T(8,128)S(1)}, f32[32,64,4,64]{1,0,3,2:T(8,128)}, u32[]{:S(2)}) copy-start(f32[32,64,4,64]{1,0,3,2:T(8,128)} %reshape.311) | copy-start | bytes 6291460
  256.0 13.3 %copy-start.2 = (f32[32,64,4,64]{3,1,2,0:T(8,128)S(1)}, f32[32,64,4,64]{3,1,2,0:T(8,128)}, u32[]{:S(2)}) copy-start(f32[32,64,4,64]{3,1,2,0:T(8,128)} %copy.151) | copy-start | bytes 6291460
  351.9 24.4 %copy-start.26 = (f32[2048,1024]{1,0:T(8,128)}, f32[2048,1024]{1,0:T(8,128)S(1)}, u32[]{:S(2)}) copy-start(f32[2048,1024]{1,0:T(8,128)S(1)} %fusion.171) | copy-start | bytes 25165828
  412.1 474.0 %reduce-scatter.6.cloned.1.call-start = ((), (), s32[]{:S(2)}) async-start(), calls=%async_computation.7 | async-start | bytes 10485760 | tf_op jit(solution)/shard_map/reduce_scatter | solution.py:168
  421.2 539.0 %reduce-scatter.8.cloned.1.call-start = ((), (), s32[]{:S(2)}) async-start(), calls=%async_computation.8 | async-start | bytes 10485760 | tf_op jit(solution)/shard_map/reduce_scatter | solution.py:169
  431.9 602.8 %reduce-scatter.4.cloned.1.call-start = ((), (), s32[]{:S(2)}) async-start(), calls=%async_computation.5 | async-start | bytes 10485760 | tf_op jit(solution)/shard_map/reduce_scatter | solution.py:142
  448.8 511.5 %copy-start.13 = (bf16[512,1024]{1,0:T(8,128)(2,1)S(1)}, bf16[512,1024]{1,0:T(8,128)(2,1)}, u32[]{:S(2)}) copy-start(bf16[512,1024]{1,0:T(8,128)(2,1)} %param.15) | copy-start | bytes 3145732
  448.8 511.4 %copy-start.43 = (f32[512]{0:T(512)S(1)}, f32[512]{0:T(512)}, u32[]{:S(2)}) copy-start(f32[512]{0:T(512)} %copy-done.42) | copy-start | bytes 6148
  448.8 511.4 %copy-start.47 = (f32[1024]{0:T(1024)S(1)}, f32[1024]{0:T(1024)}, u32[]{:S(2)}) copy-start(f32[1024]{0:T(1024)} %param.16) | copy-start | bytes 12292
  448.8 511.4 %copy-start.48 = (f32[1024]{0:T(1024)S(1)}, f32[1024]{0:T(1024)}, u32[]{:S(2)}) copy-start(f32[1024]{0:T(1024)} %param.18) | copy-start | bytes 12292
  816.3 147.3 %copy-start.57 = (f32[512]{0:T(512)S(1)}, f32[512]{0:T(512)}, u32[]{:S(2)}) copy-start(f32[512]{0:T(512)} %copy-done.56) | copy-start | bytes 6148
  816.3 147.3 %copy-start.54 = (f32[512]{0:T(512)S(1)}, f32[512]{0:T(512)}, u32[]{:S(2)}) copy-start(f32[512]{0:T(512)} %copy-done.53) | copy-start | bytes 6148
  (49 other events, 244.5 us)
Sparse Core Ops, SparseCore 0:
  14.4 37.1 all-gather.3
  53.2 34.4 all-gather.7
  89.9 34.4 all-gather.5
  412.2 400.5 all-reduce.13
  815.3 70.6 reduce-scatter.5
  888.5 71.7 reduce-scatter.7
  963.0 71.7 reduce-scatter.3
where the time goes:
time: 1060 us; the launch traced here: 1050 us
  waiting for transfers between devices  543 us (51%)
  matrix products  284 us (27%)
  local copies, waits for them, and re-layouts  90 us (8%)
  other arithmetic  72.9 us (7%)
  blocking collectives  47.8 us (5%)
  between operations  15.3 us (1%)
    psum x1, waiting for transfers between devices, shards(): lax.psum((grad_qkv, grad_out, grad_up, grad_down, grad_scale, grad_weight...  364 us
    reduce_scatter x1, waiting for transfers between devices, shards(): lax.psum_scatter(d_second, 'tensor', scatter_dimension=0, tiled=True)  74.2 us
    reduce_scatter x1, waiting for transfers between devices, shards(): lax.psum_scatter(d_first, 'tensor', scatter_dimension=0, tiled=True)  69.8 us
    dot_general x3, matrix products, linear_mixer(): jnp.einsum('bthf,bhfd->bthd', feat_q, bf_rounded(carried), precision=PREC...  45.2 us
    dot_general x3, matrix products, linear_mixer(): jnp.einsum('bshf,bshd->bhfd', feat_k, values, precision=PRECISE_MODE)  38.8 us
    psum x1, blocking collectives, shards(): lax.psum((grad_qkv, grad_out, grad_up, grad_down, grad_scale, grad_weight...  37.7 us
    dot_general x3, matrix products, linear_mixer(): jnp.einsum('bhts,bshd->bthd', bf_rounded(scores), values, precision=PRECI...  34.4 us
    dot_general x3, matrix products, linear_mixer(): jnp.einsum('bthf,bshf->bhts', feat_q, feat_k, precision=PRECISE_MODE)  31.1 us
  transfers between devices with their start and end apart: 7, of which 5 were waited for; matrix products, arithmetic and copies ran while one was open for 33% of the time, Pallas kernels for 0%

commit v1 on v0

v1 whole, which is shorter than its diff:
```python
import functools
import math

import jax
import jax.numpy as jnp
import ml_dtypes
import numpy as np
from jax import lax
from jax.experimental import pallas as pl
from jax.experimental.pallas import tpu as pltpu
from jax.sharding import PartitionSpec as P

HEAD_DIM = 64
ROT = 16
BLOCK = 64
CHUNK = 128
TILE = 256
SUB = 32
MESH = pl.DeviceIdType.MESH
F32 = jnp.float32
BF = jnp.bfloat16
NN = (((1,), (0,)), ((), ()))
NT = (((1,), (1,)), ((), ()))
TN = (((0,), (0,)), ((), ()))


def dot(left, right, dims=NN):
    return lax.dot_general(left, right, dims, preferred_element_type=F32)


def split(value):
    high = value.astype(BF)
    return high, (value - high.astype(F32)).astype(BF)


def wide(parts, axis=1):
    return jnp.concatenate(parts, axis)


def tables(blocks, heads):
    width = heads * HEAD_DIM
    freq, dims = np.arange(HEAD_DIM)[:, None], np.arange(HEAD_DIM)[None, :]
    dct = np.cos(np.pi * (dims + 0.5) * freq / HEAD_DIM) * math.sqrt(2.0 / HEAD_DIM)
    dct[0] *= math.sqrt(0.5)
    dct = np.kron(np.eye(heads), dct).astype(np.float32)
    high = dct.astype(ml_dtypes.bfloat16)
    low = (dct - high.astype(np.float32)).astype(ml_dtypes.bfloat16)
    forward = np.concatenate([high.T, high.T, low.T], 0)
    backward = np.concatenate([high, high, low], 0)
    half = ROT // 2
    lane = np.arange(2 * HEAD_DIM) % HEAD_DIM
    rate = np.where(lane < ROT, 10000.0 ** (-(lane % half) * 2.0 / ROT), 0.0)
    in_block = np.arange(BLOCK)[:, None] * rate[None]
    of_block = np.arange(blocks)[:, None] * BLOCK * rate[None]
    signs = np.stack([np.where(lane < half, -1.0, 0.0), np.where((lane >= half) & (lane < ROT), 1.0, 0.0)] + [0.0 * lane] * 6)
    angles = np.concatenate([np.cos(in_block), np.sin(in_block), np.cos(of_block), np.sin(of_block), signs], 0)
    diagonal = np.kron(np.eye(heads), np.ones((HEAD_DIM, HEAD_DIM)))
    masks = np.kron(np.eye(heads), np.ones((CHUNK, HEAD_DIM)))
    return (
        forward,
        backward,
        angles.astype(np.float32),
        diagonal.astype(np.float32),
        np.concatenate([diagonal, diagonal], 0).astype(ml_dtypes.bfloat16),
        masks.astype(ml_dtypes.bfloat16),
    )


def kernel(
    lengths,
    tok_in,
    cot_in,
    norms,
    w_qkv,
    w_out,
    w_up,
    w_down,
    feature,
    dct_fwd,
    dct_bwd,
    angles,
    diag,
    diag_two,
    masks,
    out_part,
    back_part,
    g_down,
    g_out,
    g_up,
    g_qkv,
    small,
    tok,
    cot,
    n_one,
    n_two,
    hid,
    slope,
    fqkv,
    spec,
    mixed,
    att,
    rden,
    states,
    ksums,
    state,
    krow,
    stage,
    wide_one,
    wide_two,
    sums,
    feat_sums,
    local_sem,
    send_sem,
    recv_sem,
    stage_sem,
):
    rows_own = tok_in.shape[0]
    rows = tok.shape[0]
    width = w_out.shape[0]
    heads = width // HEAD_DIM
    chunks = rows // CHUNK
    half_rows = rows_own // 2
    me = lax.axis_index("tensor")
    core = lax.rem(me, 2)
    mate = me + 1 - 2 * core
    peer = lax.rem(me + 2, 4)
    cross = 3 - me

    barrier = pltpu.get_barrier_semaphore()
    for other in (mate, peer):
        pl.semaphore_signal(barrier, inc=1, device_id={"tensor": other}, device_id_type=MESH)
    pl.semaphore_wait(barrier, 2)

    def slot(buf, owner, piece=None):
        if piece is None:
            return buf.at[pl.ds(pl.multiple_of(owner * rows_own, rows_own), rows_own)]
        return buf.at[pl.ds(pl.multiple_of(owner * rows_own + piece * half_rows, half_rows), half_rows)]

    class Gather:
        def __init__(self, source, buf, base):
            self.source, self.buf, self.base = source, buf, base

        def copy(self, number, src, dst, target):
            return pltpu.make_async_remote_copy(
                src_ref=src,
                dst_ref=dst,
                send_sem=send_sem.at[self.base + number],
                recv_sem=recv_sem.at[self.base + number],
                device_id={"tensor": target},
                device_id_type=MESH,
            )

        def local(self):
            return pltpu.make_async_copy(self.source, slot(self.buf, me), local_sem.at[self.base])

        def to_mate(self, owner):
            return self.copy(0, self.source, slot(self.buf, owner), mate)

        def to_peer(self, owner, piece):
            part = self.source.at[pl.ds(piece * half_rows, half_rows)]
            return self.copy(1 + piece, part, slot(self.buf, owner, piece), peer)

        def forward(self, owner, piece):
            return self.copy(3 + piece, slot(self.buf, owner, piece), slot(self.buf, owner, piece), mate)

    g_tok, g_cot = Gather(tok_in, tok, 0), Gather(cot_in, cot, 5)
    g_tok.to_mate(me).start()
    for piece in range(2):
        g_tok.to_peer(me, piece).start()
    g_tok.local().start()
    g_cot.to_mate(me).start()
    g_cot.local().start()

    start_one = lengths[0, 0]
    start_two = start_one + lengths[0, 1]

    def segment(block):
        return (block >= start_one).astype(jnp.int32) + (block >= start_two).astype(jnp.int32)

    def in_sequence(block):
        return block - jnp.where(block >= start_two, start_two, jnp.where(block >= start_one, start_one, 0))

    gain_one, bias_one, gain_two, bias_two = (norms[i : i + 1, :] for i in range(4))
    scale_row, weight_row = feature[0:1, :], feature[1:2, :]
    blocks = rows // BLOCK

    def rotation(row0, count):
        cos_in, sin_in = angles[0:BLOCK, :], angles[BLOCK : 2 * BLOCK, :]
        sign_a = angles[2 * BLOCK + 2 * blocks : 2 * BLOCK + 2 * blocks + 1, :]
        sign_b = angles[2 * BLOCK + 2 * blocks + 1 : 2 * BLOCK + 2 * blocks + 2, :]
        cosines, sines = [], []
        for k in range(count):
            place = in_sequence(lax.div(row0, BLOCK) + k)
            cos_at = angles[pl.ds(2 * BLOCK + place, 1), :]
            sin_at = angles[pl.ds(2 * BLOCK + blocks + place, 1), :]
            cosines.append(cos_in * cos_at - sin_in * sin_at)
            sines.append(sin_in * cos_at + cos_in * sin_at)
        cosine, sine = wide(cosines, 0), wide(sines, 0)
        return cosine, sine * sign_a, sine * sign_b

    def rotate(field, turn, back=False):
        cosine, sine_a, sine_b = turn
        parts = []
        for at in range(0, width, 2 * HEAD_DIM):
            part = field[:, at : at + 2 * HEAD_DIM]
            ahead = pltpu.roll(part, 2 * HEAD_DIM - ROT // 2, 1) * sine_a
            behind = pltpu.roll(part, ROT // 2, 1) * sine_b
            parts.append(part * cosine - (ahead + behind) if back else part * cosine + (ahead + behind))
        return wide(parts)

    def centered(at, size):
        value = tok[pl.ds(at, size), :].astype(F32)
        value = value - jnp.mean(value, -1, keepdims=True)
        deviation = lax.rsqrt(jnp.mean(value * value, -1, keepdims=True) + 1e-05)
        return value * deviation, deviation

    def project(j, carry):
        @pl.when(j == 0)
        def _():
            g_tok.local().wait()

        @pl.when(j == 2)
        def _():
            g_tok.to_mate(mate).wait_recv()

        for piece in range(2):

            @pl.when(j == 4 + 2 * piece)
            def _():
                g_tok.to_peer(peer, piece).wait_recv()
                g_tok.forward(peer, piece).start()
                g_cot.to_peer(me, piece).start()

            @pl.when(j == 5 + 2 * piece)
            def _():
                g_tok.forward(cross, piece).wait_recv()

        late = lax.div(j, 4)
        owner_early = jnp.where(j < 2, me, mate)
        owner_late = jnp.where(lax.rem(j, 2) == 0, peer, cross)
        owner = jnp.where(late == 0, owner_early, owner_late)
        piece = jnp.where(late == 0, lax.rem(j, 2), lax.div(j - 4, 2))
        row0 = pl.multiple_of(owner * rows_own + piece * TILE, TILE)

        def norm(i, inner):
            at = pl.multiple_of(row0 + i * SUB, SUB)
            unit, _ = centered(at, SUB)
            n_one[pl.ds(at, SUB), :] = (unit * gain_one + bias_one).astype(BF)
            n_two[pl.ds(at, SUB), :] = (unit * gain_two + bias_two).astype(BF)
            return inner

        lax.fori_loop(0, TILE // SUB, norm, 0)
        here = pl.ds(row0, TILE)
        first = n_one[here, :]
        turn = rotation(row0, TILE // BLOCK)
        for s in range(2):
            high, low = split(rotate(dot(first, w_qkv[s]), turn))
            spectrum = dot(wide([high, low, high]), dct_fwd[...])
            spec[s, here, :] = spectrum
            fqkv[here, s * width : (s + 1) * width] = (weight_row * jnp.exp(scale_row * spectrum)).astype(BF)
        fqkv[here, 2 * width : 3 * width] = dot(first, w_qkv[2]).astype(BF)
        second = n_two[here, :]
        for at in range(0, w_up.shape[1], TILE):
            up = dot(second, w_up[:, at : at + TILE])
            below = 0.5 * (1.0 + lax.erf(up * math.sqrt(0.5)))
            hid[here, at : at + TILE] = (up * below).astype(BF)
            slope[here, at : at + TILE] = below + up * (jnp.exp(-0.5 * up * up) * (1.0 / math.sqrt(2.0 * math.pi)))
        return carry

    lax.fori_loop(0, rows // TILE, project, 0)

    grid_t = lax.broadcasted_iota(jnp.int32, (CHUNK, CHUNK), 0)
    grid_s = lax.broadcasted_iota(jnp.int32, (CHUNK, CHUNK), 1)
    causal = jnp.where((grid_t >= grid_s) & ((grid_t < BLOCK) | (grid_s >= BLOCK)), 1.0, 0.0).astype(F32)

    def joined(block):
        return jnp.where(segment(block) == segment(block - 1), jnp.float32(1.0), jnp.float32(0.0))

    def per_head(value):
        return [value * masks[h * CHUNK : (h + 1) * CHUNK, :] for h in range(heads)]

    def halves(value):
        return [value[k * BLOCK : (k + 1) * BLOCK] for k in range(CHUNK // BLOCK)]

    state[...] = jnp.zeros_like(state)
    krow[...] = jnp.zeros_like(krow)

    def mix(i, carry):
        here = pl.ds(pl.multiple_of(i * CHUNK, CHUNK), CHUNK)
        query, key, value = (fqkv[here, s * width : (s + 1) * width] for s in range(3))
        stacked = dot(wide(per_head(query), 0), key, NT)
        highs, lows = zip(*(split(stacked[h * CHUNK : (h + 1) * CHUNK] * causal) for h in range(heads)))
        scores = wide(highs)
        over = dot(scores, wide(per_head(value), 0))
        under = dot(scores, masks[...]) + dot(wide(lows), masks[...])
        now, row = state[...], krow[0:1, :]
        overs, rows_under = [], []
        for k, (query_k, key_k, value_k) in enumerate(zip(*map(halves, (query, key, value)))):
            carried = now.astype(BF)
            states[2 * i + k] = carried
            ksums[2 * i + k] = jnp.broadcast_to(row, (8, width))
            overs.append(dot(query_k, carried))
            rows_under.append(query_k.astype(F32) * row)
            keep = joined(2 * i + k + 1)
            now = (now + dot(key_k, value_k, TN) * diag[...]) * keep
            row = (row + jnp.sum(key_k.astype(F32), 0, keepdims=True)) * keep
        state[...] = now
        krow[0:1, :] = row
        high, low = split(wide(rows_under, 0))
        over = over + wide(overs, 0)
        under = under + dot(wide([high, low]), diag_two[...])
        inverse = 1.0 / under
        attended = over * inverse
        att[here, :] = attended
        rden[here, :] = inverse
        mixed[here, :] = attended.astype(BF)
        return carry

    lax.fori_loop(0, chunks, mix, 0)

    for piece in range(2):
        g_cot.to_peer(peer, piece).wait_recv()
        g_cot.forward(peer, piece).start()

    def staged(number, target):
        return pltpu.make_async_copy(stage.at[number], target, stage_sem.at[number])

    def put(j, tile, target, first):
        number = lax.rem(j, 2)
        if first is None:
            staged(number, target).wait()
        else:

            @pl.when(j >= first + 2)
            def _():
                staged(number, target).wait()

        stage[number] = tile.astype(BF)
        staged(number, target).start()

    def drain(target):
        for number in range(2):
            staged(number, target).wait()

    def produce(j, carry):
        here = pl.ds(pl.multiple_of(j * TILE, TILE), TILE)
        tile = dot(mixed[here, :], w_out[...]) + dot(hid[here, :], w_down[...])
        put(j, tile, out_part.at[here], 0)
        return carry

    lax.fori_loop(0, rows // TILE, produce, 0)
    drain(out_part.at[pl.ds(0, TILE)])

    for piece in range(2):
        g_cot.forward(cross, piece).wait_recv()
    g_cot.to_mate(mate).wait_recv()
    g_cot.local().wait()

    def down(j, carry):
        at = pl.ds(pl.multiple_of(j * TILE, TILE), TILE)
        put(j, dot(hid[:, at], cot[...], TN), g_down.at[at], 0)
        return carry

    lax.fori_loop(0, hid.shape[1] // TILE, down, 0)
    put(0, dot(mixed[...], cot[...], TN), g_out, None)
    drain(g_out)

    def descend(j, carry):
        here = pl.ds(pl.multiple_of(j * TILE, TILE), TILE)
        for at in range(0, hid.shape[1], TILE):
            d_hidden = dot(cot[here, :], w_down[at : at + TILE, :], NT)
            hid[here, at : at + TILE] = (d_hidden * slope[here, at : at + TILE]).astype(BF)
        return carry

    lax.fori_loop(0, rows // TILE, descend, 0)

    def upward(j, carry):
        at = pl.ds(pl.multiple_of(j * TILE, TILE), TILE)
        put(j, dot(n_two[:, at], hid[...], TN), g_up.at[at], 0)
        return carry

    lax.fori_loop(0, n_two.shape[1] // TILE, upward, 0)
    drain(g_out)

    state[...] = jnp.zeros_like(state)
    krow[...] = jnp.zeros_like(krow)
    feat_sums[...] = jnp.zeros_like(feat_sums)

    def unmix(step, carry):
        i = chunks - 1 - step
        row0 = pl.multiple_of(i * CHUNK, CHUNK)
        here = pl.ds(row0, CHUNK)
        query, key, value = (fqkv[here, s * width : (s + 1) * width] for s in range(3))
        inverse, attended = rden[here, :], att[here, :]
        d_over = dot(cot[here, :], w_out[...], NT) * inverse
        high, low = split(d_over * attended)
        d_under = -dot(wide([high, low]), diag_two[...])
        over_high, over_low = split(d_over)
        both = wide([wide(per_head(over_high), 0), wide(per_head(over_low), 0)])
        stacked = dot(both, wide([value, value]), NT)
        heads_high, heads_low = [], []
        for h in range(heads):
            d_scores = stacked[h * CHUNK : (h + 1) * CHUNK] + d_under[:, h * HEAD_DIM : h * HEAD_DIM + 1]
            high, low = split(d_scores * causal)
            heads_high.append(high)
            heads_low.append(low)
        query_heads = wide(per_head(query), 0)
        key_heads = wide(per_head(key), 0)
        over_both = wide([over_high, over_low])
        d_query = dot(wide(heads_high + heads_low), wide([key_heads, key_heads], 0))
        d_key = dot(wide(heads_high + heads_low, 0), wide([query_heads, query_heads], 0), TN)
        stacked = dot(query_heads, key, NT)
        scores = [(stacked[h * CHUNK : (h + 1) * CHUNK] * causal).astype(BF) for h in range(heads)]
        d_value = dot(wide(scores, 0), both, TN)
        d_value = d_value[:, :width] + d_value[:, width:]
        later, later_row = state[...], krow[0:1, :]
        more_query, more_key, more_value = [], [], []
        parts = list(zip(*map(halves, (query, key, value, over_both, over_high, over_low, d_under))))
        for k in reversed(range(len(parts))):
            query_k, key_k, value_k, both_k, high_k, low_k, under_k = parts[k]
            carried, row = states[2 * i + k], ksums[2 * i + k][0:1, :]
            more_query.insert(0, dot(both_k, wide([carried, carried]), NT) + under_k * row)
            keep = joined(2 * i + k + 1)
            later_high, later_low = split(later * keep)
            more_key.insert(0, dot(wide([value_k, value_k]), wide([later_high, later_low]), NT) + later_row * keep)
            more_value.insert(0, dot(wide([key_k, key_k]), wide([later_high, later_low], 0)))
            add = dot(wide([query_k, query_k], 0), wide([high_k, low_k], 0), TN)
            later = later * keep + add * diag[...]
            later_row = later_row * keep + jnp.sum(query_k.astype(F32) * under_k, 0, keepdims=True)
        state[...] = later
        krow[0:1, :] = later_row
        d_query = d_query + wide(more_query, 0)
        d_key = d_key + wide(more_key, 0)
        d_value = d_value + wide(more_value, 0)
        turn = rotation(row0, CHUNK // BLOCK)
        for s, grad in enumerate((d_query, d_key)):
            spectrum = spec[s, here, :]
            grad = grad * (weight_row * jnp.exp(scale_row * spectrum))
            feat_sums[0:1, :] += jnp.sum(grad * spectrum, 0, keepdims=True)
            feat_sums[1:2, :] += jnp.sum(grad, 0, keepdims=True)
            high, low = split(grad * scale_row)
            fqkv[here, s * width : (s + 1) * width] = rotate(
                dot(wide([high, low, high]), dct_bwd[...]), turn, True
            ).astype(BF)
        fqkv[here, 2 * width : 3 * width] = d_value.astype(BF)
        return carry

    lax.fori_loop(0, chunks, unmix, 0)

    def projected(j, carry):
        at = pl.ds(pl.multiple_of(j * TILE, TILE), TILE)
        number = lax.rem(j, 2)
        tile = dot(n_one[:, at], fqkv[...], TN)

        def piece(s):
            return pltpu.make_async_copy(
                stage.at[number, :, s * width : (s + 1) * width], g_qkv.at[s, at], stage_sem.at[number]
            )

        @pl.when(j >= 2)
        def _():
            for s in range(3):
                piece(s).wait()

        stage[number, :, 0 : 3 * width] = tile.astype(BF)
        for s in range(3):
            piece(s).start()
        return carry

    lax.fori_loop(0, n_one.shape[1] // TILE, projected, 0)
    for number in range(2):
        for s in range(3):
            pltpu.make_async_copy(
                stage.at[number, :, s * width : (s + 1) * width], g_qkv.at[s, pl.ds(0, TILE)], stage_sem.at[number]
            ).wait()

    sums[...] = jnp.zeros_like(sums)

    def inputs(j, carry):
        row0 = pl.multiple_of(j * TILE, TILE)
        here = pl.ds(row0, TILE)
        total = dot(fqkv[here, 0:width], w_qkv[0], NT)
        for s in (1, 2):
            total = total + dot(fqkv[here, s * width : (s + 1) * width], w_qkv[s], NT)
        wide_one[...] = total
        wide_two[...] = dot(hid[here, :], w_up[...], NT)

        def fold(i, inner):
            at = pl.ds(pl.multiple_of(i * SUB, SUB), SUB)
            unit, _ = centered(pl.multiple_of(row0 + i * SUB, SUB), SUB)
            one, two = wide_one[at, :], wide_two[at, :]
            for number, term in enumerate((one * unit, one, two * unit, two)):
                sums[number] += jnp.sum(term.reshape(SUB // 8, 8, term.shape[1]), 0)
            wide_one[at, :] = one * gain_one + two * gain_two
            return inner

        lax.fori_loop(0, TILE // SUB, fold, 0)
        put(j, wide_one[...], back_part.at[here], 0)
        return carry

    lax.fori_loop(0, rows // TILE, inputs, 0)
    drain(back_part.at[pl.ds(0, TILE)])
    small[...] = jnp.zeros_like(small)
    for number in range(4):
        small[number : number + 1, :] = jnp.sum(sums[number], 0, keepdims=True)
    small[4:5, 0:width] = feat_sums[0:1, :]
    small[5:6, 0:width] = feat_sums[1:2, :] / weight_row

    for gather in (g_tok, g_cot):
        gather.to_mate(me).wait_send()
        for piece in range(2):
            gather.to_peer(me, piece).wait_send()
            gather.forward(peer, piece).wait_send()


def shards(
    tokens,
    ln1_gain,
    ln1_bias,
    ln2_gain,
    ln2_bias,
    w_qkv,
    w_out,
    w_up,
    w_down,
    feature_scale,
    feature_weight,
    lengths,
    cotangent,
):
    rows_own, model = tokens.shape
    rows = 4 * rows_own
    heads = feature_scale.shape[0]
    width = heads * HEAD_DIM
    hidden = w_up.shape[1]
    consts = tables(rows // BLOCK, heads)
    norms = jnp.stack([ln1_gain, ln1_bias, ln2_gain, ln2_bias])
    feature = jnp.stack([feature_scale.reshape(-1), feature_weight.reshape(-1)])
    anywhere = pl.BlockSpec(memory_space=pl.ANY)
    vmem = pl.BlockSpec(memory_space=pltpu.VMEM)
    smem = pl.BlockSpec(memory_space=pltpu.SMEM)
    shape = jax.ShapeDtypeStruct
    out_part, back_part, g_down, g_out, g_up, g_qkv, small = pl.pallas_call(
        kernel,
        out_shape=(
            shape((rows, model), BF),
            shape((rows, model), BF),
            shape((hidden, model), BF),
            shape((width, model), BF),
            shape((model, hidden), BF),
            shape((3, model, width), BF),
            shape((8, model), F32),
        ),
        in_specs=[smem, anywhere, anywhere] + [vmem] * 12,
        out_specs=(anywhere,) * 6 + (vmem,),
        scratch_shapes=[
            pltpu.VMEM((rows, model), BF),
            pltpu.VMEM((rows, model), BF),
            pltpu.VMEM((rows, model), BF),
            pltpu.VMEM((rows, model), BF),
            pltpu.VMEM((rows, hidden), BF),
            pltpu.VMEM((rows, hidden), F32),
            pltpu.VMEM((rows, 3 * width), BF),
            pltpu.VMEM((2, rows, width), F32),
            pltpu.VMEM((rows, width), BF),
            pltpu.VMEM((rows, width), F32),
            pltpu.VMEM((rows, width), F32),
            pltpu.VMEM((rows // BLOCK, width, width), BF),
            pltpu.VMEM((rows // BLOCK, 8, width), F32),
            pltpu.VMEM((width, width), F32),
            pltpu.VMEM((8, width), F32),
            pltpu.VMEM((2, TILE, model), BF),
            pltpu.VMEM((TILE, model), F32),
            pltpu.VMEM((TILE, model), F32),
            pltpu.VMEM((4, 8, model), F32),
            pltpu.VMEM((8, width), F32),
            pltpu.SemaphoreType.DMA((10,)),
            pltpu.SemaphoreType.DMA((10,)),
            pltpu.SemaphoreType.DMA((10,)),
            pltpu.SemaphoreType.DMA((2,)),
        ],
        compiler_params=pltpu.CompilerParams(
            collective_id=0, has_side_effects=True, vmem_limit_bytes=63 * 2**20
        ),
    )(lengths, tokens, cotangent, norms, w_qkv, w_out, w_up, w_down, feature, *consts)
    branches = lax.psum_scatter(out_part.astype(F32), "tensor", scatter_dimension=0, tiled=True).astype(F32)
    mixed_out = (tokens.astype(F32) + branches).astype(BF)
    d_rows = lax.psum_scatter(back_part.astype(F32), "tensor", scatter_dimension=0, tiled=True).astype(F32)
    rows_in = tokens.astype(F32)
    unit = rows_in - jnp.mean(rows_in, -1, keepdims=True)
    deviation = lax.rsqrt(jnp.mean(unit * unit, -1, keepdims=True) + 1e-05)
    unit = unit * deviation
    inner = d_rows - jnp.mean(d_rows, -1, keepdims=True) - unit * jnp.mean(d_rows * unit, -1, keepdims=True)
    input_grad = (cotangent.astype(F32) + deviation * inner).astype(BF)
    g_down, g_out, g_up, g_qkv = (
        lax.psum(tuple(g.astype(F32) for g in (g_down, g_out, g_up, g_qkv)), "dp")
    )
    norm_sums = lax.psum(small[0:4], ("dp", "tensor"))
    feat_sums = lax.psum(small[4:6, 0:width], "dp").reshape(2, heads, HEAD_DIM)
    return (
        mixed_out,
        input_grad,
        norm_sums[0],
        norm_sums[1],
        norm_sums[2],
        norm_sums[3],
        g_qkv,
        g_out,
        g_up,
        g_down,
        feat_sums[0],
        feat_sums[1],
    )


def solution(mesh):
    placed = (
        P(("dp", "tensor"), None),
        P(),
        P(),
        P(),
        P(),
        P(None, None, "tensor"),
        P("tensor", None),
        P(None, "tensor"),
        P("tensor", None),
        P("tensor", None),
        P("tensor", None),
        P("dp", None),
        P(("dp", "tensor"), None),
    )
    return jax.shard_map(
        shards,
        mesh=mesh,
        in_specs=placed,
        out_specs=(
            P(("dp", "tensor"), None),
            P(("dp", "tensor"), None),
            P(),
            P(),
            P(),
            P(),
            P(None, None, "tensor"),
            P("tensor", None),
            P(None, "tensor"),
            P("tensor", None),
            P("tensor", None),
            P("tensor", None),
        ),
        check_vma=False,
    )
```

time: 1060 us -> 709 us (0.67)
  waiting for transfers between devices: 543 us -> 0.06 us
  blocking collectives: 47.8 us -> 526 us
  matrix products: 284 us -> 0 us
  Pallas kernels: 0 us -> 140 us
  local copies, waits for them, and re-layouts: 90 us -> 5.23 us
  other arithmetic: 72.9 us -> 22.2 us
    psum x2, blocking collectives: 47.8 us -> 526 us  [the longest x1 488 us: shards(): lax.psum(tuple((g.astype(F32) for g in (g_down, g_out, g_up, g_qkv))), 'dp')]
    psum x1 -> x0, waiting for transfers between devices: 364 us -> none  [shards(): lax.psum((grad_qkv, grad_out, grad_up, grad_down, grad_scale, grad_weight...]
    dot_general x34 -> x0, matrix products: 284 us -> none  [the longest x3 45.2 us: linear_mixer(): jnp.einsum('bthf,bhfd->bthd', feat_q, bf_rounded(carried), precision=PREC...]
    reduce_scatter x3 -> x2, waiting for transfers between devices: 165 us -> 0.02 us  [the longest x1 0.02 us: shards(): lax.psum_scatter(out_part.astype(F32), 'tensor', scatter_dimension=0, til...]
    pallas_call x0 -> x1, Pallas kernels: none -> 140 us  [shards(): pl.pallas_call(kernel, out_shape=(shape((rows, model), BF), shape((rows,...]
    reshape x9 -> x0, local copies, waits for them, and re-layouts: 45.4 us -> none  [the longest x3 15.1 us: linear_mixer(): bf_rounded(features(keys_rot, table, scale_part, weight_part))]
    unnamed x132 -> x8, local copies, waits for them, and re-layouts: 23 us -> 1.74 us
    convert_element_type x6 -> x3, other arithmetic: 36.4 us -> 17.2 us  [the longest x1 6.72 us: shards(): out_part.astype(F32)]
  transfers between devices with their start and end apart: 7 -> 2, of which waited for: 5 -> 0; matrix products, arithmetic and copies ran while one was open for 33% -> 2% of each run, Pallas kernels for 0% -> 0%
where the time goes in v1:
time: 709 us; the launch traced here: 708 us
  blocking collectives  526 us (74%)
  Pallas kernels  140 us (20%)
  other arithmetic  22.2 us (3%)
  between operations  14.1 us (2%)
    psum x1, blocking collectives, shards(): lax.psum(tuple((g.astype(F32) for g in (g_down, g_out, g_up, g_qkv))), 'dp')  488 us
    pallas_call x1, Pallas kernels, shards(): pl.pallas_call(kernel, out_shape=(shape((rows, model), BF), shape((rows,...  140 us
    psum x1, blocking collectives, shards(): norm_sums = lax.psum(small[0:4], ('dp', 'tensor'))  38.7 us
  transfers between devices with their start and end apart: 2, of which 0 were waited for; matrix products, arithmetic and copies ran while one was open for 2% of the time, Pallas kernels for 0%

profile of v1, /device:TPU:0, one launch (start us, length us, event | category | flops | bytes accessed | tf_op | source)
XLA Modules:
  0.0 708.2 jit_solution(8517215510488976390)
XLA Ops:
  7.2 0.0 reduce-scatter.5.cloned.1.call-start
  7.2 0.8 stack_reshape.7
  8.0 0.8 stack_reshape.6
  8.7 0.6 pad_maximum_fusion.1.feature
  9.3 1.4 pad_maximum_fusion.norms
  10.7 140.1 %shard_map.274 = (bf16[2048,1024]{1,0:T(8,128)(2,1)}, bf16[2048,1024]{1,0:T(8,128)(2,1)}, bf16[1024,1024]{1,0:T(8,128)(2,1)}, bf16[256,1024]{1,0:T(8,128)(2,1)},...) custom-call(s32[1,3]{1,0:T(1,128)} %lengths.1, bf16[512,1024]{1,0:T(8,128)(2,1)} %tok_in.1, ...), custom_call_target="tpu_custom_call" | custom-call | tf_op jit(solution)/shard_map/pallas_call | solution.py:543
  150.8 6.5 convert_element_type.35
  157.3 0.0 reduce-scatter.5.cloned.1.call-update
  157.3 0.2 reduce-scatter.3.cloned.1.call-start
  157.6 6.7 convert_element_type.32
  164.3 0.0 reduce-scatter.3.cloned.1.call-update
  164.3 0.7 copy-done.3
  165.0 1.0 copy-done.2
  166.1 487.5 %all-reduce.2 = (f32[3,1024,256]{2,1,0:T(8,128)}, f32[256,1024]{1,0:T(8,128)}, f32[1024,1024]{1,0:T(8,128)}, f32[1024,1024]{1,0:T(8,128)}, f32[2,256]{1,0:T(2,128)S(1)}) all-reduce(bf16[3,1024,256]{2,1,0:T(8,128)(2,1)} %get-tuple-element.22, bf16[256,1024]{1,0:T(8,128)(2,1)} %get-tuple-element.23, ...), channel_id=1, replica_groups=mesh['dp'=8,'tensor'=4] {'dp'}, use_global_device_ids=true, to_apply=%region_7.0 | all-reduce | flops 3146240 | bytes 18878464 | tf_op jit(solution)/shard_map/psum | solution.py:596
  653.6 0.7 squeeze.22
  654.2 0.7 squeeze.23
  654.9 38.7 %psum.42 = f32[4,1024]{1,0:T(4,128)S(1)} all-reduce(f32[4,1024]{1,0:T(4,128)S(1)} %slice.26), channel_id=1, replica_groups=mesh['dp'=8,'tensor'=4] {'dp','tensor'}, use_global_device_ids=true, to_apply=%region_6.0 | all-reduce | flops 4096 | bytes 32768 | tf_op jit(solution)/shard_map/psum | solution.py:598
  693.6 0.0 copy-done
  693.6 0.2 convert_reduce_fusion
  693.9 0.4 fusion.9
  694.3 0.6 fusion.12
  694.9 2.4 fusion.11
  697.3 0.0 reduce-scatter.3.cloned.1.call-done
  697.3 4.0 fusion.8
  (12 shorter events, 0.1 us)
Async XLA Ops:
  7.2 687.7 %reduce-scatter.5.cloned.1.call-start = ((), (), s32[]{:S(2)}) async-start(), calls=%async_computation.3 | async-start | bytes 10485760 | tf_op jit(solution)/shard_map/reduce_scatter | solution.py:588
  157.3 540.0 %reduce-scatter.3.cloned.1.call-start = ((), (), s32[]{:S(2)}) async-start(), calls=%async_computation.2 | async-start | bytes 10485760 | tf_op jit(solution)/shard_map/reduce_scatter | solution.py:586
  164.3 0.8 copy-start.3
  164.3 1.8 copy-start.2
  166.0 527.6 %copy-start = (bf16[512,1024]{1,0:T(8,128)(2,1)S(1)}, bf16[512,1024]{1,0:T(8,128)(2,1)}, u32[]{:S(2)}) copy-start(bf16[512,1024]{1,0:T(8,128)(2,1)} %tok_in.1) | copy-start | bytes 3145732
  694.9 2.4 copy-start.1
Sparse Core Ops, SparseCore 0:
  157.5 72.1 reduce-scatter.4
  232.4 71.7 reduce-scatter.2

commit v2 on v1

--- a/solution.py
+++ b/solution.py
@@ -15,7 +15,9 @@
 BLOCK = 64
 CHUNK = 128
 TILE = 256
+UNIT = 128
 SUB = 32
+SLOTS = 12
 MESH = pl.DeviceIdType.MESH
 F32 = jnp.float32
 BF = jnp.bfloat16
@@ -45,8 +47,7 @@
     dct = np.kron(np.eye(heads), dct).astype(np.float32)
     high = dct.astype(ml_dtypes.bfloat16)
     low = (dct - high.astype(np.float32)).astype(ml_dtypes.bfloat16)
-    forward = np.concatenate([high.T, high.T, low.T], 0)
-    backward = np.concatenate([high, high, low], 0)
+    halves = np.concatenate([high, high, low], 1)
     half = ROT // 2
     lane = np.arange(2 * HEAD_DIM) % HEAD_DIM
     rate = np.where(lane < ROT, 10000.0 ** (-(lane % half) * 2.0 / ROT), 0.0)
@@ -57,44 +58,45 @@
     diagonal = np.kron(np.eye(heads), np.ones((HEAD_DIM, HEAD_DIM)))
     masks = np.kron(np.eye(heads), np.ones((CHUNK, HEAD_DIM)))
     return (
-        forward,
-        backward,
+        halves,
         angles.astype(np.float32),
-        diagonal.astype(np.float32),
         np.concatenate([diagonal, diagonal], 0).astype(ml_dtypes.bfloat16),
         masks.astype(ml_dtypes.bfloat16),
     )
 
 
 def kernel(
+    reduce_dp,
     lengths,
     tok_in,
     cot_in,
-    norms,
+    gain_one_in,
+    bias_one_in,
+    gain_two_in,
+    bias_two_in,
     w_qkv,
     w_out,
     w_up,
     w_down,
-    feature,
-    dct_fwd,
-    dct_bwd,
+    feature_scale,
+    feature_weight,
+    dct,
     angles,
-    diag,
     diag_two,
     masks,
-    out_part,
-    back_part,
-    g_down,
-    g_out,
-    g_up,
-    g_qkv,
+    mixed_out,
+    input_grad,
+    grads_out,
+    qkv_out,
+    slopes,
+    own_part,
     small,
+    feat_out,
     tok,
     cot,
     n_one,
     n_two,
     hid,
-    slope,
     fqkv,
     spec,
     mixed,
@@ -104,15 +106,30 @@
     ksums,
     state,
     krow,
-    stage,
-    wide_one,
-    wide_two,
+    grads,
+    recv_a,
+    recv_b,
+    rs_out,
+    rs_in,
+    y_in,
+    temp,
     sums,
     feat_sums,
+    small_in,
     local_sem,
     send_sem,
     recv_sem,
-    stage_sem,
+    ar_send,
+    ar_recv,
+    rs_send,
+    rs_recv,
+    small_send,
+    small_recv,
+    grad_sem,
+    temp_sem,
+    result_sem,
+    free_mate,
+    free_peer,
 ):
     rows_own = tok_in.shape[0]
     rows = tok.shape[0]
@@ -125,11 +142,40 @@
     mate = me + 1 - 2 * core
     peer = lax.rem(me + 2, 4)
     cross = 3 - me
+    group = lax.axis_index("dp")
+    along_x = lax.rem(group, 2)
+    across = group + 1 - 2 * along_x
+    along_z = lax.div(group, 2)
+    middle = along_z * (3 - along_z)
+
+    def at_end(step):
+        pl.when(middle == 0)(step)
+
+    def at_mid(step):
+        pl.when(middle > 0)(step)
+
+    side = jnp.where(along_z < 2, 0, 1)
+    inward = group + 2 - 4 * side
+    outward = group - 2 + 4 * side
+    units = grads.shape[0]
 
     barrier = pltpu.get_barrier_semaphore()
     for other in (mate, peer):
         pl.semaphore_signal(barrier, inc=1, device_id={"tensor": other}, device_id_type=MESH)
-    pl.semaphore_wait(barrier, 2)
+    if reduce_dp:
+        for other in (across, inward):
+            pl.semaphore_signal(barrier, inc=1, device_id={"dp": other}, device_id_type=MESH)
+
+        @at_mid
+        def _():
+            pl.semaphore_signal(barrier, inc=1, device_id={"dp": outward}, device_id_type=MESH)
+            pl.semaphore_wait(barrier, 5)
+
+        @at_end
+        def _():
+            pl.semaphore_wait(barrier, 4)
+    else:
+        pl.semaphore_wait(barrier, 2)
 
     def slot(buf, owner, piece=None):
         if piece is None:
@@ -180,8 +226,10 @@
     def in_sequence(block):
         return block - jnp.where(block >= start_two, start_two, jnp.where(block >= start_one, start_one, 0))
 
-    gain_one, bias_one, gain_two, bias_two = (norms[i : i + 1, :] for i in range(4))
-    scale_row, weight_row = feature[0:1, :], feature[1:2, :]
+    gain_one, bias_one, gain_two, bias_two = gain_one_in[...], bias_one_in[...], gain_two_in[...], bias_two_in[...]
+    scale_row, weight_row = (
+        wide([field[h : h + 1, :] for h in range(heads)]) for field in (feature_scale, feature_weight)
+    )
     blocks = rows // BLOCK
 
     def rotation(row0, count):
@@ -255,19 +303,29 @@
         turn = rotation(row0, TILE // BLOCK)
         for s in range(2):
             high, low = split(rotate(dot(first, w_qkv[s]), turn))
-            spectrum = dot(wide([high, low, high]), dct_fwd[...])
+            spectrum = dot(wide([high, low]), dct[:, 0 : 2 * width], NT) + dot(high, dct[:, 2 * width :], NT)
             spec[s, here, :] = spectrum
             fqkv[here, s * width : (s + 1) * width] = (weight_row * jnp.exp(scale_row * spectrum)).astype(BF)
         fqkv[here, 2 * width : 3 * width] = dot(first, w_qkv[2]).astype(BF)
         second = n_two[here, :]
+        parity = lax.rem(j, 2)
+
+        @pl.when(j >= 2)
+        def _():
+            pltpu.make_async_copy(temp.at[parity], slopes.at[here], temp_sem.at[parity]).wait()
+
         for at in range(0, w_up.shape[1], TILE):
             up = dot(second, w_up[:, at : at + TILE])
             below = 0.5 * (1.0 + lax.erf(up * math.sqrt(0.5)))
             hid[here, at : at + TILE] = (up * below).astype(BF)
-            slope[here, at : at + TILE] = below + up * (jnp.exp(-0.5 * up * up) * (1.0 / math.sqrt(2.0 * math.pi)))
+            temp[parity, :, at : at + TILE] = below + up * (jnp.exp(-0.5 * up * up) * (1.0 / math.sqrt(2.0 * math.pi)))
+        pltpu.make_async_copy(temp.at[parity], slopes.at[here], temp_sem.at[parity]).start()
         return carry
 
-    lax.fori_loop(0, rows // TILE, project, 0)
+    with jax.named_scope("project"):
+        lax.fori_loop(0, rows // TILE, project, 0)
+    for parity in range(2):
+        pltpu.make_async_copy(temp.at[parity], slopes.at[pl.ds(0, TILE)], temp_sem.at[parity]).wait()
 
     grid_t = lax.broadcasted_iota(jnp.int32, (CHUNK, CHUNK), 0)
     grid_s = lax.broadcasted_iota(jnp.int32, (CHUNK, CHUNK), 1)
@@ -286,6 +344,7 @@
     krow[...] = jnp.zeros_like(krow)
 
     def mix(i, carry):
+        diag = diag_two[0:width, :].astype(F32)
         here = pl.ds(pl.multiple_of(i * CHUNK, CHUNK), CHUNK)
         query, key, value = (fqkv[here, s * width : (s + 1) * width] for s in range(3))
         stacked = dot(wide(per_head(query), 0), key, NT)
@@ -297,12 +356,12 @@
         overs, rows_under = [], []
         for k, (query_k, key_k, value_k) in enumerate(zip(*map(halves, (query, key, value)))):
             carried = now.astype(BF)
-            states[2 * i + k] = carried
+            states[2 * i + k] = sum(now[h * HEAD_DIM : (h + 1) * HEAD_DIM] for h in range(heads)).astype(BF)
             ksums[2 * i + k] = jnp.broadcast_to(row, (8, width))
             overs.append(dot(query_k, carried))
             rows_under.append(query_k.astype(F32) * row)
             keep = joined(2 * i + k + 1)
-            now = (now + dot(key_k, value_k, TN) * diag[...]) * keep
+            now = (now + dot(key_k, value_k, TN) * diag) * keep
             row = (row + jnp.sum(key_k.astype(F32), 0, keepdims=True)) * keep
         state[...] = now
         krow[0:1, :] = row
@@ -312,75 +371,451 @@
         inverse = 1.0 / under
         attended = over * inverse
         att[here, :] = attended
-        rden[here, :] = inverse
+        rden[here, :] = wide([inverse[:, h * HEAD_DIM : h * HEAD_DIM + HEAD_DIM // 2] for h in range(heads)])
         mixed[here, :] = attended.astype(BF)
         return carry
 
-    lax.fori_loop(0, chunks, mix, 0)
+    with jax.named_scope("mixer"):
+        lax.fori_loop(0, chunks, mix, 0)
 
     for piece in range(2):
         g_cot.to_peer(peer, piece).wait_recv()
         g_cot.forward(peer, piece).start()
 
-    def staged(number, target):
-        return pltpu.make_async_copy(stage.at[number], target, stage_sem.at[number])
-
-    def put(j, tile, target, first):
+    def add_parts(base, first, count, sources):
+        for at in range(0, count, SUB):
+            total = base[pl.ds(first + at, SUB), :].astype(F32)
+            for source, place in sources:
+                total = total + source[pl.ds(place + at, SUB), :].astype(F32)
+            base[pl.ds(first + at, SUB), :] = total.astype(BF)
+
+    def bring(base, first, box, place, count):
+        base[pl.ds(first, count), :] = box[pl.ds(place, count), :]
+
+    half, quarter = UNIT // 2, UNIT // 4
+
+    def rows_of(index, size):
+        return pl.multiple_of(index * size, size)
+
+    def hop(n, kind, source, target, device):
+        return pltpu.make_async_remote_copy(
+            src_ref=source,
+            dst_ref=target,
+            send_sem=ar_send.at[n, kind],
+            recv_sem=ar_recv.at[n, kind],
+            device_id={"dp": device},
+            device_id_type=MESH,
+        )
+
+    plain = units - 3 * width // UNIT
+
+    class Copies:
+        def __init__(self, n):
+            self.n = n
+
+        def whole(self):
+            first = pl.multiple_of(self.n * UNIT, UNIT)
+            return pltpu.make_async_copy(grads.at[self.n], grads_out.at[pl.ds(first, UNIT)], grad_sem.at[self.n])
+
+        def piece(self, q):
+            u = self.n - plain
+            at = 4 * lax.div(u, 2) + q
+            row = pl.multiple_of(lax.div(at, 3) * TILE + lax.rem(u, 2) * UNIT, UNIT)
+            return pltpu.make_async_copy(
+                grads.at[self.n, :, q * width : (q + 1) * width],
+                qkv_out.at[lax.rem(at, 3), pl.ds(row, UNIT)],
+                grad_sem.at[self.n],
+            )
+
+        def start(self):
+            pl.when(self.n < plain)(lambda: self.whole().start())
+
+            @pl.when(self.n >= plain)
+            def _():
+                for q in range(4):
+                    self.piece(q).start()
+
+        def wait(self):
+            pl.when(self.n < plain)(lambda: self.whole().wait())
+
+            @pl.when(self.n >= plain)
+            def _():
+                for q in range(4):
+                    self.piece(q).wait()
+
+    def begin(n):
+        place = lax.rem(lax.div(n, 2), SLOTS // 2)
+        code = 4 * lax.rem(n, 2) + middle
+
+        @pl.when(code < 4)
+        def _():
+            theirs = grads.at[n, pl.ds(rows_of(1 - along_x, half), half)]
+            hop(n, 0, theirs, recv_a.at[place, pl.ds(0, half)], across).start()
+
+        @pl.when(code == 4)
+        def _():
+            hop(n, 0, grads.at[n], recv_b.at[place, pl.ds(0, UNIT)], inward).start()
+
+    def advance(n, stage):
+        kind = jnp.where(n < 0, 2, jnp.where(n >= units, 2, lax.rem(n, 2)))
+        code = 4 * kind + middle
+        place = lax.rem(lax.div(n, 2), SLOTS // 2)
+
+        def case(number):
+            return pl.when(code == number)
+
+        base, box = grads.at[n], recv_a.at[place]
+        mine_at, theirs_at = rows_of(along_x, half), rows_of(1 - along_x, half)
+        own_at = pl.multiple_of(along_x * half + side * quarter, quarter)
+        other_at = pl.multiple_of(along_x * half + (1 - side) * quarter, quarter)
+        own_in, other_in = rows_of(side, quarter), rows_of(1 - side, quarter)
+
+        def rows(first, size):
+            return base.at[pl.ds(first, size)]
+
+        def x_one():
+            return hop(n, 0, rows(theirs_at, half), box.at[pl.ds(0, half)], across)
+
+        def z_one():
+            return hop(n, 1, rows(mine_at, half), box.at[pl.ds(half, half)], inward)
+
+        def z_two():
+            return hop(n, 2, rows(other_at, quarter), box.at[pl.ds(2 * half, quarter)], inward)
+
+        def z_swap():
+            return hop(n, 3, rows(own_at, quarter), box.at[pl.ds(swap_at, quarter)], inward)
+
+        def out(kind, first, place_in):
+            return hop(n, kind, rows(first, quarter), box.at[pl.ds(half + place_in, quarter)], outward)
+
+        def x_two():
+            return hop(n, 6, rows(mine_at, half), box.at[pl.ds(last_at, half)], across)
+
+        swap_at, last_at = 2 * half + quarter, 3 * half
+
+        if stage == 1:
+
+            @case(0)
+            def _():
+                x_one().wait_recv()
+                add_parts(base, mine_at, half, [(box, 0)])
+                z_one().start()
+
+        if stage == 2:
+
+            @case(2)
+            def _():
+                x_one().wait_recv()
+                z_one().wait_recv()
+                add_parts(base, other_at, quarter, [(box, other_in), (box, half + other_in)])
+                z_two().start()
+
+        if stage == 3:
+
+            @case(2)
+            def _():
+                z_two().wait_recv()
+                add_parts(base, own_at, quarter, [(box, own_in), (box, half + own_in), (box, 2 * half)])
+                z_swap().start()
+                out(4, own_at, own_in).start()
+
+        if stage == 4:
+
+            @case(2)
+            def _():
+                z_swap().wait_recv()
+                z_two().wait_send()
+                bring(base, other_at, box, swap_at, quarter)
+                out(5, other_at, other_in).start()
+                x_two().start()
+
+        if stage == 5:
+
+            @case(0)
+            def _():
+                z_one().wait_send()
+                out(4, own_at, own_in).wait_recv()
+                out(5, other_at, other_in).wait_recv()
+                bring(base, mine_at, box, half, half)
+                x_two().start()
+
+        if stage == 6:
+
+            @case(2)
+            def _():
+                z_swap().wait_send()
+                out(4, own_at, own_in).wait_send()
+                out(5, other_at, other_in).wait_send()
+
+            @pl.when(kind == 0)
+            def _():
+                x_one().wait_send()
+                x_two().wait()
+                bring(base, theirs_at, box, last_at, half)
+
+        box_b = recv_b.at[place]
+        mine_z, theirs_z = rows_of(side, half), rows_of(1 - side, half)
+        own_x = pl.multiple_of(side * half + along_x * quarter, quarter)
+        other_x = pl.multiple_of(side * half + (1 - along_x) * quarter, quarter)
+        own_part_at, other_part_at = rows_of(along_x, quarter), rows_of(1 - along_x, quarter)
+
+        def z_in():
+            return hop(n, 0, base, box_b.at[pl.ds(0, UNIT)], inward)
+
+        def z_mid():
+            return hop(n, 1, rows(theirs_z, half), box_b.at[pl.ds(UNIT, half)], inward)
+
+        def x_mid():
+            return hop(n, 2, rows(other_x, quarter), box_b.at[pl.ds(UNIT + half, quarter)], across)
+
+        def x_swap():
+            return hop(n, 3, rows(own_x, quarter), box_b.at[pl.ds(swap_at, quarter)], across)
+
+        def z_share():
+            return hop(n, 4, rows(mine_z, half), box_b.at[pl.ds(last_at, half)], inward)
+
+        def z_out(kind, first):
+            return hop(n, kind, rows(first, half), box_b.at[pl.ds(first, half)], outward)
+
+        swap_at, last_at = UNIT + half + quarter, 2 * UNIT
+
+        if stage == 1:
+
+            @case(6)
+            def _():
+                z_in().wait_recv()
+                add_parts(base, theirs_z, half, [(box_b, theirs_z)])
+                z_mid().start()
+
+        if stage == 2:
+
+            @case(6)
+            def _():
+                z_mid().wait_recv()
+                add_parts(base, other_x, quarter, [(box_b, other_x), (box_b, UNIT + other_part_at)])
+                x_mid().start()
+
+        if stage == 3:
+
+            @case(6)
+            def _():
+                x_mid().wait_recv()
+                add_parts(
+                    base, own_x, quarter, [(box_b, own_x), (box_b, UNIT + own_part_at), (box_b, UNIT + half)]
+                )
+                x_swap().start()
+
+        if stage == 4:
+
+            @case(6)
+            def _():
+                x_swap().wait_recv()
+                x_mid().wait_send()
+                bring(base, other_x, box_b, swap_at, quarter)
+                z_share().start()
+                z_out(5, mine_z).start()
+
+        if stage == 5:
+
+            @case(6)
+            def _():
+                z_share().wait_recv()
+                z_mid().wait_send()
+                bring(base, theirs_z, box_b, last_at, half)
+                z_out(6, theirs_z).start()
+
+        if stage == 6:
+
+            @case(6)
+            def _():
+                x_swap().wait_send()
+                z_share().wait_send()
+                z_out(5, mine_z).wait_send()
+                z_out(6, theirs_z).wait_send()
+
+            @case(4)
+            def _():
+                z_in().wait_send()
+                z_out(5, mine_z).wait_recv()
+                z_out(6, theirs_z).wait_recv()
+                bring(base, 0, box_b, 0, UNIT)
+
+            pl.when(kind < 2)(lambda: Copies(n).start())
+
+    def ready(first, count):
+        for n in (first + k for k in range(count)):
+            if reduce_dp:
+                pl.when(n < SLOTS)(functools.partial(begin, n))
+            else:
+                Copies(n).start()
+
+    def tick(t):
+        if not reduce_dp:
+            return
+        for stage in (6, 5, 4, 3, 2, 1):
+            advance(t - 2 * (stage - 1), stage)
+        later = t + 2
+
+        @pl.when(jnp.where(later < SLOTS, 0, jnp.where(later >= units, 0, 1)) == 1)
+        def _():
+            begin(later)
+
+    def tick_at(j, every, first):
+        @pl.when(lax.rem(j, every) == every - 1)
+        def _():
+            tick(first + lax.div(j, every))
+
+    ticks = units + 10
+
+    def to_mate(which, number):
+        return pltpu.make_async_remote_copy(
+            src_ref=rs_out.at[lax.rem(number, 2)],
+            dst_ref=rs_in.at[number],
+            send_sem=rs_send.at[which, number],
+            recv_sem=rs_recv.at[which, number],
+            device_id={"tensor": mate},
+            device_id_type=MESH,
+        )
+
+    def to_peer(which, number):
+        return pltpu.make_async_remote_copy(
+            src_ref=rs_in.at[number],
+            dst_ref=y_in.at[number],
+            send_sem=rs_send.at[which, 4 + number],
+            recv_sem=rs_recv.at[which, 4 + number],
+            device_id={"tensor": peer},
+            device_id_type=MESH,
+        )
+
+    def scatter(j, which, compute):
+        owner = jnp.where(j < 2, cross, jnp.where(j < 4, peer, mate))
         number = lax.rem(j, 2)
-        if first is None:
-            staged(number, target).wait()
-        else:
-
-            @pl.when(j >= first + 2)
-            def _():
-                staged(number, target).wait()
-
-        stage[number] = tile.astype(BF)
-        staged(number, target).start()
-
-    def drain(target):
+        compute(pl.multiple_of(owner * rows_own + number * TILE, TILE))
+
+        @pl.when(lax.div(j, 2) != 1)
+        def _():
+            at = jnp.where(j < 2, j, j - 2)
+            pl.when(j >= 4)(lambda: to_mate(which, number).wait_send())
+            rs_out[number] = temp[0].astype(BF)
+            to_mate(which, at).start()
+
+        @pl.when(lax.div(j, 2) == 1)
+        def _():
+            to_mate(which, number).wait_recv()
+            add_into_wide(rs_in.at[number])
+            to_peer(which, number).start()
+
+    def add_into_wide(target):
+        def step(i, carry):
+            at = pl.ds(pl.multiple_of(i * SUB, SUB), SUB)
+            target[at, :] = (target[at, :].astype(F32) + temp[0, at, :]).astype(BF)
+            return carry
+
+        lax.fori_loop(0, TILE // SUB, step, 0)
+
+    def gathered(which, number):
+        to_mate(which, 2 + number).wait_recv()
+        to_peer(which, number).wait_recv()
+
+    def settle(which):
         for number in range(2):
-            staged(number, target).wait()
-
-    def produce(j, carry):
-        here = pl.ds(pl.multiple_of(j * TILE, TILE), TILE)
-        tile = dot(mixed[here, :], w_out[...]) + dot(hid[here, :], w_down[...])
-        put(j, tile, out_part.at[here], 0)
-        return carry
-
-    lax.fori_loop(0, rows // TILE, produce, 0)
-    drain(out_part.at[pl.ds(0, TILE)])
+            to_mate(which, 2 + number).wait_send()
+            to_peer(which, number).wait_send()
+
+    def stored(number, target):
+        return pltpu.make_async_copy(rs_out.at[number], target, result_sem.at[number])
 
     for piece in range(2):
         g_cot.forward(cross, piece).wait_recv()
     g_cot.to_mate(mate).wait_recv()
     g_cot.local().wait()
 
+    def keep_unit(n, value):
+        for k in range(value.shape[0] // UNIT):
+            grads[n + k] = value[k * UNIT : (k + 1) * UNIT]
+        ready(n, value.shape[0] // UNIT)
+
+    per_tile = TILE // UNIT
+    first_out = hid.shape[1] // UNIT
+    first_up = first_out + width // UNIT
+
     def down(j, carry):
         at = pl.ds(pl.multiple_of(j * TILE, TILE), TILE)
-        put(j, dot(hid[:, at], cot[...], TN), g_down.at[at], 0)
+        keep_unit(per_tile * j, dot(hid[:, at], cot[...], TN).astype(BF))
         return carry
 
-    lax.fori_loop(0, hid.shape[1] // TILE, down, 0)
-    put(0, dot(mixed[...], cot[...], TN), g_out, None)
-    drain(g_out)
+    with jax.named_scope("grad_down"):
+        lax.fori_loop(0, hid.shape[1] // TILE, down, 0)
+    keep_unit(first_out, dot(mixed[...], cot[...], TN).astype(BF))
+
+    def branch(row0):
+        here = pl.ds(row0, TILE)
+        temp[0] = dot(mixed[here, :], w_out[...]) + dot(hid[here, :], w_down[...])
+
+    def own_copy(number, back=False):
+        held = own_part.at[pl.ds(pl.multiple_of(number * TILE, TILE), TILE)]
+        return pltpu.make_async_copy(*((held, temp.at[0]) if back else (temp.at[0], held)), temp_sem.at[0])
+
+    def produce(j, carry):
+        @pl.when(j < 6)
+        def _():
+            scatter(j, 0, branch)
+
+        @pl.when(j >= 6)
+        def _():
+            branch(pl.multiple_of(me * rows_own + (j - 6) * TILE, TILE))
+            own_copy(j - 6).start()
+            own_copy(j - 6).wait()
+
+        tick_at(j, 4, 0)
+        return carry
+
+    with jax.named_scope("outputs"):
+        lax.fori_loop(0, 8, produce, 0)
+
+    def finish(number, carry):
+        row0 = pl.multiple_of(me * rows_own + number * TILE, TILE)
+        own_copy(number, True).start()
+        own_copy(number, True).wait()
+        gathered(0, number)
+
+        def step(i, inner):
+            at = pl.ds(pl.multiple_of(i * SUB, SUB), SUB)
+            total = temp[0, at, :] + rs_in[2 + number, at, :].astype(F32) + y_in[number, at, :].astype(F32)
+            total = total + tok[pl.ds(pl.multiple_of(row0 + i * SUB, SUB), SUB), :].astype(F32)
+            rs_out[number, at, :] = total.astype(BF)
+            return inner
+
+        lax.fori_loop(0, TILE // SUB, step, 0)
+        stored(number, mixed_out.at[pl.ds(pl.multiple_of(number * TILE, TILE), TILE)]).start()
+        return carry
+
+    def slope(j):
+        here = pl.ds(pl.multiple_of(j * TILE, TILE), TILE)
+        return pltpu.make_async_copy(slopes.at[here], temp.at[lax.rem(j, 2)], temp_sem.at[lax.rem(j, 2)])
 
     def descend(j, carry):
         here = pl.ds(pl.multiple_of(j * TILE, TILE), TILE)
+        slope(j).wait()
+        pl.when(j + 1 < rows // TILE)(lambda: slope(j + 1).start())
         for at in range(0, hid.shape[1], TILE):
             d_hidden = dot(cot[here, :], w_down[at : at + TILE, :], NT)
-            hid[here, at : at + TILE] = (d_hidden * slope[here, at : at + TILE]).astype(BF)
+            hid[here, at : at + TILE] = (d_hidden * temp[lax.rem(j, 2), :, at : at + TILE]).astype(BF)
+        tick_at(j, 4, 2)
         return carry
 
-    lax.fori_loop(0, rows // TILE, descend, 0)
+    with jax.named_scope("grad_gelu"):
+        slope(0).start()
+        lax.fori_loop(0, rows // TILE, descend, 0)
 
     def upward(j, carry):
         at = pl.ds(pl.multiple_of(j * TILE, TILE), TILE)
-        put(j, dot(n_two[:, at], hid[...], TN), g_up.at[at], 0)
+        keep_unit(first_up + per_tile * j, dot(n_two[:, at], hid[...], TN).astype(BF))
+        tick_at(j, 2, 4)
         return carry
 
-    lax.fori_loop(0, n_two.shape[1] // TILE, upward, 0)
-    drain(g_out)
+    with jax.named_scope("grad_up"):
+        lax.fori_loop(0, n_two.shape[1] // TILE, upward, 0)
 
     state[...] = jnp.zeros_like(state)
     krow[...] = jnp.zeros_like(krow)
@@ -388,10 +823,12 @@
 
     def unmix(step, carry):
         i = chunks - 1 - step
+        diag = diag_two[0:width, :].astype(F32)
         row0 = pl.multiple_of(i * CHUNK, CHUNK)
         here = pl.ds(row0, CHUNK)
         query, key, value = (fqkv[here, s * width : (s + 1) * width] for s in range(3))
-        inverse, attended = rden[here, :], att[here, :]
+        attended, packed = att[here, :], rden[here, :]
+        inverse = wide([packed[:, h // 2 * HEAD_DIM // 2 : (h // 2 + 1) * HEAD_DIM // 2] for h in range(2 * heads)])
         d_over = dot(cot[here, :], w_out[...], NT) * inverse
         high, low = split(d_over * attended)
         d_under = -dot(wide([high, low]), diag_two[...])
@@ -418,14 +855,15 @@
         parts = list(zip(*map(halves, (query, key, value, over_both, over_high, over_low, d_under))))
         for k in reversed(range(len(parts))):
             query_k, key_k, value_k, both_k, high_k, low_k, under_k = parts[k]
-            carried, row = states[2 * i + k], ksums[2 * i + k][0:1, :]
+            carried = wide([states[2 * i + k]] * heads, 0) * diag_two[0:width, :]
+            row = ksums[2 * i + k][0:1, :]
             more_query.insert(0, dot(both_k, wide([carried, carried]), NT) + under_k * row)
             keep = joined(2 * i + k + 1)
             later_high, later_low = split(later * keep)
             more_key.insert(0, dot(wide([value_k, value_k]), wide([later_high, later_low]), NT) + later_row * keep)
             more_value.insert(0, dot(wide([key_k, key_k]), wide([later_high, later_low], 0)))
             add = dot(wide([query_k, query_k], 0), wide([high_k, low_k], 0), TN)
-            later = later * keep + add * diag[...]
+            later = later * keep + add * diag
             later_row = later_row * keep + jnp.sum(query_k.astype(F32) * under_k, 0, keepdims=True)
         state[...] = later
         krow[0:1, :] = later_row
@@ -439,73 +877,183 @@
             feat_sums[0:1, :] += jnp.sum(grad * spectrum, 0, keepdims=True)
             feat_sums[1:2, :] += jnp.sum(grad, 0, keepdims=True)
             high, low = split(grad * scale_row)
-            fqkv[here, s * width : (s + 1) * width] = rotate(
-                dot(wide([high, low, high]), dct_bwd[...]), turn, True
-            ).astype(BF)
+            turned = dot(high, dct[:, 0:width]) + dot(low, dct[:, 0:width]) + dot(high, dct[:, 2 * width :])
+            fqkv[here, s * width : (s + 1) * width] = rotate(turned, turn, True).astype(BF)
         fqkv[here, 2 * width : 3 * width] = d_value.astype(BF)
+
+        tick_at(step, 2, 6)
         return carry
 
-    lax.fori_loop(0, chunks, unmix, 0)
-
-    def projected(j, carry):
-        at = pl.ds(pl.multiple_of(j * TILE, TILE), TILE)
-        number = lax.rem(j, 2)
-        tile = dot(n_one[:, at], fqkv[...], TN)
-
-        def piece(s):
-            return pltpu.make_async_copy(
-                stage.at[number, :, s * width : (s + 1) * width], g_qkv.at[s, at], stage_sem.at[number]
-            )
-
-        @pl.when(j >= 2)
-        def _():
-            for s in range(3):
-                piece(s).wait()
-
-        stage[number, :, 0 : 3 * width] = tile.astype(BF)
+    with jax.named_scope("mixer_back"):
+        lax.fori_loop(0, chunks, unmix, 0)
+
+    for j in range(n_one.shape[1] // TILE):
+        tile = dot(n_one[:, j * TILE : (j + 1) * TILE], fqkv[...], TN).astype(BF)
         for s in range(3):
-            piece(s).start()
+            at = 3 * j + s
+            for k in range(per_tile):
+                grads[plain + at // 4 * per_tile + k, :, at % 4 * width : (at % 4 + 1) * width] = tile[
+                    k * UNIT : (k + 1) * UNIT, s * width : (s + 1) * width
+                ]
+        if j:
+            ready(plain + (j - 1) * per_tile, per_tile)
+
+    def pause(t, carry):
+        tick(t)
         return carry
 
-    lax.fori_loop(0, n_one.shape[1] // TILE, projected, 0)
-    for number in range(2):
-        for s in range(3):
-            pltpu.make_async_copy(
-                stage.at[number, :, s * width : (s + 1) * width], g_qkv.at[s, pl.ds(0, TILE)], stage_sem.at[number]
-            ).wait()
+    lax.fori_loop(14, 16, pause, 0)
 
     sums[...] = jnp.zeros_like(sums)
 
-    def inputs(j, carry):
-        row0 = pl.multiple_of(j * TILE, TILE)
+    def row_grads(row0):
         here = pl.ds(row0, TILE)
         total = dot(fqkv[here, 0:width], w_qkv[0], NT)
         for s in (1, 2):
             total = total + dot(fqkv[here, s * width : (s + 1) * width], w_qkv[s], NT)
-        wide_one[...] = total
-        wide_two[...] = dot(hid[here, :], w_up[...], NT)
+        temp[0] = total
+        temp[1] = dot(hid[here, :], w_up[...], NT)
 
         def fold(i, inner):
             at = pl.ds(pl.multiple_of(i * SUB, SUB), SUB)
             unit, _ = centered(pl.multiple_of(row0 + i * SUB, SUB), SUB)
-            one, two = wide_one[at, :], wide_two[at, :]
+            one, two = temp[0, at, :], temp[1, at, :]
             for number, term in enumerate((one * unit, one, two * unit, two)):
                 sums[number] += jnp.sum(term.reshape(SUB // 8, 8, term.shape[1]), 0)
-            wide_one[at, :] = one * gain_one + two * gain_two
+            temp[0, at, :] = one * gain_one + two * gain_two
             return inner
 
         lax.fori_loop(0, TILE // SUB, fold, 0)
-        put(j, wide_one[...], back_part.at[here], 0)
+
+    with jax.named_scope("finish"):
+        settle(0)
+        lax.fori_loop(0, 2, finish, 0)
+    for number in range(2):
+        stored(number, mixed_out.at[pl.ds(0, TILE)]).wait()
+    pl.semaphore_signal(free_mate, inc=1, device_id={"tensor": mate}, device_id_type=MESH)
+    pl.semaphore_signal(free_peer, inc=1, device_id={"tensor": peer}, device_id_type=MESH)
+    pl.semaphore_wait(free_mate, 1)
+    pl.semaphore_wait(free_peer, 1)
+
+    def inputs(j, carry):
+        scatter(j, 1, row_grads)
+        tick(16 + j)
         return carry
 
-    lax.fori_loop(0, rows // TILE, inputs, 0)
-    drain(back_part.at[pl.ds(0, TILE)])
+    with jax.named_scope("row_grads"):
+        lax.fori_loop(0, 6, inputs, 0)
+    settle(1)
+
+    def conclude(number, carry):
+        row0 = pl.multiple_of(me * rows_own + number * TILE, TILE)
+        row_grads(row0)
+        gathered(1, number)
+
+        def step(i, inner):
+            at = pl.ds(pl.multiple_of(i * SUB, SUB), SUB)
+            group_at = pl.multiple_of(row0 + i * SUB, SUB)
+            unit, deviation = centered(group_at, SUB)
+            total = temp[0, at, :] + rs_in[2 + number, at, :].astype(F32) + y_in[number, at, :].astype(F32)
+            along = jnp.mean(total * unit, -1, keepdims=True)
+            total = total - jnp.mean(total, -1, keepdims=True) - unit * along
+            total = cot[pl.ds(group_at, SUB), :].astype(F32) + deviation * total
+            rs_out[number, at, :] = total.astype(BF)
+            return inner
+
+        lax.fori_loop(0, TILE // SUB, step, 0)
+        stored(number, input_grad.at[pl.ds(pl.multiple_of(number * TILE, TILE), TILE)]).start()
+        tick(22 + number)
+        return carry
+
+    with jax.named_scope("conclude"):
+        lax.fori_loop(0, 2, conclude, 0)
+
     small[...] = jnp.zeros_like(small)
     for number in range(4):
         small[number : number + 1, :] = jnp.sum(sums[number], 0, keepdims=True)
     small[4:5, 0:width] = feat_sums[0:1, :]
     small[5:6, 0:width] = feat_sums[1:2, :] / weight_row
 
+    def small_hop(number, device, count=8):
+        return pltpu.make_async_remote_copy(
+            src_ref=small,
+            dst_ref=small_in.at[number],
+            send_sem=small_send.at[number],
+            recv_sem=small_recv.at[number],
+            device_id=device,
+            device_id_type=MESH,
+        )
+
+    row_number = lax.broadcasted_iota(jnp.int32, small.shape, 0)
+    over_tensor = jnp.where(row_number < 4, 1.0, 0.0).astype(F32)
+    to_both = [small_hop(0, {"tensor": mate}), small_hop(1, {"tensor": peer}), small_hop(2, {"dp": across})]
+    inner, centre, outer = small_hop(3, {"dp": inward}), small_hop(4, {"dp": inward}), small_hop(5, {"dp": outward})
+
+    def add_small(number):
+        to_both[number].wait()
+        small[...] += small_in[number] * over_tensor if number < 2 else small_in[number]
+
+    def small_step(k):
+        if k < 3:
+            if k:
+                add_small(k - 1)
+            if k < 2 or reduce_dp:
+                to_both[k].start()
+        if not reduce_dp:
+            return
+        if k == 3:
+            add_small(2)
+            at_end(inner.start)
+        if k == 4:
+
+            @at_mid
+            def _():
+                inner.wait_recv()
+                small[...] += small_in[3]
+                centre.start()
+
+        if k == 5:
+
+            @at_mid
+            def _():
+                centre.wait()
+                small[...] += small_in[4]
+                outer.start()
+
+        if k == 6:
+            at_mid(outer.wait_send)
+
+            @at_end
+            def _():
+                inner.wait_send()
+                outer.wait_recv()
+                small[...] = small_in[5]
+
+    if reduce_dp:
+
+        def rest(t, carry):
+            for k in range(7):
+                pl.when(t == 24 + k)(functools.partial(small_step, k))
+            tick(t)
+            return carry
+
+        lax.fori_loop(24, ticks, rest, 0)
+    else:
+        for k in range(3):
+            small_step(k)
+    for h in range(heads):
+        at = slice(h * HEAD_DIM, (h + 1) * HEAD_DIM)
+        feat_out[0, h : h + 1, :] = small[4:5, at]
+        feat_out[1, h : h + 1, :] = small[5:6, at]
+
+    def copied(n, carry):
+        Copies(n).wait()
+        return carry
+
+    lax.fori_loop(0, units, copied, 0)
+    for number in range(2):
+        stored(number, input_grad.at[pl.ds(0, TILE)]).wait()
+
     for gather in (g_tok, g_cot):
         gather.to_mate(me).wait_send()
         for piece in range(2):
@@ -514,6 +1062,7 @@
 
 
 def shards(
+    reduce_dp,
     tokens,
     ln1_gain,
     ln1_bias,
@@ -534,69 +1083,81 @@
     width = heads * HEAD_DIM
     hidden = w_up.shape[1]
     consts = tables(rows // BLOCK, heads)
-    norms = jnp.stack([ln1_gain, ln1_bias, ln2_gain, ln2_bias])
-    feature = jnp.stack([feature_scale.reshape(-1), feature_weight.reshape(-1)])
+    norms = [value.reshape(1, model) for value in (ln1_gain, ln1_bias, ln2_gain, ln2_bias)]
     anywhere = pl.BlockSpec(memory_space=pl.ANY)
     vmem = pl.BlockSpec(memory_space=pltpu.VMEM)
     smem = pl.BlockSpec(memory_space=pltpu.SMEM)
     shape = jax.ShapeDtypeStruct
-    out_part, back_part, g_down, g_out, g_up, g_qkv, small = pl.pallas_call(
-        kernel,
+    plain = 2 * hidden + width
+    units = (plain + 3 * width) // UNIT
+    mixed_out, input_grad, grads, g_qkv, _, _, small, feats = pl.pallas_call(
+        functools.partial(kernel, reduce_dp),
         out_shape=(
-            shape((rows, model), BF),
-            shape((rows, model), BF),
-            shape((hidden, model), BF),
-            shape((width, model), BF),
-            shape((model, hidden), BF),
+            shape((rows_own, model), BF),
+            shape((rows_own, model), BF),
+            shape((plain, model), BF),
             shape((3, model, width), BF),
+            shape((rows, hidden), F32),
+            shape((rows_own, model), F32),
             shape((8, model), F32),
+            shape((2, heads, HEAD_DIM), F32),
         ),
-        in_specs=[smem, anywhere, anywhere] + [vmem] * 12,
-        out_specs=(anywhere,) * 6 + (vmem,),
+        in_specs=[smem, anywhere, anywhere] + [vmem] * 14,
+        out_specs=(anywhere,) * 6 + (vmem, vmem),
         scratch_shapes=[
             pltpu.VMEM((rows, model), BF),
             pltpu.VMEM((rows, model), BF),
             pltpu.VMEM((rows, model), BF),
             pltpu.VMEM((rows, model), BF),
             pltpu.VMEM((rows, hidden), BF),
-            pltpu.VMEM((rows, hidden), F32),
             pltpu.VMEM((rows, 3 * width), BF),
             pltpu.VMEM((2, rows, width), F32),
             pltpu.VMEM((rows, width), BF),
             pltpu.VMEM((rows, width), F32),
-            pltpu.VMEM((rows, width), F32),
-            pltpu.VMEM((rows // BLOCK, width, width), BF),
+            pltpu.VMEM((rows, width // 2), F32),
+            pltpu.VMEM((rows // BLOCK, HEAD_DIM, width), BF),
             pltpu.VMEM((rows // BLOCK, 8, width), F32),
             pltpu.VMEM((width, width), F32),
             pltpu.VMEM((8, width), F32),
+            pltpu.VMEM((units, UNIT, model), BF),
+            pltpu.VMEM((SLOTS // 2, 2 * UNIT, model), BF),
+            pltpu.VMEM((SLOTS // 2, 5 * UNIT // 2, model), BF),
             pltpu.VMEM((2, TILE, model), BF),
-            pltpu.VMEM((TILE, model), F32),
-            pltpu.VMEM((TILE, model), F32),
+            pltpu.VMEM((4, TILE, model), BF),
+            pltpu.VMEM((2, TILE, model), BF),
+            pltpu.VMEM((2, TILE, model), F32),
             pltpu.VMEM((4, 8, model), F32),
             pltpu.VMEM((8, width), F32),
+            pltpu.VMEM((6, 8, model), F32),
             pltpu.SemaphoreType.DMA((10,)),
             pltpu.SemaphoreType.DMA((10,)),
             pltpu.SemaphoreType.DMA((10,)),
+            pltpu.SemaphoreType.DMA((units, 7)),
+            pltpu.SemaphoreType.DMA((units, 7)),
+            pltpu.SemaphoreType.DMA((2, 6)),
+            pltpu.SemaphoreType.DMA((2, 6)),
+            pltpu.SemaphoreType.DMA((6,)),
+            pltpu.SemaphoreType.DMA((6,)),
+            pltpu.SemaphoreType.DMA((units,)),
             pltpu.SemaphoreType.DMA((2,)),
+            pltpu.SemaphoreType.DMA((2,)),
+            pltpu.SemaphoreType.REGULAR,
+            pltpu.SemaphoreType.REGULAR,
         ],
         compiler_params=pltpu.CompilerParams(
-            collective_id=0, has_side_effects=True, vmem_limit_bytes=63 * 2**20
+            collective_id=0, has_side_effects=True, vmem_limit_bytes=62 * 2**20
         ),
-    )(lengths, tokens, cotangent, norms, w_qkv, w_out, w_up, w_down, feature, *consts)
-    branches = lax.psum_scatter(out_part.astype(F32), "tensor", scatter_dimension=0, tiled=True).astype(F32)
-    mixed_out = (tokens.astype(F32) + branches).astype(BF)
-    d_rows = lax.psum_scatter(back_part.astype(F32), "tensor", scatter_dimension=0, tiled=True).astype(F32)
-    rows_in = tokens.astype(F32)
-    unit = rows_in - jnp.mean(rows_in, -1, keepdims=True)
-    deviation = lax.rsqrt(jnp.mean(unit * unit, -1, keepdims=True) + 1e-05)
-    unit = unit * deviation
-    inner = d_rows - jnp.mean(d_rows, -1, keepdims=True) - unit * jnp.mean(d_rows * unit, -1, keepdims=True)
-    input_grad = (cotangent.astype(F32) + deviation * inner).astype(BF)
-    g_down, g_out, g_up, g_qkv = (
-        lax.psum(tuple(g.astype(F32) for g in (g_down, g_out, g_up, g_qkv)), "dp")
+    )(lengths, tokens, cotangent, *norms, w_qkv, w_out, w_up, w_down, feature_scale, feature_weight, *consts)
+    norm_sums = small[0:4]
+    if not reduce_dp:
+        grads, g_qkv, norm_sums, feats = lax.psum(
+            (*lax.optimization_barrier((grads.astype(F32), g_qkv.astype(F32))), norm_sums, feats), "dp"
+        )
+    g_down, g_out, g_up = (
+        grads[first:last].astype(F32)
+        for first, last in ((0, hidden), (hidden, hidden + width), (hidden + width, plain))
     )
-    norm_sums = lax.psum(small[0:4], ("dp", "tensor"))
-    feat_sums = lax.psum(small[4:6, 0:width], "dp").reshape(2, heads, HEAD_DIM)
+    g_qkv = g_qkv.astype(F32)
     return (
         mixed_out,
         input_grad,
@@ -608,8 +1169,8 @@
         g_out,
         g_up,
         g_down,
-        feat_sums[0],
-        feat_sums[1],
+        feats[0],
+        feats[1],
     )
 
 
@@ -630,7 +1191,7 @@
         P(("dp", "tensor"), None),
     )
     return jax.shard_map(
-        shards,
+        functools.partial(shards, mesh.shape["dp"] == 8),
         mesh=mesh,
         in_specs=placed,
         out_specs=(

time: 709 us -> 250 us (0.35)
  blocking collectives: 526 us -> 0 us
  Pallas kernels: 140 us -> 234 us
  between operations: 14.1 us -> 0.67 us
  other arithmetic: 22.2 us -> 11 us
    psum x2 -> x0, blocking collectives: 526 us -> none  [the longest x1 488 us: shards(): lax.psum(tuple((g.astype(F32) for g in (g_down, g_out, g_up, g_qkv))), 'dp')]
    pallas_call x1, Pallas kernels: 140 us -> 234 us  [shards(): pl.pallas_call(functools.partial(kernel, reduce_dp), out_shape=(shape((ro...]
  transfers between devices with their start and end apart: 2 -> 0, of which waited for: 0 -> 0; matrix products, arithmetic and copies ran while one was open for 2% -> 0% of each run, Pallas kernels for 0% -> 0%
where the time goes in v2:
time: 250 us
  Pallas kernels  234 us (94%)
  other arithmetic  11 us (4%)
  local copies, waits for them, and re-layouts  4.06 us (2%)
    pallas_call x1, Pallas kernels, shards(): pl.pallas_call(functools.partial(kernel, reduce_dp), out_shape=(shape((ro...  234 us
    convert_element_type x2, other arithmetic, shards(): grads[first:last].astype(F32)  9.06 us

profile of v2, /device:TPU:0, one launch (start us, length us, event | category | flops | bytes accessed | tf_op | source)
XLA Modules:
  0.0 249.6 jit_solution(5188676553837463319)
XLA Ops:
  0.6 233.9 %shard_map.256 = (bf16[512,1024]{1,0:T(8,128)(2,1)}, bf16[512,1024]{1,0:T(8,128)(2,1)}, bf16[2304,1024]{1,0:T(8,128)(2,1)}, bf16[3,1024,256]{2,1,0:T(8,128)(2,1)...) custom-call(s32[1,3]{1,0:T(1,128)} %lengths.1, ...), custom_call_target="tpu_custom_call" | custom-call | tf_op jit(solution)/shard_map/pallas_call | solution.py:1093
  234.6 1.5 fusion
  236.1 0.0 copy-start.3
  236.1 0.0 copy-start
  236.1 6.8 %slice_convert_fusion = (f32[1024,1024]{1,0:T(8,128)}, f32[1024,1024]{1,0:T(8,128)}) fusion(bf16[2304,1024]{1,0:T(8,128)(2,1)} %get-tuple-element.22), kind=kLoop, calls=%fused_computation | loop fusion | flops 2097152 | bytes 12582912 | tf_op jit(solution)/shard_map/convert_element_type | solution.py:1157
  242.9 0.0 copy-start.2
  242.9 0.0 copy-start.1
  242.9 2.3 slice_convert_fusion.2
  245.2 0.0 copy-done.3
  245.2 0.6 slice_bitcast_fusion
  245.8 0.0 copy-done
  245.8 1.9 convert_element_type.12
  247.7 0.0 copy-done.2
  247.7 1.0 copy.31
  248.7 0.0 copy-done.1
  248.7 1.0 copy.32
Async XLA Ops:
  236.1 9.1 %copy-start.3 = (f32[2,4,64]{2,1,0:T(4,128)S(1)}, f32[2,4,64]{2,1,0:T(4,128)}, u32[]{:S(2)}) copy-start(f32[2,4,64]{2,1,0:T(4,128)} %get-tuple-element.23) | copy-start | bytes 6148
  236.1 9.7 %copy-start = (bf16[3,1024,256]{2,1,0:T(8,128)(2,1)S(1)}, bf16[3,1024,256]{2,1,0:T(8,128)(2,1)}, u32[]{:S(2)}) copy-start(bf16[3,1024,256]{2,1,0:T(8,128)(2,1)} %get-tuple-element.21) | copy-start | bytes 4718596
  242.9 4.8 %copy-start.2 = (bf16[512,1024]{1,0:T(8,128)(2,1)S(1)}, bf16[512,1024]{1,0:T(8,128)(2,1)}, u32[]{:S(2)}) copy-start(bf16[512,1024]{1,0:T(8,128)(2,1)} %get-tuple-element.44) | copy-start | bytes 3145732
  242.9 5.8 %copy-start.1 = (bf16[512,1024]{1,0:T(8,128)(2,1)S(1)}, bf16[512,1024]{1,0:T(8,128)(2,1)}, u32[]{:S(2)}) copy-start(bf16[512,1024]{1,0:T(8,128)(2,1)} %get-tuple-element.45) | copy-start | bytes 3145732

commit v3 on v2

v3 whole, which is shorter than its diff:
```python
import functools
import math

import jax
import jax.numpy as jnp
import ml_dtypes
import numpy as np
from jax import lax
from jax.experimental import pallas as pl
from jax.experimental.pallas import tpu as pltpu
from jax.sharding import PartitionSpec as P

HEAD_DIM = 64
ROT = 16
BLOCK = 64
CHUNK = 128
TILE = 256
UNIT = 128
SUB = 32
SLOTS = 12
MESH = pl.DeviceIdType.MESH
F32 = jnp.float32
BF = jnp.bfloat16
NN = (((1,), (0,)), ((), ()))
NT = (((1,), (1,)), ((), ()))
TN = (((0,), (0,)), ((), ()))


def dot(left, right, dims=NN):
    return lax.dot_general(left, right, dims, preferred_element_type=F32)


def split(value):
    high = value.astype(BF)
    return high, (value - high.astype(F32)).astype(BF)


def wide(parts, axis=1):
    return jnp.concatenate(parts, axis)


def tables(blocks, heads):
    width = heads * HEAD_DIM
    freq, dims = np.arange(HEAD_DIM)[:, None], np.arange(HEAD_DIM)[None, :]
    dct = np.cos(np.pi * (dims + 0.5) * freq / HEAD_DIM) * math.sqrt(2.0 / HEAD_DIM)
    dct[0] *= math.sqrt(0.5)
    dct = np.kron(np.eye(heads), dct).astype(np.float32)
    high = dct.astype(ml_dtypes.bfloat16)
    low = (dct - high.astype(np.float32)).astype(ml_dtypes.bfloat16)
    halves = np.concatenate([high, high, low], 1)
    half = ROT // 2
    lane = np.arange(2 * HEAD_DIM) % HEAD_DIM
    rate = np.where(lane < ROT, 10000.0 ** (-(lane % half) * 2.0 / ROT), 0.0)
    in_block = np.arange(BLOCK)[:, None] * rate[None]
    of_block = np.arange(blocks)[:, None] * BLOCK * rate[None]
    signs = np.stack([np.where(lane < half, -1.0, 0.0), np.where((lane >= half) & (lane < ROT), 1.0, 0.0)] + [0.0 * lane] * 6)
    angles = np.concatenate([np.cos(in_block), np.sin(in_block), np.cos(of_block), np.sin(of_block), signs], 0)
    diagonal = np.kron(np.eye(heads), np.ones((HEAD_DIM, HEAD_DIM)))
    masks = np.kron(np.eye(heads), np.ones((CHUNK, HEAD_DIM)))
    return (
        halves,
        angles.astype(np.float32),
        np.concatenate([diagonal, diagonal], 0).astype(ml_dtypes.bfloat16),
        masks.astype(ml_dtypes.bfloat16),
    )


def kernel(
    reduce_dp,
    lengths,
    tok_in,
    cot_in,
    gain_one_in,
    bias_one_in,
    gain_two_in,
    bias_two_in,
    w_qkv_in,
    w_out_in,
    w_up_in,
    w_down_in,
    feature_scale,
    feature_weight,
    dct,
    angles,
    diag_two,
    masks,
    mixed_out,
    input_grad,
    grads_out,
    qkv_out,
    slopes,
    own_part,
    tok_kept,
    small,
    feat_out,
    tok_tile,
    cot,
    n_one,
    n_two,
    hid,
    fqkv,
    spec,
    mixed,
    att,
    rden,
    states,
    ksums,
    state,
    krow,
    grads,
    recv_a,
    recv_b,
    rs_out,
    rs_in,
    y_in,
    temp,
    sums,
    feat_sums,
    small_in,
    small_wide,
    w_qkv,
    w_out,
    w_up,
    w_down,
    local_sem,
    send_sem,
    recv_sem,
    weight_sem,
    ar_send,
    ar_recv,
    rs_send,
    rs_recv,
    small_send,
    small_recv,
    grad_sem,
    temp_sem,
    tok_sem,
    result_sem,
    free_mate,
    free_peer,
):
    rows_own = tok_in.shape[0]
    rows = cot.shape[0]
    tok = grads
    width = w_out_in.shape[0]
    heads = width // HEAD_DIM
    chunks = rows // CHUNK
    me = lax.axis_index("tensor")
    core = lax.rem(me, 2)
    mate = me + 1 - 2 * core
    peer = lax.rem(me + 2, 4)
    cross = 3 - me
    group = lax.axis_index("dp")
    along_x = lax.rem(group, 2)
    across = group + 1 - 2 * along_x
    along_z = lax.div(group, 2)
    middle = along_z * (3 - along_z)

    def at_end(step):
        pl.when(middle == 0)(step)

    def at_mid(step):
        pl.when(middle > 0)(step)

    side = jnp.where(along_z < 2, 0, 1)
    inward = group + 2 - 4 * side
    outward = group - 2 + 4 * side
    units = grads.shape[0] // UNIT

    weight_copies = [
        pltpu.make_async_copy(source, target, weight_sem.at[k])
        for k, (source, target) in enumerate(
            ((w_qkv_in, w_qkv), (w_up_in, w_up), (w_out_in, w_out), (w_down_in, w_down))
        )
    ]
    for copy in weight_copies:
        copy.start()

    barrier = pltpu.get_barrier_semaphore()
    members = 8 if reduce_dp else 1
    for step in range(1, 4):
        other = lax.rem(me + step, 4)
        pl.semaphore_signal(barrier, inc=1, device_id={"tensor": other}, device_id_type=MESH)
    for step in range(1, members):
        other = lax.rem(group + step, members)
        pl.semaphore_signal(barrier, inc=1, device_id={"dp": other}, device_id_type=MESH)
    pl.semaphore_wait(barrier, 2 + members)

    def slot(buf, owner, piece=None, columns=False):
        if piece is None:
            return buf.at[pl.ds(pl.multiple_of(owner * rows_own, rows_own), rows_own)]
        if columns:
            here = pl.ds(pl.multiple_of(owner * rows_own, rows_own), rows_own)
            return buf.at[here, piece * TILE : (piece + 1) * TILE]
        return buf.at[pl.ds(pl.multiple_of(owner * rows_own + piece * UNIT, UNIT), UNIT)]

    class Gather:
        def __init__(self, source, buf, base, columns):
            self.source, self.buf, self.base, self.columns = source, buf, base, columns
            self.pieces = source.shape[1] // TILE if columns else source.shape[0] // UNIT

        def copy(self, number, src, dst, target):
            return pltpu.make_async_remote_copy(
                src_ref=src,
                dst_ref=dst,
                send_sem=send_sem.at[self.base + number],
                recv_sem=recv_sem.at[self.base + number],
                device_id={"tensor": target},
                device_id_type=MESH,
            )

        def local(self):
            return pltpu.make_async_copy(self.source, slot(self.buf, me), local_sem.at[self.base])

        def to_mate(self, owner):
            return self.copy(0, self.source, slot(self.buf, owner), mate)

        def to_peer(self, owner, piece):
            if self.columns:
                part = self.source.at[:, piece * TILE : (piece + 1) * TILE]
            else:
                part = self.source.at[pl.ds(piece * UNIT, UNIT)]
            return self.copy(1 + piece, part, slot(self.buf, owner, piece, self.columns), peer)

        def forward(self, owner, piece):
            part = slot(self.buf, owner, piece, self.columns)
            return self.copy(1 + self.pieces + piece, part, part, mate)

    g_tok, g_cot = Gather(tok_in, tok, 0, False), Gather(cot_in, cot, 1 + 2 * (rows_own // UNIT), True)
    g_tok.to_mate(me).start()
    for piece in range(g_tok.pieces):
        g_tok.to_peer(me, piece).start()
    g_tok.local().start()
    g_cot.to_mate(me).start()
    g_cot.local().start()

    start_one = lengths[0, 0]
    start_two = start_one + lengths[0, 1]

    def segment(block):
        return (block >= start_one).astype(jnp.int32) + (block >= start_two).astype(jnp.int32)

    def in_sequence(block):
        return block - jnp.where(block >= start_two, start_two, jnp.where(block >= start_one, start_one, 0))

    gain_one, bias_one, gain_two, bias_two = gain_one_in[...], bias_one_in[...], gain_two_in[...], bias_two_in[...]
    scale_row, weight_row = (
        wide([field[h : h + 1, :] for h in range(heads)]) for field in (feature_scale, feature_weight)
    )
    blocks = rows // BLOCK

    def rotation(row0, count):
        cos_in, sin_in = angles[0:BLOCK, :], angles[BLOCK : 2 * BLOCK, :]
        sign_a = angles[2 * BLOCK + 2 * blocks : 2 * BLOCK + 2 * blocks + 1, :]
        sign_b = angles[2 * BLOCK + 2 * blocks + 1 : 2 * BLOCK + 2 * blocks + 2, :]
        cosines, sines = [], []
        for k in range(count):
            place = in_sequence(lax.div(row0, BLOCK) + k)
            cos_at = angles[pl.ds(2 * BLOCK + place, 1), :]
            sin_at = angles[pl.ds(2 * BLOCK + blocks + place, 1), :]
            cosines.append(cos_in * cos_at - sin_in * sin_at)
            sines.append(sin_in * cos_at + cos_in * sin_at)
        cosine, sine = wide(cosines, 0), wide(sines, 0)
        return cosine, sine * sign_a, sine * sign_b

    def rotate(field, turn, back=False):
        cosine, sine_a, sine_b = turn
        parts = []
        for at in range(0, width, 2 * HEAD_DIM):
            part = field[:, at : at + 2 * HEAD_DIM]
            ahead = pltpu.roll(part, 2 * HEAD_DIM - ROT // 2, 1) * sine_a
            behind = pltpu.roll(part, ROT // 2, 1) * sine_b
            parts.append(part * cosine - (ahead + behind) if back else part * cosine + (ahead + behind))
        return wide(parts)

    def centered(source, at, size):
        value = source[pl.ds(at, size), :].astype(F32)
        value = value - jnp.mean(value, -1, keepdims=True)
        deviation = lax.rsqrt(jnp.mean(value * value, -1, keepdims=True) + 1e-05)
        return value * deviation, deviation

    chip_row = pl.multiple_of(lax.div(me, 2) * 2 * rows_own, rows_own)

    def slope_copy(p, back=False):
        held = slopes.at[pl.ds(pl.multiple_of(p * TILE, TILE), TILE)]
        slot_of = temp.at[lax.rem(p, 2)]
        return pltpu.make_async_copy(*((held, slot_of) if back else (slot_of, held)), temp_sem.at[lax.rem(p, 2)])

    def project(j, carry):
        @pl.when(j == 0)
        def _():
            g_tok.local().wait()

            g_cot.local().wait()

        @pl.when(j == 2)
        def _():
            g_tok.to_mate(mate).wait_recv()
            g_cot.to_mate(mate).wait_recv()

        for piece in range(g_tok.pieces):

            @pl.when(j == 4 + piece)
            def _():
                g_tok.to_peer(peer, piece).wait_recv()
                g_tok.forward(peer, piece).start()
                g_cot.to_peer(me, piece).start()
                g_tok.forward(cross, piece).wait_recv()

        late = lax.div(j, 4)
        early_at = jnp.where(j < 2, me, mate) * rows_own + lax.rem(j, 2) * TILE
        row_a = pl.multiple_of(jnp.where(late == 0, early_at, peer * rows_own + (j - 4) * UNIT), UNIT)
        row_b = pl.multiple_of(jnp.where(late == 0, early_at + UNIT, cross * rows_own + (j - 4) * UNIT), UNIT)
        here = [pl.ds(row_a, UNIT), pl.ds(row_b, UNIT)]

        def norm(i, inner):
            for row0 in (row_a, row_b):
                at = pl.multiple_of(row0 + i * SUB, SUB)
                unit, _ = centered(tok, at, SUB)
                n_one[pl.ds(at, SUB), :] = (unit * gain_one + bias_one).astype(BF)
                n_two[pl.ds(at, SUB), :] = (unit * gain_two + bias_two).astype(BF)
            return inner

        lax.fori_loop(0, UNIT // SUB, norm, 0)
        first = wide([n_one[at, :] for at in here], 0)
        turn = [wide(pair, 0) for pair in zip(*(rotation(at, UNIT // BLOCK) for at in (row_a, row_b)))]

        def keep(write, value):
            for k, at in enumerate(here):
                write(at, value[k * UNIT : (k + 1) * UNIT])

        def keep_field(s, value):
            def write(at, part):
                fqkv[at, s * width : (s + 1) * width] = part

            keep(write, value.astype(BF))

        for s in range(2):
            high, low = split(rotate(dot(first, w_qkv[s]), turn))
            spectrum = dot(wide([high, low]), dct[:, 0 : 2 * width], NT) + dot(high, dct[:, 2 * width :], NT)

            def keep_spectrum(at, part):
                spec[s, at, :] = part

            keep(keep_spectrum, spectrum)
            keep_field(s, weight_row * jnp.exp(scale_row * spectrum))
        keep_field(2, dot(first, w_qkv[2]))
        second = wide([n_two[at, :] for at in here], 0)
        parity = lax.rem(j, 2)
        pl.when(j >= 6)(lambda: slope_copy(j - 6).wait())
        for at in range(0, w_up.shape[1], TILE):
            up = dot(second, w_up[:, at : at + TILE])
            below = 0.5 * (1.0 + lax.erf(up * math.sqrt(0.5)))

            def keep_hidden(rows_at, part):
                hid[rows_at, at : at + TILE] = part

            keep(keep_hidden, (up * below).astype(BF))
            temp[parity, :, at : at + TILE] = below + up * (
                jnp.exp(-0.5 * up * up) * (1.0 / math.sqrt(2.0 * math.pi))
            )

        @pl.when(late == 0)
        def _():
            turned = wide([cot[at, :] for at in here], 0)
            first_at = pl.multiple_of(rows + row_a - chip_row, TILE)
            for at in range(0, hid.shape[1], TILE):
                d_hidden = dot(turned, w_down[at : at + TILE, :], NT)
                grads[pl.ds(first_at, TILE), at : at + TILE] = (d_hidden * temp[parity, :, at : at + TILE]).astype(BF)

        pl.when(late == 1)(lambda: slope_copy(j - 4).start())
        return carry

    for copy in weight_copies:
        copy.wait()
    with jax.named_scope("project"):
        lax.fori_loop(0, rows // TILE, project, 0)
    for p in (2, 3):
        slope_copy(p).wait()
    keep_tok = pltpu.make_async_copy(tok.at[pl.ds(0, rows)], tok_kept, tok_sem.at[0])
    keep_tok.start()

    grid_t = lax.broadcasted_iota(jnp.int32, (CHUNK, CHUNK), 0)
    grid_s = lax.broadcasted_iota(jnp.int32, (CHUNK, CHUNK), 1)
    together = (grid_t < BLOCK) == (grid_s < BLOCK)
    causal = wide([jnp.where((grid_t >= grid_s) & together, 1.0, 0.0).astype(F32)] * heads)
    causal_back = wide([jnp.where((grid_t <= grid_s) & together, 1.0, 0.0).astype(F32)] * heads)
    head_rows = jnp.where(
        lax.broadcasted_iota(jnp.int32, (8, width), 0) == lax.div(lax.broadcasted_iota(jnp.int32, (8, width), 1), HEAD_DIM),
        1.0,
        0.0,
    ).astype(BF)
    both_chunks = range(2)
    both_blocks = range(CHUNK // BLOCK)

    def joined(block):
        return jnp.where(segment(block) == segment(block - 1), jnp.float32(1.0), jnp.float32(0.0))

    def per_head(value):
        return wide([value * masks[h * CHUNK : (h + 1) * CHUNK, :] for h in range(heads)], 0)

    def halves(value):
        return [value[k * BLOCK : (k + 1) * BLOCK] for k in both_blocks]

    def chunk_rows(pair):
        return [pl.ds(pl.multiple_of((2 * pair + c) * CHUNK, CHUNK), CHUNK) for c in both_chunks]

    state[...] = jnp.zeros_like(state)
    krow[...] = jnp.zeros_like(krow)

    def mix(pair, carry):
        diag = diag_two[0:width, :].astype(F32)
        here = chunk_rows(pair)
        query, key, value = ([fqkv[at, s * width : (s + 1) * width] for at in here] for s in range(3))
        scores = [split(dot(query[c], per_head(key[c]), NT) * causal) for c in both_chunks]
        turned = [key[c].T for c in both_chunks]
        over = [dot(scores[c][0], per_head(value[c])) for c in both_chunks]
        under = [dot(scores[c][0], masks[...]) + dot(scores[c][1], masks[...]) for c in both_chunks]
        made = [
            dot(turned[c][:, k * BLOCK : (k + 1) * BLOCK], halves(value[c])[k]) * diag
            for c in both_chunks
            for k in both_blocks
        ]
        row_made = [jnp.sum(halves(key[c])[k].astype(F32), 0, keepdims=True) for c in both_chunks for k in both_blocks]
        now, row = state[...], krow[0:1, :]
        carried, rows_in = [], []
        for k in range(4):
            carried.append(now.astype(BF))
            rows_in.append(row)
            states[4 * pair + k] = sum(now[h * HEAD_DIM : (h + 1) * HEAD_DIM] for h in range(heads)).astype(BF)
            ksums[4 * pair + k] = jnp.broadcast_to(row, (8, width))
            keep = joined(4 * pair + k + 1)
            now = (now + made[k]) * keep
            row = (row + row_made[k]) * keep
        state[...] = now
        krow[0:1, :] = row
        for c in both_chunks:
            parts = halves(query[c])
            more = wide([dot(parts[k], carried[2 * c + k]) for k in both_blocks], 0)
            high, low = split(wide([parts[k].astype(F32) * rows_in[2 * c + k] for k in both_blocks], 0))
            inverse = 1.0 / (under[c] + dot(wide([high, low]), diag_two[...]))
            attended = (over[c] + more) * inverse
            att[here[c], :] = attended
            rden[here[c], :] = wide([inverse[:, h * HEAD_DIM : h * HEAD_DIM + HEAD_DIM // 2] for h in range(heads)])
            mixed[here[c], :] = attended.astype(BF)

        return carry

    def add_parts(base, first, count, sources):
        for at in range(0, count, SUB):
            total = base[pl.ds(first + at, SUB), :].astype(F32)
            for source, place in sources:
                total = total + source[pl.ds(place + at, SUB), :].astype(F32)
            base[pl.ds(first + at, SUB), :] = total.astype(BF)

    def bring(base, first, box, place, count):
        base[pl.ds(first, count), :] = box[pl.ds(place, count), :]

    half, quarter = UNIT // 2, UNIT // 4

    def rows_of(index, size):
        return pl.multiple_of(index * size, size)

    def unit_of(n):
        return grads.at[pl.ds(pl.multiple_of(n * UNIT, UNIT), UNIT)]

    def hop(n, kind, source, target, device):
        return pltpu.make_async_remote_copy(
            src_ref=source,
            dst_ref=target,
            send_sem=ar_send.at[n, kind],
            recv_sem=ar_recv.at[n, kind],
            device_id={"dp": device},
            device_id_type=MESH,
        )

    plain = units - 3 * width // UNIT

    class Copies:
        def __init__(self, n):
            self.n = n

        def whole(self):
            first = pl.multiple_of(self.n * UNIT, UNIT)
            return pltpu.make_async_copy(unit_of(self.n), grads_out.at[pl.ds(first, UNIT)], grad_sem.at[self.n])

        def piece(self, q):
            u = self.n - plain
            at = 4 * lax.div(u, 2) + q
            row = pl.multiple_of(lax.div(at, 3) * TILE + lax.rem(u, 2) * UNIT, UNIT)
            return pltpu.make_async_copy(
                unit_of(self.n).at[:, q * width : (q + 1) * width],
                qkv_out.at[lax.rem(at, 3), pl.ds(row, UNIT)],
                grad_sem.at[self.n],
            )

        def start(self):
            pl.when(self.n < plain)(lambda: self.whole().start())

            @pl.when(self.n >= plain)
            def _():
                for q in range(4):
                    self.piece(q).start()

        def wait(self):
            pl.when(self.n < plain)(lambda: self.whole().wait())

            @pl.when(self.n >= plain)
            def _():
                for q in range(4):
                    self.piece(q).wait()

    def begin(n):
        place = lax.rem(lax.div(n, 2), SLOTS // 2)
        code = 4 * lax.rem(n, 2) + middle

        @pl.when(code < 4)
        def _():
            theirs = unit_of(n).at[pl.ds(rows_of(1 - along_x, half), half)]
            hop(n, 0, theirs, recv_a.at[place, pl.ds(0, half)], across).start()

        @pl.when(code == 4)
        def _():
            hop(n, 0, unit_of(n), recv_b.at[place, pl.ds(0, UNIT)], inward).start()

    def advance(n, stage):
        kind = jnp.where(n < 0, 2, jnp.where(n >= units, 2, lax.rem(n, 2)))
        code = 4 * kind + middle
        place = lax.rem(lax.div(n, 2), SLOTS // 2)

        def case(number):
            return pl.when(code == number)

        base, box = unit_of(n), recv_a.at[place]
        mine_at, theirs_at = rows_of(along_x, half), rows_of(1 - along_x, half)
        own_at = pl.multiple_of(along_x * half + side * quarter, quarter)
        other_at = pl.multiple_of(along_x * half + (1 - side) * quarter, quarter)
        own_in, other_in = rows_of(side, quarter), rows_of(1 - side, quarter)

        def rows(first, size):
            return base.at[pl.ds(first, size)]

        def x_one():
            return hop(n, 0, rows(theirs_at, half), box.at[pl.ds(0, half)], across)

        def z_one():
            return hop(n, 1, rows(mine_at, half), box.at[pl.ds(half, half)], inward)

        def z_two():
            return hop(n, 2, rows(other_at, quarter), box.at[pl.ds(2 * half, quarter)], inward)

        def z_swap():
            return hop(n, 3, rows(own_at, quarter), box.at[pl.ds(swap_at, quarter)], inward)

        def out(kind, first, place_in):
            return hop(n, kind, rows(first, quarter), box.at[pl.ds(half + place_in, quarter)], outward)

        def x_two():
            return hop(n, 6, rows(mine_at, half), box.at[pl.ds(last_at, half)], across)

        swap_at, last_at = 2 * half + quarter, 3 * half

        if stage == 1:

            @case(0)
            def _():
                x_one().wait_recv()
                add_parts(base, mine_at, half, [(box, 0)])
                z_one().start()

        if stage == 2:

            @case(2)
            def _():
                x_one().wait_recv()
                z_one().wait_recv()
                add_parts(base, other_at, quarter, [(box, other_in), (box, half + other_in)])
                z_two().start()

        if stage == 3:

            @case(2)
            def _():
                z_two().wait_recv()
                add_parts(base, own_at, quarter, [(box, own_in), (box, half + own_in), (box, 2 * half)])
                z_swap().start()
                out(4, own_at, own_in).start()

        if stage == 4:

            @case(2)
            def _():
                z_swap().wait_recv()
                z_two().wait_send()
                bring(base, other_at, box, swap_at, quarter)
                out(5, other_at, other_in).start()
                x_two().start()

        if stage == 5:

            @case(0)
            def _():
                z_one().wait_send()
                out(4, own_at, own_in).wait_recv()
                out(5, other_at, other_in).wait_recv()
                bring(base, mine_at, box, half, half)
                x_two().start()

        if stage == 6:

            @case(2)
            def _():
                z_swap().wait_send()
                out(4, own_at, own_in).wait_send()
                out(5, other_at, other_in).wait_send()

            @pl.when(kind == 0)
            def _():
                x_one().wait_send()
                x_two().wait()
                bring(base, theirs_at, box, last_at, half)

        box_b = recv_b.at[place]
        mine_z, theirs_z = rows_of(side, half), rows_of(1 - side, half)
        own_x = pl.multiple_of(side * half + along_x * quarter, quarter)
        other_x = pl.multiple_of(side * half + (1 - along_x) * quarter, quarter)
        own_part_at, other_part_at = rows_of(along_x, quarter), rows_of(1 - along_x, quarter)

        def z_in():
            return hop(n, 0, base, box_b.at[pl.ds(0, UNIT)], inward)

        def z_mid():
            return hop(n, 1, rows(theirs_z, half), box_b.at[pl.ds(UNIT, half)], inward)

        def x_mid():
            return hop(n, 2, rows(other_x, quarter), box_b.at[pl.ds(UNIT + half, quarter)], across)

        def x_swap():
            return hop(n, 3, rows(own_x, quarter), box_b.at[pl.ds(swap_at, quarter)], across)

        def z_share():
            return hop(n, 4, rows(mine_z, half), box_b.at[pl.ds(last_at, half)], inward)

        def z_out(kind, first):
            return hop(n, kind, rows(first, half), box_b.at[pl.ds(first, half)], outward)

        swap_at, last_at = UNIT + half + quarter, 2 * UNIT

        if stage == 1:

            @case(6)
            def _():
                z_in().wait_recv()
                add_parts(base, theirs_z, half, [(box_b, theirs_z)])
                z_mid().start()

        if stage == 2:

            @case(6)
            def _():
                z_mid().wait_recv()
                add_parts(base, other_x, quarter, [(box_b, other_x), (box_b, UNIT + other_part_at)])
                x_mid().start()

        if stage == 3:

            @case(6)
            def _():
                x_mid().wait_recv()
                add_parts(
                    base, own_x, quarter, [(box_b, own_x), (box_b, UNIT + own_part_at), (box_b, UNIT + half)]
                )
                x_swap().start()

        if stage == 4:

            @case(6)
            def _():
                x_swap().wait_recv()
                x_mid().wait_send()
                bring(base, other_x, box_b, swap_at, quarter)
                z_share().start()
                z_out(5, mine_z).start()

        if stage == 5:

            @case(6)
            def _():
                z_share().wait_recv()
                z_mid().wait_send()
                bring(base, theirs_z, box_b, last_at, half)
                z_out(6, theirs_z).start()

        if stage == 6:

            @case(6)
            def _():
                x_swap().wait_send()
                z_share().wait_send()
                z_out(5, mine_z).wait_send()
                z_out(6, theirs_z).wait_send()

            @case(4)
            def _():
                z_in().wait_send()
                z_out(5, mine_z).wait_recv()
                z_out(6, theirs_z).wait_recv()
                bring(base, 0, box_b, 0, UNIT)

            pl.when(kind < 2)(lambda: Copies(n).start())

    def at_ready(n):
        return jnp.where(n < 2, 1, jnp.where(n < plain, 0, jnp.where(n < plain + 2, 1, 0)))

    def ready(first, count):
        for n in (first + k for k in range(count)):
            if reduce_dp:
                pl.when(at_ready(n) == 1)(functools.partial(begin, n))
            else:
                Copies(n).start()

    def tick(t):
        if reduce_dp:
            with jax.named_scope("dp_tick"):
                move(t)

    def move(t):
        for stage in (6, 5, 4, 3, 2, 1):
            advance(t - 2 * (stage - 1), stage)
        later = t + 2

        @pl.when(jnp.where(later >= units, 1, at_ready(later)) == 0)
        def _():
            begin(later)

    def tick_at(j, every, first):
        @pl.when(lax.rem(j, every) == every - 1)
        def _():
            tick(first + lax.div(j, every))

    ticks = units + 10

    def to_mate(which, number):
        return pltpu.make_async_remote_copy(
            src_ref=rs_out.at[lax.rem(number, 2)],
            dst_ref=rs_in.at[number],
            send_sem=rs_send.at[which, number],
            recv_sem=rs_recv.at[which, number],
            device_id={"tensor": mate},
            device_id_type=MESH,
        )

    def to_peer(which, number):
        return pltpu.make_async_remote_copy(
            src_ref=rs_in.at[number],
            dst_ref=y_in.at[number],
            send_sem=rs_send.at[which, 4 + number],
            recv_sem=rs_recv.at[which, 4 + number],
            device_id={"tensor": peer},
            device_id_type=MESH,
        )

    def scatter(j, which, compute):
        owner = jnp.where(j < 2, cross, jnp.where(j < 4, peer, mate))
        number = lax.rem(j, 2)
        row0 = pl.multiple_of(owner * rows_own + number * TILE, TILE)

        @pl.when(lax.div(j, 2) != 1)
        def _():
            at = jnp.where(j < 2, j, j - 2)
            pl.when(j >= 4)(lambda: to_mate(which, number).wait_send())

            def put(rows_at, part):
                rs_out[number, rows_at, :] = part.astype(BF)

            compute(row0, put)
            to_mate(which, at).start()

        @pl.when(lax.div(j, 2) == 1)
        def _():
            to_mate(which, number).wait_recv()

            def put(rows_at, part):
                rs_in[number, rows_at, :] = (rs_in[number, rows_at, :].astype(F32) + part).astype(BF)

            compute(row0, put)
            to_peer(which, number).start()

    def gathered(which, number):
        to_mate(which, 2 + number).wait_recv()
        to_peer(which, number).wait_recv()

    def settle(which):
        for number in range(2):
            to_mate(which, 2 + number).wait_send()
            to_peer(which, number).wait_send()

    def stored(number, target):
        return pltpu.make_async_copy(rs_out.at[number], target, result_sem.at[number])

    keep_tok.wait()
    for piece in range(g_tok.pieces):
        g_tok.forward(peer, piece).wait_send()

    def keep_unit(n, value):
        grads[pl.ds(pl.multiple_of(n * UNIT, UNIT), value.shape[0]), :] = value
        ready(n, value.shape[0] // UNIT)

    per_tile = TILE // UNIT
    first_out = hid.shape[1] // UNIT
    first_up = first_out + width // UNIT

    def arrive(piece):
        g_cot.to_peer(peer, piece).wait_recv()
        g_cot.forward(peer, piece).start()

    def down(piece):
        g_cot.forward(cross, piece).wait_recv()
        tile = dot(cot[:, piece * TILE : (piece + 1) * TILE], hid[...], TN)
        keep_unit(per_tile * piece, tile.astype(BF))

    def mix_some(first, last):
        with jax.named_scope("mixer"):
            lax.fori_loop(first, last, mix, 0)

    pairs = chunks // 2
    with jax.named_scope("grad_down"):
        arrive(0)
        arrive(1)
        down(0)
        down(1)
    tick(jnp.int32(0))
    mix_some(0, pairs // 4)
    arrive(2)
    mix_some(pairs // 4, pairs // 2)
    with jax.named_scope("grad_down"):
        down(2)

    def pause(t, carry):
        tick(t)
        return carry

    lax.fori_loop(1, 3, pause, 0)
    mix_some(pairs // 2, 3 * pairs // 4)
    arrive(3)
    mix_some(3 * pairs // 4, pairs)
    with jax.named_scope("grad_down"):
        down(3)
    tick(jnp.int32(3))
    keep_unit(first_out, dot(mixed[...], cot[...], TN).astype(BF))
    tick(jnp.int32(4))

    def branch(row0, put):
        here = pl.ds(row0, TILE)
        put(pl.ds(0, TILE), dot(mixed[here, :], w_out[...]) + dot(hid[here, :], w_down[...]))

    def keep_temp(rows_at, part):
        temp[0, rows_at, :] = part

    def own_copy(number, back=False):
        held = own_part.at[pl.ds(pl.multiple_of(number * TILE, TILE), TILE)]
        return pltpu.make_async_copy(*((held, temp.at[0]) if back else (temp.at[0], held)), temp_sem.at[0])

    def produce(j, carry):
        @pl.when(j >= 2)
        def _():
            scatter(j - 2, 0, branch)

        @pl.when(j < 2)
        def _():
            branch(pl.multiple_of(me * rows_own + j * TILE, TILE), keep_temp)
            own_copy(j).start()
            own_copy(j).wait()

        pl.when(j == 1)(lambda: slope_copy(0, True).start())
        pl.when(j == 2)(lambda: slope_copy(1, True).start())
        tick_at(j, 4, 5)
        return carry

    with jax.named_scope("outputs"):
        lax.fori_loop(0, 8, produce, 0)
    bring_up = pltpu.make_async_copy(
        grads.at[pl.ds(rows, 2 * rows_own)], hid.at[pl.ds(chip_row, 2 * rows_own)], tok_sem.at[0]
    )
    bring_up.start()

    def descend(p, carry):
        here = [pl.ds(pl.multiple_of(owner * rows_own + p * UNIT, UNIT), UNIT) for owner in (peer, cross)]
        parity = lax.rem(p, 2)
        slope_copy(p, True).wait()
        turned = wide([cot[at, :] for at in here], 0)
        for at in range(0, hid.shape[1], TILE):
            d_hidden = dot(turned, w_down[at : at + TILE, :], NT)
            d_up = (d_hidden * temp[parity, :, at : at + TILE]).astype(BF)
            for k, rows_at in enumerate(here):
                hid[rows_at, at : at + TILE] = d_up[k * UNIT : (k + 1) * UNIT]
        pl.when(p < 2)(lambda: slope_copy(p + 2, True).start())
        tick_at(p, 4, 7)
        return carry

    with jax.named_scope("grad_gelu"):
        lax.fori_loop(0, 4, descend, 0)
    bring_up.wait()

    def upward(j, carry):
        at = pl.ds(pl.multiple_of(j * TILE, TILE), TILE)
        keep_unit(first_up + per_tile * j, dot(n_two[:, at], hid[...], TN).astype(BF))
        tick_at(j, 2, 8)
        return carry

    with jax.named_scope("grad_up"):
        lax.fori_loop(0, n_two.shape[1] // TILE, upward, 0)

    state[...] = jnp.zeros_like(state)
    krow[...] = jnp.zeros_like(krow)
    feat_sums[...] = jnp.zeros_like(feat_sums)

    def unmix(step, carry):
        pair = chunks // 2 - 1 - step
        diag = diag_two[0:width, :].astype(F32)
        row_pair = pl.multiple_of(pair * 2 * CHUNK, 2 * CHUNK)
        d_mixed = dot(cot[pl.ds(row_pair, 2 * CHUNK), :], w_out[...], NT)
        here = chunk_rows(pair)
        query, key, value = ([fqkv[at, s * width : (s + 1) * width] for at in here] for s in range(3))
        d_over, under_parts = [], []
        for c in both_chunks:
            packed = rden[here[c], :]
            inverse = wide(
                [packed[:, h // 2 * HEAD_DIM // 2 : (h // 2 + 1) * HEAD_DIM // 2] for h in range(2 * heads)]
            )
            d_over.append(d_mixed[c * CHUNK : (c + 1) * CHUNK] * inverse)
            under_parts.append(wide(split(d_over[c] * att[here[c], :])))
        d_under = [-dot(under_parts[c], diag_two[...]) for c in both_chunks]
        under_row = [-dot(wide([head_rows, head_rows]), under_parts[c], NT) for c in both_chunks]
        over_split = [split(d_over[c]) for c in both_chunks]
        over_both = [wide(over_split[c]) for c in both_chunks]
        over_heads = [wide([per_head(part) for part in over_split[c]]) for c in both_chunks]
        query_heads, key_heads, value_heads = ([per_head(field[c]) for c in both_chunks] for field in (query, key, value))
        scores_back = [(dot(key[c], query_heads[c], NT) * causal_back).astype(BF) for c in both_chunks]
        d_scores = [dot(over_both[c], wide([value_heads[c]] * 2), NT) for c in both_chunks]
        d_back = [dot(wide([value[c]] * 2), over_heads[c], NT) for c in both_chunks]
        turned = [query[c].T for c in both_chunks]
        made = []
        for c in both_chunks:
            for k in both_blocks:
                left = turned[c][:, k * BLOCK : (k + 1) * BLOCK]
                made.append(dot(wide([left, left]), wide([halves(part)[k] for part in over_split[c]], 0)) * diag)
        d_scores = [
            wide(
                split(
                    (
                        d_scores[c]
                        + wide(
                            [
                                jnp.broadcast_to(d_under[c][:, h * HEAD_DIM : h * HEAD_DIM + 1], (CHUNK, CHUNK))
                                for h in range(heads)
                            ]
                        )
                    )
                    * causal
                )
            )
            for c in both_chunks
        ]
        d_back = [
            wide(split((d_back[c] + wide([under_row[c][h : h + 1, :] for h in range(heads)])) * causal_back))
            for c in both_chunks
        ]
        d_query = [dot(d_scores[c], wide([key_heads[c]] * 2, 0)) for c in both_chunks]
        d_key = [dot(d_back[c], wide([query_heads[c]] * 2, 0)) for c in both_chunks]
        d_value = [dot(scores_back[c], over_heads[c]) for c in both_chunks]
        later, later_row = state[...], krow[0:1, :]
        more = {}
        for at in reversed(range(4)):
            c, k = divmod(at, 2)
            block = 4 * pair + at
            query_k, key_k, value_k, both_k, under_k = (
                halves(field[c])[k] for field in (query, key, value, over_both, d_under)
            )
            carried = wide([states[block]] * heads, 0) * diag_two[0:width, :]
            keep = joined(block + 1)
            later, later_row = later * keep, later_row * keep
            high, low = split(later)
            more[at] = (
                dot(both_k, wide([carried, carried]), NT) + under_k * ksums[block][0:1, :],
                dot(wide([value_k, value_k]), wide([high, low]), NT) + later_row,
                dot(wide([key_k, key_k]), wide([high, low], 0)),
            )
            later = later + made[at]
            later_row = later_row + jnp.sum(query_k.astype(F32) * under_k, 0, keepdims=True)
        state[...] = later
        krow[0:1, :] = later_row
        turn = rotation(row_pair, 2 * CHUNK // BLOCK)
        here = pl.ds(row_pair, 2 * CHUNK)
        for s, found in enumerate((d_query, d_key)):
            grad = wide(found, 0) + wide([more[at][s] for at in range(4)], 0)
            spectrum = spec[s, here, :]
            grad = grad * (weight_row * jnp.exp(scale_row * spectrum))
            feat_sums[0:1, :] += jnp.sum(grad * spectrum, 0, keepdims=True)
            feat_sums[1:2, :] += jnp.sum(grad, 0, keepdims=True)
            high, low = split(grad * scale_row)
            back = dot(high, dct[:, 0:width]) + dot(low, dct[:, 0:width]) + dot(high, dct[:, 2 * width :])
            fqkv[here, s * width : (s + 1) * width] = rotate(back, turn, True).astype(BF)
        d_value = wide([d_value[c][:, :width] + d_value[c][:, width:] for c in both_chunks], 0)
        fqkv[here, 2 * width : 3 * width] = (d_value + wide([more[at][2] for at in range(4)], 0)).astype(BF)
        tick(10 + step)

        return carry

    with jax.named_scope("mixer_back"):
        lax.fori_loop(0, chunks // 2, unmix, 0)

    for j in range(n_one.shape[1] // TILE):
        tile = dot(n_one[:, j * TILE : (j + 1) * TILE], fqkv[...], TN).astype(BF)
        for s in range(3):
            at = 3 * j + s
            first = plain * UNIT + at // 4 * TILE
            grads[first : first + TILE, at % 4 * width : (at % 4 + 1) * width] = tile[:, s * width : (s + 1) * width]
        if j:
            ready(plain + (j - 1) * per_tile, per_tile)


    tick(jnp.int32(18))

    sums[...] = jnp.zeros_like(sums)

    def tok_copy(row0):
        return pltpu.make_async_copy(tok_kept.at[pl.ds(row0, TILE)], tok_tile, tok_sem.at[0])

    def row_grads(row0, put):
        here = pl.ds(row0, TILE)
        tok_copy(row0).start()
        total = dot(fqkv[here, 0:width], w_qkv[0], NT)
        for s in (1, 2):
            total = total + dot(fqkv[here, s * width : (s + 1) * width], w_qkv[s], NT)
        temp[0] = total
        temp[1] = dot(hid[here, :], w_up[...], NT)
        tok_copy(row0).wait()

        def fold(i, inner):
            at = pl.ds(pl.multiple_of(i * SUB, SUB), SUB)
            unit, _ = centered(tok_tile, pl.multiple_of(i * SUB, SUB), SUB)
            one, two = temp[0, at, :], temp[1, at, :]
            for number, term in enumerate((one * unit, one, two * unit, two)):
                sums[number] += jnp.sum(term.reshape(SUB // 8, 8, term.shape[1]), 0)
            put(at, one * gain_one + two * gain_two)
            return inner

        lax.fori_loop(0, TILE // SUB, fold, 0)

    def finish(number, carry):
        row0 = pl.multiple_of(me * rows_own + number * TILE, TILE)
        own_copy(number, True).start()
        tok_copy(row0).start()
        own_copy(number, True).wait()
        tok_copy(row0).wait()
        gathered(0, number)

        def step(i, inner):
            at = pl.ds(pl.multiple_of(i * SUB, SUB), SUB)
            total = temp[0, at, :] + rs_in[2 + number, at, :].astype(F32) + y_in[number, at, :].astype(F32)
            total = total + tok_tile[at, :].astype(F32)
            rs_out[number, at, :] = total.astype(BF)
            return inner

        lax.fori_loop(0, TILE // SUB, step, 0)
        stored(number, mixed_out.at[pl.ds(pl.multiple_of(number * TILE, TILE), TILE)]).start()
        return carry

    with jax.named_scope("finish"):
        settle(0)
        lax.fori_loop(0, 2, finish, 0)
    pl.semaphore_signal(free_mate, inc=1, device_id={"tensor": mate}, device_id_type=MESH)
    pl.semaphore_signal(free_peer, inc=1, device_id={"tensor": peer}, device_id_type=MESH)
    for number in range(2):
        stored(number, mixed_out.at[pl.ds(0, TILE)]).wait()
    pl.semaphore_wait(free_mate, 1)
    pl.semaphore_wait(free_peer, 1)

    def inputs(j, carry):
        @pl.when(j < 6)
        def _():
            scatter(j, 1, row_grads)

        @pl.when(j >= 6)
        def _():
            row_grads(pl.multiple_of(me * rows_own + (j - 6) * TILE, TILE), keep_temp)
            own_copy(j - 6).start()
            own_copy(j - 6).wait()

        tick(19 + j)
        return carry

    with jax.named_scope("row_grads"):
        lax.fori_loop(0, 8, inputs, 0)

    def conclude(number):
        row0 = pl.multiple_of(me * rows_own + number * TILE, TILE)
        own_copy(number, True).start()
        tok_copy(row0).start()
        gathered(1, number)
        own_copy(number, True).wait()
        tok_copy(row0).wait()

        def step(i, inner):
            at = pl.ds(pl.multiple_of(i * SUB, SUB), SUB)
            group_at = pl.multiple_of(row0 + i * SUB, SUB)
            unit, deviation = centered(tok_tile, pl.multiple_of(i * SUB, SUB), SUB)
            total = temp[0, at, :] + rs_in[2 + number, at, :].astype(F32) + y_in[number, at, :].astype(F32)
            along = jnp.mean(total * unit, -1, keepdims=True)
            total = total - jnp.mean(total, -1, keepdims=True) - unit * along
            total = cot[pl.ds(group_at, SUB), :].astype(F32) + deviation * total
            rs_out[number, at, :] = total.astype(BF)
            return inner

        lax.fori_loop(0, TILE // SUB, step, 0)
        stored(number, input_grad.at[pl.ds(number * TILE, TILE)]).start()

    small[...] = jnp.zeros_like(small)
    for number in range(4):
        small[number : number + 1, :] = jnp.sum(sums[number], 0, keepdims=True)
    small[4:5, 0:width] = feat_sums[0:1, :]
    small[5:6, 0:width] = feat_sums[1:2, :] / weight_row

    def small_hops(axis, own, count, boxes, first):
        hops = []
        for step in range(1, count):
            hops.append(
                pltpu.make_async_remote_copy(
                    src_ref=small,
                    dst_ref=boxes.at[own],
                    send_sem=small_send.at[first + step - 1],
                    recv_sem=small_recv.at[first + step - 1],
                    device_id={axis: lax.rem(own + step, count)},
                    device_id_type=MESH,
                )
            )
        return hops

    over_tensor = small_hops("tensor", me, 4, small_in, 0)
    over_dp = small_hops("dp", group, members, small_wide, 3)

    def small_step(k):
        if k == 0:
            for copy in over_tensor:
                copy.start()
            small_in[me] = small[...]
        if k == 1:
            for copy in over_tensor:
                copy.wait()
            total = small_in[0]
            for member in range(1, 4):
                total = total + small_in[member]
            small[0:4, :] = total[0:4, :]
        if k == 1 and reduce_dp:
            for copy in over_dp:
                copy.start()
            small_wide[group] = small[...]
        if k == 2 and reduce_dp:
            for copy in over_dp:
                copy.wait()
            total = small_wide[0]
            for member in range(1, members):
                total = total + small_wide[member]
            small[...] = total

    settle_at, late = 28, {27: 0, 29: 1, 32: 2}
    if reduce_dp:

        def rest(t, carry):
            for at, k in late.items():
                pl.when(t == at)(functools.partial(small_step, k))
            for number in range(2):

                @pl.when(t == settle_at + 2 * number)
                def _():
                    if number == 0:
                        settle(1)
                    conclude(number)

            tick(t)
            return carry

        lax.fori_loop(27, ticks, rest, 0)
    else:
        for k in range(2):
            small_step(k)
        settle(1)
        for number in range(2):
            conclude(number)
    for h in range(heads):
        at = slice(h * HEAD_DIM, (h + 1) * HEAD_DIM)
        feat_out[0, h : h + 1, :] = small[4:5, at]
        feat_out[1, h : h + 1, :] = small[5:6, at]

    def copied(n, carry):
        Copies(n).wait()
        return carry

    lax.fori_loop(0, units, copied, 0)
    for number in range(2):
        stored(number, input_grad.at[pl.ds(0, TILE)]).wait()

    for gather in (g_tok, g_cot):
        gather.to_mate(me).wait_send()
        for piece in range(gather.pieces):
            gather.to_peer(me, piece).wait_send()
    for piece in range(g_cot.pieces):
        g_cot.forward(peer, piece).wait_send()


def widen(down_in, out_in, up_in, qkv_in, *outs):
    down, out, up, qkv = outs
    down[...] = down_in[...].astype(F32).T
    out[...] = out_in[...].astype(F32)
    up[...] = up_in[...].astype(F32)
    qkv[...] = qkv_in[...].astype(F32)


def shards(
    reduce_dp,
    tokens,
    ln1_gain,
    ln1_bias,
    ln2_gain,
    ln2_bias,
    w_qkv,
    w_out,
    w_up,
    w_down,
    feature_scale,
    feature_weight,
    lengths,
    cotangent,
):
    rows_own, model = tokens.shape
    rows = 4 * rows_own
    heads = feature_scale.shape[0]
    width = heads * HEAD_DIM
    hidden = w_up.shape[1]
    consts = tables(rows // BLOCK, heads)
    norms = [value.reshape(1, model) for value in (ln1_gain, ln1_bias, ln2_gain, ln2_bias)]
    anywhere = pl.BlockSpec(memory_space=pl.ANY)
    vmem = pl.BlockSpec(memory_space=pltpu.VMEM)
    smem = pl.BlockSpec(memory_space=pltpu.SMEM)
    shape = jax.ShapeDtypeStruct
    plain = 2 * hidden + width
    units = (plain + 3 * width) // UNIT
    mixed_out, input_grad, grads, g_qkv, _, _, _, small, feats = pl.pallas_call(
        functools.partial(kernel, reduce_dp),
        out_shape=(
            shape((rows_own, model), BF),
            shape((rows_own, model), BF),
            shape((plain, model), BF),
            shape((3, model, width), BF),
            shape((rows // 2, hidden), F32),
            shape((rows_own, model), F32),
            shape((rows, model), BF),
            shape((8, model), F32),
            shape((2, heads, HEAD_DIM), F32),
        ),
        in_specs=[smem, anywhere, anywhere] + [vmem] * 4 + [anywhere] * 4 + [vmem] * 6,
        out_specs=(anywhere,) * 7 + (vmem, vmem),
        scratch_shapes=[
            pltpu.VMEM((TILE, model), BF),
            pltpu.VMEM((rows, model), BF),
            pltpu.VMEM((rows, model), BF),
            pltpu.VMEM((rows, model), BF),
            pltpu.VMEM((rows, hidden), BF),
            pltpu.VMEM((rows, 3 * width), BF),
            pltpu.VMEM((2, rows, width), F32),
            pltpu.VMEM((rows, width), BF),
            pltpu.VMEM((rows, width), F32),
            pltpu.VMEM((rows, width // 2), F32),
            pltpu.VMEM((rows // BLOCK, HEAD_DIM, width), BF),
            pltpu.VMEM((rows // BLOCK, 8, width), F32),
            pltpu.VMEM((width, width), F32),
            pltpu.VMEM((8, width), F32),
            pltpu.VMEM((units * UNIT, model), BF),
            pltpu.VMEM((SLOTS // 2, 2 * UNIT, model), BF),
            pltpu.VMEM((SLOTS // 2, 5 * UNIT // 2, model), BF),
            pltpu.VMEM((2, TILE, model), BF),
            pltpu.VMEM((4, TILE, model), BF),
            pltpu.VMEM((2, TILE, model), BF),
            pltpu.VMEM((2, TILE, model), F32),
            pltpu.VMEM((4, 8, model), F32),
            pltpu.VMEM((8, width), F32),
            pltpu.VMEM((4, 8, model), F32),
            pltpu.VMEM((8, 8, model), F32),
            pltpu.VMEM(w_qkv.shape, BF),
            pltpu.VMEM(w_out.shape, BF),
            pltpu.VMEM(w_up.shape, BF),
            pltpu.VMEM(w_down.shape, BF),
            pltpu.SemaphoreType.DMA((2 + 2 * rows_own // UNIT,)),
            pltpu.SemaphoreType.DMA((2 + 2 * rows_own // UNIT + 2 * model // TILE,)),
            pltpu.SemaphoreType.DMA((2 + 2 * rows_own // UNIT + 2 * model // TILE,)),
            pltpu.SemaphoreType.DMA((4,)),
            pltpu.SemaphoreType.DMA((units, 7)),
            pltpu.SemaphoreType.DMA((units, 7)),
            pltpu.SemaphoreType.DMA((2, 6)),
            pltpu.SemaphoreType.DMA((2, 6)),
            pltpu.SemaphoreType.DMA((10,)),
            pltpu.SemaphoreType.DMA((10,)),
            pltpu.SemaphoreType.DMA((units,)),
            pltpu.SemaphoreType.DMA((2,)),
            pltpu.SemaphoreType.DMA((1,)),
            pltpu.SemaphoreType.DMA((2,)),
            pltpu.SemaphoreType.REGULAR,
            pltpu.SemaphoreType.REGULAR,
        ],
        compiler_params=pltpu.CompilerParams(
            collective_id=0, has_side_effects=True, vmem_limit_bytes=62 * 2**20
        ),
    )(lengths, tokens, cotangent, *norms, w_qkv, w_out, w_up, w_down, feature_scale, feature_weight, *consts)
    norm_sums = small[0:4]
    if not reduce_dp:
        grads, g_qkv, norm_sums, feats = lax.psum(
            (*lax.optimization_barrier((grads.astype(F32), g_qkv.astype(F32))), norm_sums, feats), "dp"
        )
    steps = 8
    down_cut, out_cut, up_cut, row_cut = hidden // steps, width // steps, model // steps, model // steps
    g_down, g_out, g_up, g_qkv = pl.pallas_call(
        widen,
        grid=(steps,),
        out_shape=(
            shape((hidden, model), F32),
            shape((width, model), F32),
            shape((model, hidden), F32),
            shape((3, model, width), F32),
        ),
        in_specs=[
            pl.BlockSpec((model, down_cut), lambda i: (0, i)),
            pl.BlockSpec((out_cut, model), lambda i: (hidden // out_cut + i, 0)),
            pl.BlockSpec((up_cut, hidden), lambda i: ((hidden + width) // up_cut + i, 0)),
            pl.BlockSpec((3, row_cut, width), lambda i: (0, i, 0)),
        ],
        out_specs=(
            pl.BlockSpec((down_cut, model), lambda i: (i, 0)),
            pl.BlockSpec((out_cut, model), lambda i: (i, 0)),
            pl.BlockSpec((up_cut, hidden), lambda i: (i, 0)),
            pl.BlockSpec((3, row_cut, width), lambda i: (0, i, 0)),
        ),
        compiler_params=pltpu.CompilerParams(vmem_limit_bytes=24 * 2**20),
    )(grads, grads, grads, g_qkv)
    return (
        mixed_out,
        input_grad,
        norm_sums[0],
        norm_sums[1],
        norm_sums[2],
        norm_sums[3],
        g_qkv,
        g_out,
        g_up,
        g_down,
        feats[0],
        feats[1],
    )


def solution(mesh):
    placed = (
        P(("dp", "tensor"), None),
        P(),
        P(),
        P(),
        P(),
        P(None, None, "tensor"),
        P("tensor", None),
        P(None, "tensor"),
        P("tensor", None),
        P("tensor", None),
        P("tensor", None),
        P("dp", None),
        P(("dp", "tensor"), None),
    )
    return jax.shard_map(
        functools.partial(shards, mesh.shape["dp"] == 8),
        mesh=mesh,
        in_specs=placed,
        out_specs=(
            P(("dp", "tensor"), None),
            P(("dp", "tensor"), None),
            P(),
            P(),
            P(),
            P(),
            P(None, None, "tensor"),
            P("tensor", None),
            P(None, "tensor"),
            P("tensor", None),
            P("tensor", None),
            P("tensor", None),
        ),
        check_vma=False,
    )
```

time: 250 us -> 217 us (0.87)
  Pallas kernels: 234 us -> 207 us
  other arithmetic: 11 us -> 0 us
  local copies, waits for them, and re-layouts: 4.06 us -> 8.47 us
    pallas_call x1, Pallas kernels: 234 us -> 202 us  [shards(): pl.pallas_call(functools.partial(kernel, reduce_dp), out_shape=(shape((ro...]
    convert_element_type x3 -> x0, other arithmetic: 11 us -> none  [the longest x2 9.06 us: shards(): grads[first:last].astype(F32)]
    pallas_call x0 -> x1, Pallas kernels: none -> 5.77 us  [shards(): pl.pallas_call(widen, grid=(steps,), out_shape=(shape((hidden, model), F3...]
    unnamed x10, local copies, waits for them, and re-layouts: 1.95 us -> 5.69 us
where the time goes in v3:
time: 217 us
  Pallas kernels  207 us (95%)
  local copies, waits for them, and re-layouts  8.47 us (4%)
    pallas_call x1, Pallas kernels, shards(): pl.pallas_call(functools.partial(kernel, reduce_dp), out_shape=(shape((ro...  202 us
    pallas_call x1, Pallas kernels, shards(): pl.pallas_call(widen, grid=(steps,), out_shape=(shape((hidden, model), F3...  5.77 us
    unnamed x10, local copies, waits for them, and re-layouts  5.69 us

profile of v3, /device:TPU:0, one launch (start us, length us, event | category | flops | bytes accessed | tf_op | source)
XLA Modules:
  0.0 216.5 jit_solution(10464333777058392319)
XLA Ops:
  0.6 201.6 %shard_map.256 = (bf16[512,1024]{1,0:T(8,128)(2,1)}, bf16[512,1024]{1,0:T(8,128)(2,1)}, bf16[2304,1024]{1,0:T(8,128)(2,1)}, bf16[3,1024,256]{2,1,0:T(8,128)(2,1)...) custom-call(s32[1,3]{1,0:T(1,128)} %lengths.1, ...), custom_call_target="tpu_custom_call" | custom-call | tf_op jit(solution)/shard_map/pallas_call | solution.py:1249
  202.3 1.3 slice_bitcast_fusion
  203.6 1.5 fusion
  205.1 0.0 copy-start
  205.1 2.3 %copy-done = bf16[2304,1024]{1,0:T(8,128)(2,1)S(1)} copy-done((bf16[2304,1024]{1,0:T(8,128)(2,1)S(1)}, bf16[2304,1024]{1,0:T(8,128)(2,1)}, u32[]{:S(2)}) %copy-start) | copy-done | bytes 4718616
  207.4 0.0 copy-start.1
  207.4 1.4 copy-done.1
  208.8 0.0 copy-start.3
  208.8 0.0 copy-start.2
  208.8 5.8 %shard_map.257 = (f32[1024,1024]{1,0:T(8,128)}, f32[256,1024]{1,0:T(8,128)}, f32[1024,1024]{1,0:T(8,128)}, f32[3,1024,256]{2,1,0:T(8,128)}) custom-call(bf16[2304,1024]{1,0:T(8,128)(2,1)S(1)} %copy-done, bf16[2304,1024]{1,0:T(8,128)(2,1)S(1)} %copy-done, bf16[2304,1024]{1,0:T(8,128)(2,1)S(1)} %copy-done, bf16[3,1024,256]{2,1,0:T(8,128)(2,1)S(1)} %copy-done.1), custom_call_target="tpu_custom_call" | custom-call | tf_op jit(solution)/shard_map/pallas_call | solution.py:1322
  214.6 0.0 copy-done.3
  214.6 1.0 copy.31
  215.6 0.0 copy-done.2
  215.6 1.0 copy.32
Async XLA Ops:
  205.1 2.3 %copy-start = (bf16[2304,1024]{1,0:T(8,128)(2,1)S(1)}, bf16[2304,1024]{1,0:T(8,128)(2,1)}, u32[]{:S(2)}) copy-start(bf16[2304,1024]{1,0:T(8,128)(2,1)} %get-tuple-element.25.down_in.out_in.up_in) | copy-start | bytes 14155780
  207.4 1.4 copy-start.1
  208.8 5.8 %copy-start.3 = (bf16[512,1024]{1,0:T(8,128)(2,1)S(1)}, bf16[512,1024]{1,0:T(8,128)(2,1)}, u32[]{:S(2)}) copy-start(bf16[512,1024]{1,0:T(8,128)(2,1)} %get-tuple-element.50) | copy-start | bytes 3145732
  208.8 6.7 %copy-start.2 = (bf16[512,1024]{1,0:T(8,128)(2,1)S(1)}, bf16[512,1024]{1,0:T(8,128)(2,1)}, u32[]{:S(2)}) copy-start(bf16[512,1024]{1,0:T(8,128)(2,1)} %get-tuple-element.51) | copy-start | bytes 3145732

commit v4 on v3

--- a/solution.py
+++ b/solution.py
@@ -17,7 +17,9 @@
 TILE = 256
 UNIT = 128
 SUB = 32
-SLOTS = 12
+BOXES_X = 9
+BOXES_Z = 6
+LATE = 18
 MESH = pl.DeviceIdType.MESH
 F32 = jnp.float32
 BF = jnp.bfloat16
@@ -93,7 +95,6 @@
     tok_kept,
     small,
     feat_out,
-    tok_tile,
     cot,
     n_one,
     n_two,
@@ -273,8 +274,7 @@
             parts.append(part * cosine - (ahead + behind) if back else part * cosine + (ahead + behind))
         return wide(parts)
 
-    def centered(source, at, size):
-        value = source[pl.ds(at, size), :].astype(F32)
+    def unit_rows(value):
         value = value - jnp.mean(value, -1, keepdims=True)
         deviation = lax.rsqrt(jnp.mean(value * value, -1, keepdims=True) + 1e-05)
         return value * deviation, deviation
@@ -313,16 +313,14 @@
         row_b = pl.multiple_of(jnp.where(late == 0, early_at + UNIT, cross * rows_own + (j - 4) * UNIT), UNIT)
         here = [pl.ds(row_a, UNIT), pl.ds(row_b, UNIT)]
 
-        def norm(i, inner):
-            for row0 in (row_a, row_b):
-                at = pl.multiple_of(row0 + i * SUB, SUB)
-                unit, _ = centered(tok, at, SUB)
-                n_one[pl.ds(at, SUB), :] = (unit * gain_one + bias_one).astype(BF)
-                n_two[pl.ds(at, SUB), :] = (unit * gain_two + bias_two).astype(BF)
-            return inner
-
-        lax.fori_loop(0, UNIT // SUB, norm, 0)
-        first = wide([n_one[at, :] for at in here], 0)
+        for at in here:
+            pltpu.make_async_copy(tok.at[at], tok_kept.at[at], tok_sem.at[0]).start()
+        unit, _ = unit_rows(wide([tok[at, :] for at in here], 0).astype(F32))
+        first = (unit * gain_one + bias_one).astype(BF)
+        second = (unit * gain_two + bias_two).astype(BF)
+        for k, at in enumerate(here):
+            n_one[at, :] = first[k * UNIT : (k + 1) * UNIT]
+            n_two[at, :] = second[k * UNIT : (k + 1) * UNIT]
         turn = [wide(pair, 0) for pair in zip(*(rotation(at, UNIT // BLOCK) for at in (row_a, row_b)))]
 
         def keep(write, value):
@@ -345,7 +343,6 @@
             keep(keep_spectrum, spectrum)
             keep_field(s, weight_row * jnp.exp(scale_row * spectrum))
         keep_field(2, dot(first, w_qkv[2]))
-        second = wide([n_two[at, :] for at in here], 0)
         parity = lax.rem(j, 2)
         pl.when(j >= 6)(lambda: slope_copy(j - 6).wait())
         for at in range(0, w_up.shape[1], TILE):
@@ -377,8 +374,6 @@
         lax.fori_loop(0, rows // TILE, project, 0)
     for p in (2, 3):
         slope_copy(p).wait()
-    keep_tok = pltpu.make_async_copy(tok.at[pl.ds(0, rows)], tok_kept, tok_sem.at[0])
-    keep_tok.start()
 
     grid_t = lax.broadcasted_iota(jnp.int32, (CHUNK, CHUNK), 0)
     grid_s = lax.broadcasted_iota(jnp.int32, (CHUNK, CHUNK), 1)
@@ -428,7 +423,7 @@
             carried.append(now.astype(BF))
             rows_in.append(row)
             states[4 * pair + k] = sum(now[h * HEAD_DIM : (h + 1) * HEAD_DIM] for h in range(heads)).astype(BF)
-            ksums[4 * pair + k] = jnp.broadcast_to(row, (8, width))
+            ksums[pl.ds(4 * pair + k, 1), :] = row
             keep = joined(4 * pair + k + 1)
             now = (now + made[k]) * keep
             row = (row + row_made[k]) * keep
@@ -510,9 +505,16 @@
                 for q in range(4):
                     self.piece(q).wait()
 
+    def kind_of(n):
+        return jnp.where(n < LATE, lax.rem(n, 2), 0)
+
+    def box_of(n):
+        first = jnp.where(n < LATE, lax.div(n, 2), n - LATE // 2)
+        return lax.rem(first, BOXES_X), lax.rem(lax.div(n, 2), BOXES_Z)
+
     def begin(n):
-        place = lax.rem(lax.div(n, 2), SLOTS // 2)
-        code = 4 * lax.rem(n, 2) + middle
+        place, place_b = box_of(n)
+        code = 4 * kind_of(n) + middle
 
         @pl.when(code < 4)
         def _():
@@ -521,12 +523,12 @@
 
         @pl.when(code == 4)
         def _():
-            hop(n, 0, unit_of(n), recv_b.at[place, pl.ds(0, UNIT)], inward).start()
+            hop(n, 0, unit_of(n), recv_b.at[place_b, pl.ds(0, UNIT)], inward).start()
 
     def advance(n, stage):
-        kind = jnp.where(n < 0, 2, jnp.where(n >= units, 2, lax.rem(n, 2)))
+        kind = jnp.where(n < 0, 2, jnp.where(n >= units, 2, kind_of(n)))
         code = 4 * kind + middle
-        place = lax.rem(lax.div(n, 2), SLOTS // 2)
+        place, place_b = box_of(n)
 
         def case(number):
             return pl.when(code == number)
@@ -620,7 +622,7 @@
                 x_two().wait()
                 bring(base, theirs_at, box, last_at, half)
 
-        box_b = recv_b.at[place]
+        box_b = recv_b.at[place_b]
         mine_z, theirs_z = rows_of(side, half), rows_of(1 - side, half)
         own_x = pl.multiple_of(side * half + along_x * quarter, quarter)
         other_x = pl.multiple_of(side * half + (1 - along_x) * quarter, quarter)
@@ -770,8 +772,8 @@
             at = jnp.where(j < 2, j, j - 2)
             pl.when(j >= 4)(lambda: to_mate(which, number).wait_send())
 
-            def put(rows_at, part):
-                rs_out[number, rows_at, :] = part.astype(BF)
+            def put(columns, part):
+                rs_out[number, :, columns] = part.astype(BF)
 
             compute(row0, put)
             to_mate(which, at).start()
@@ -780,8 +782,8 @@
         def _():
             to_mate(which, number).wait_recv()
 
-            def put(rows_at, part):
-                rs_in[number, rows_at, :] = (rs_in[number, rows_at, :].astype(F32) + part).astype(BF)
+            def put(columns, part):
+                rs_in[number, :, columns] = (rs_in[number, :, columns].astype(F32) + part).astype(BF)
 
             compute(row0, put)
             to_peer(which, number).start()
@@ -798,7 +800,7 @@
     def stored(number, target):
         return pltpu.make_async_copy(rs_out.at[number], target, result_sem.at[number])
 
-    keep_tok.wait()
+    pltpu.make_async_copy(tok.at[pl.ds(0, rows)], tok_kept, tok_sem.at[0]).wait()
     for piece in range(g_tok.pieces):
         g_tok.forward(peer, piece).wait_send()
 
@@ -829,8 +831,8 @@
         arrive(1)
         down(0)
         down(1)
+    mix_some(0, pairs // 4)
     tick(jnp.int32(0))
-    mix_some(0, pairs // 4)
     arrive(2)
     mix_some(pairs // 4, pairs // 2)
     with jax.named_scope("grad_down"):
@@ -842,24 +844,34 @@
 
     lax.fori_loop(1, 3, pause, 0)
     mix_some(pairs // 2, 3 * pairs // 4)
+    tick(jnp.int32(3))
     arrive(3)
     mix_some(3 * pairs // 4, pairs)
     with jax.named_scope("grad_down"):
         down(3)
-    tick(jnp.int32(3))
+    tick(jnp.int32(4))
     keep_unit(first_out, dot(mixed[...], cot[...], TN).astype(BF))
-    tick(jnp.int32(4))
+    tick(jnp.int32(5))
+
+    column_tiles = [slice(at, at + TILE) for at in range(0, cot.shape[1], TILE)]
 
     def branch(row0, put):
         here = pl.ds(row0, TILE)
-        put(pl.ds(0, TILE), dot(mixed[here, :], w_out[...]) + dot(hid[here, :], w_down[...]))
-
-    def keep_temp(rows_at, part):
-        temp[0, rows_at, :] = part
+        left, right = mixed[here, :], hid[here, :]
+        for columns in column_tiles:
+            put(columns, dot(left, w_out[:, columns]) + dot(right, w_down[:, columns]))
+
+    def keep_temp(number):
+        def put(columns, part):
+            temp[number, :, columns] = part
+
+        return put
 
     def own_copy(number, back=False):
         held = own_part.at[pl.ds(pl.multiple_of(number * TILE, TILE), TILE)]
-        return pltpu.make_async_copy(*((held, temp.at[0]) if back else (temp.at[0], held)), temp_sem.at[0])
+        if back:
+            return pltpu.make_async_copy(held, temp.at[number], temp_sem.at[number])
+        return pltpu.make_async_copy(temp.at[0], held, temp_sem.at[0])
 
     def produce(j, carry):
         @pl.when(j >= 2)
@@ -868,13 +880,17 @@
 
         @pl.when(j < 2)
         def _():
-            branch(pl.multiple_of(me * rows_own + j * TILE, TILE), keep_temp)
+            branch(pl.multiple_of(me * rows_own + j * TILE, TILE), keep_temp(0))
             own_copy(j).start()
             own_copy(j).wait()
 
         pl.when(j == 1)(lambda: slope_copy(0, True).start())
         pl.when(j == 2)(lambda: slope_copy(1, True).start())
-        tick_at(j, 4, 5)
+
+        @pl.when(lax.div(j, 2) == 1)
+        def _():
+            tick(4 + j)
+
         return carry
 
     with jax.named_scope("outputs"):
@@ -895,7 +911,6 @@
             for k, rows_at in enumerate(here):
                 hid[rows_at, at : at + TILE] = d_up[k * UNIT : (k + 1) * UNIT]
         pl.when(p < 2)(lambda: slope_copy(p + 2, True).start())
-        tick_at(p, 4, 7)
         return carry
 
     with jax.named_scope("grad_gelu"):
@@ -982,7 +997,7 @@
             later, later_row = later * keep, later_row * keep
             high, low = split(later)
             more[at] = (
-                dot(both_k, wide([carried, carried]), NT) + under_k * ksums[block][0:1, :],
+                dot(both_k, wide([carried, carried]), NT) + under_k * ksums[pl.ds(block, 1), :],
                 dot(wide([value_k, value_k]), wide([high, low]), NT) + later_row,
                 dot(wide([key_k, key_k]), wide([high, low], 0)),
             )
@@ -1010,6 +1025,14 @@
     with jax.named_scope("mixer_back"):
         lax.fori_loop(0, chunks // 2, unmix, 0)
 
+    def own_tok(number):
+        return pltpu.make_async_copy(tok_in.at[pl.ds(number * TILE, TILE)], rs_out.at[number], result_sem.at[number])
+
+    settle(0)
+    for number in range(2):
+        own_copy(number, True).start()
+        own_tok(number).start()
+
     for j in range(n_one.shape[1] // TILE):
         tile = dot(n_one[:, j * TILE : (j + 1) * TILE], fqkv[...], TN).astype(BF)
         for s in range(3):
@@ -1024,43 +1047,41 @@
 
     sums[...] = jnp.zeros_like(sums)
 
-    def tok_copy(row0):
-        return pltpu.make_async_copy(tok_kept.at[pl.ds(row0, TILE)], tok_tile, tok_sem.at[0])
-
-    def row_grads(row0, put):
-        here = pl.ds(row0, TILE)
-        tok_copy(row0).start()
-        total = dot(fqkv[here, 0:width], w_qkv[0], NT)
-        for s in (1, 2):
-            total = total + dot(fqkv[here, s * width : (s + 1) * width], w_qkv[s], NT)
-        temp[0] = total
-        temp[1] = dot(hid[here, :], w_up[...], NT)
-        tok_copy(row0).wait()
-
-        def fold(i, inner):
-            at = pl.ds(pl.multiple_of(i * SUB, SUB), SUB)
-            unit, _ = centered(tok_tile, pl.multiple_of(i * SUB, SUB), SUB)
-            one, two = temp[0, at, :], temp[1, at, :]
-            for number, term in enumerate((one * unit, one, two * unit, two)):
-                sums[number] += jnp.sum(term.reshape(SUB // 8, 8, term.shape[1]), 0)
-            put(at, one * gain_one + two * gain_two)
-            return inner
-
-        lax.fori_loop(0, TILE // SUB, fold, 0)
+    def row_of(j):
+        owner = jnp.where(j < 2, cross, jnp.where(j < 4, peer, jnp.where(j < 6, mate, me)))
+        return pl.multiple_of(owner * rows_own + lax.rem(j, 2) * TILE, TILE)
+
+    def tok_copy(j):
+        which = lax.rem(j, 2)
+        return pltpu.make_async_copy(
+            tok_kept.at[pl.ds(row_of(j), TILE)], n_two.at[pl.ds(pl.multiple_of(which * TILE, TILE), TILE)], tok_sem.at[which]
+        )
+
+    def row_grads(j):
+        def compute(row0, put):
+            here = pl.ds(row0, TILE)
+            unit, _ = unit_rows(n_two[pl.ds(pl.multiple_of(lax.rem(j, 2) * TILE, TILE), TILE), :].astype(F32))
+            fields = [fqkv[here, s * width : (s + 1) * width] for s in range(3)]
+            right = hid[here, :]
+            for columns in column_tiles:
+                one = sum(dot(fields[s], w_qkv[s, columns, :], NT) for s in range(3))
+                two = dot(right, w_up[columns, :], NT)
+                part = unit[:, columns]
+                for number, term in enumerate((one * part, one, two * part, two)):
+                    sums[number, :, columns] += jnp.sum(term.reshape(TILE // 8, 8, TILE), 0)
+                put(columns, one * gain_one[:, columns] + two * gain_two[:, columns])
+
+        return compute
 
     def finish(number, carry):
-        row0 = pl.multiple_of(me * rows_own + number * TILE, TILE)
-        own_copy(number, True).start()
-        tok_copy(row0).start()
         own_copy(number, True).wait()
-        tok_copy(row0).wait()
+        own_tok(number).wait()
         gathered(0, number)
 
         def step(i, inner):
             at = pl.ds(pl.multiple_of(i * SUB, SUB), SUB)
-            total = temp[0, at, :] + rs_in[2 + number, at, :].astype(F32) + y_in[number, at, :].astype(F32)
-            total = total + tok_tile[at, :].astype(F32)
-            rs_out[number, at, :] = total.astype(BF)
+            total = temp[number, at, :] + rs_in[2 + number, at, :].astype(F32) + y_in[number, at, :].astype(F32)
+            rs_out[number, at, :] = (total + rs_out[number, at, :].astype(F32)).astype(BF)
             return inner
 
         lax.fori_loop(0, TILE // SUB, step, 0)
@@ -1068,45 +1089,45 @@
         return carry
 
     with jax.named_scope("finish"):
-        settle(0)
         lax.fori_loop(0, 2, finish, 0)
     pl.semaphore_signal(free_mate, inc=1, device_id={"tensor": mate}, device_id_type=MESH)
     pl.semaphore_signal(free_peer, inc=1, device_id={"tensor": peer}, device_id_type=MESH)
+    tok_copy(0).start()
     for number in range(2):
         stored(number, mixed_out.at[pl.ds(0, TILE)]).wait()
     pl.semaphore_wait(free_mate, 1)
     pl.semaphore_wait(free_peer, 1)
 
     def inputs(j, carry):
+        tok_copy(j).wait()
+        pl.when(j < 7)(lambda: tok_copy(j + 1).start())
+
         @pl.when(j < 6)
         def _():
-            scatter(j, 1, row_grads)
+            scatter(j, 1, row_grads(j))
 
         @pl.when(j >= 6)
         def _():
-            row_grads(pl.multiple_of(me * rows_own + (j - 6) * TILE, TILE), keep_temp)
-            own_copy(j - 6).start()
-            own_copy(j - 6).wait()
+            row_grads(j)(row_of(j), keep_temp(lax.rem(j, 2)))
 
         tick(19 + j)
         return carry
 
     with jax.named_scope("row_grads"):
         lax.fori_loop(0, 8, inputs, 0)
+    settle(1)
+    for number in range(2):
+        own_tok(number).start()
 
     def conclude(number):
-        row0 = pl.multiple_of(me * rows_own + number * TILE, TILE)
-        own_copy(number, True).start()
-        tok_copy(row0).start()
+        own_tok(number).wait()
         gathered(1, number)
-        own_copy(number, True).wait()
-        tok_copy(row0).wait()
 
         def step(i, inner):
             at = pl.ds(pl.multiple_of(i * SUB, SUB), SUB)
-            group_at = pl.multiple_of(row0 + i * SUB, SUB)
-            unit, deviation = centered(tok_tile, pl.multiple_of(i * SUB, SUB), SUB)
-            total = temp[0, at, :] + rs_in[2 + number, at, :].astype(F32) + y_in[number, at, :].astype(F32)
+            group_at = pl.multiple_of(me * rows_own + number * TILE + i * SUB, SUB)
+            unit, deviation = unit_rows(rs_out[number, at, :].astype(F32))
+            total = temp[number, at, :] + rs_in[2 + number, at, :].astype(F32) + y_in[number, at, :].astype(F32)
             along = jnp.mean(total * unit, -1, keepdims=True)
             total = total - jnp.mean(total, -1, keepdims=True) - unit * along
             total = cot[pl.ds(group_at, SUB), :].astype(F32) + deviation * total
@@ -1174,8 +1195,6 @@
 
                 @pl.when(t == settle_at + 2 * number)
                 def _():
-                    if number == 0:
-                        settle(1)
                     conclude(number)
 
             tick(t)
@@ -1185,7 +1204,6 @@
     else:
         for k in range(2):
             small_step(k)
-        settle(1)
         for number in range(2):
             conclude(number)
     for h in range(heads):
@@ -1262,7 +1280,6 @@
         in_specs=[smem, anywhere, anywhere] + [vmem] * 4 + [anywhere] * 4 + [vmem] * 6,
         out_specs=(anywhere,) * 7 + (vmem, vmem),
         scratch_shapes=[
-            pltpu.VMEM((TILE, model), BF),
             pltpu.VMEM((rows, model), BF),
             pltpu.VMEM((rows, model), BF),
             pltpu.VMEM((rows, model), BF),
@@ -1273,12 +1290,12 @@
             pltpu.VMEM((rows, width), F32),
             pltpu.VMEM((rows, width // 2), F32),
             pltpu.VMEM((rows // BLOCK, HEAD_DIM, width), BF),
-            pltpu.VMEM((rows // BLOCK, 8, width), F32),
+            pltpu.VMEM((rows // BLOCK, width), F32),
             pltpu.VMEM((width, width), F32),
             pltpu.VMEM((8, width), F32),
             pltpu.VMEM((units * UNIT, model), BF),
-            pltpu.VMEM((SLOTS // 2, 2 * UNIT, model), BF),
-            pltpu.VMEM((SLOTS // 2, 5 * UNIT // 2, model), BF),
+            pltpu.VMEM((BOXES_X, 2 * UNIT, model), BF),
+            pltpu.VMEM((BOXES_Z, 5 * UNIT // 2, model), BF),
             pltpu.VMEM((2, TILE, model), BF),
             pltpu.VMEM((4, TILE, model), BF),
             pltpu.VMEM((2, TILE, model), BF),
@@ -1303,7 +1320,7 @@
             pltpu.SemaphoreType.DMA((10,)),
             pltpu.SemaphoreType.DMA((units,)),
             pltpu.SemaphoreType.DMA((2,)),
-            pltpu.SemaphoreType.DMA((1,)),
+            pltpu.SemaphoreType.DMA((2,)),
             pltpu.SemaphoreType.DMA((2,)),
             pltpu.SemaphoreType.REGULAR,
             pltpu.SemaphoreType.REGULAR,

time: 217 us -> 207 us (0.954)
  Pallas kernels: 207 us -> 197 us
    pallas_call x1, Pallas kernels: 202 us -> 192 us  [shards(): pl.pallas_call(functools.partial(kernel, reduce_dp), out_shape=(shape((ro...]
where the time goes in v4:
time: 207 us; the launch traced here: 206 us
  Pallas kernels  197 us (95%)
  local copies, waits for them, and re-layouts  8.47 us (4%)
    pallas_call x1, Pallas kernels, shards(): pl.pallas_call(functools.partial(kernel, reduce_dp), out_shape=(shape((ro...  192 us
    pallas_call x1, Pallas kernels, shards(): pl.pallas_call(widen, grid=(steps,), out_shape=(shape((hidden, model), F3...  5.77 us
    unnamed x10, local copies, waits for them, and re-layouts  5.69 us

profile of v4, /device:TPU:0, one launch (start us, length us, event | category | flops | bytes accessed | tf_op | source)
XLA Modules:
  0.0 206.5 jit_solution(8100084958229037540)
XLA Ops:
  0.6 191.6 %shard_map.256 = (bf16[512,1024]{1,0:T(8,128)(2,1)}, bf16[512,1024]{1,0:T(8,128)(2,1)}, bf16[2304,1024]{1,0:T(8,128)(2,1)}, bf16[3,1024,256]{2,1,0:T(8,128)(2,1)...) custom-call(s32[1,3]{1,0:T(1,128)} %lengths.1, ...), custom_call_target="tpu_custom_call" | custom-call | tf_op jit(solution)/shard_map/pallas_call | solution.py:1267
  192.2 1.3 slice_bitcast_fusion
  193.5 1.5 fusion
  195.0 0.0 copy-start
  195.0 2.3 %copy-done = bf16[2304,1024]{1,0:T(8,128)(2,1)S(1)} copy-done((bf16[2304,1024]{1,0:T(8,128)(2,1)S(1)}, bf16[2304,1024]{1,0:T(8,128)(2,1)}, u32[]{:S(2)}) %copy-start) | copy-done | bytes 4718616
  197.3 0.0 copy-start.1
  197.3 1.4 copy-done.1
  198.7 0.0 copy-start.3
  198.7 0.0 copy-start.2
  198.7 5.8 %shard_map.257 = (f32[1024,1024]{1,0:T(8,128)}, f32[256,1024]{1,0:T(8,128)}, f32[1024,1024]{1,0:T(8,128)}, f32[3,1024,256]{2,1,0:T(8,128)}) custom-call(bf16[2304,1024]{1,0:T(8,128)(2,1)S(1)} %copy-done, bf16[2304,1024]{1,0:T(8,128)(2,1)S(1)} %copy-done, bf16[2304,1024]{1,0:T(8,128)(2,1)S(1)} %copy-done, bf16[3,1024,256]{2,1,0:T(8,128)(2,1)S(1)} %copy-done.1), custom_call_target="tpu_custom_call" | custom-call | tf_op jit(solution)/shard_map/pallas_call | solution.py:1339
  204.5 0.0 copy-done.3
  204.5 1.0 copy.31
  205.5 0.0 copy-done.2
  205.5 1.0 copy.32
Async XLA Ops:
  195.0 2.3 %copy-start = (bf16[2304,1024]{1,0:T(8,128)(2,1)S(1)}, bf16[2304,1024]{1,0:T(8,128)(2,1)}, u32[]{:S(2)}) copy-start(bf16[2304,1024]{1,0:T(8,128)(2,1)} %get-tuple-element.25.down_in.out_in.up_in) | copy-start | bytes 14155780
  197.3 1.4 copy-start.1
  198.7 5.8 %copy-start.3 = (bf16[512,1024]{1,0:T(8,128)(2,1)S(1)}, bf16[512,1024]{1,0:T(8,128)(2,1)}, u32[]{:S(2)}) copy-start(bf16[512,1024]{1,0:T(8,128)(2,1)} %get-tuple-element.50) | copy-start | bytes 3145732
  198.7 6.7 %copy-start.2 = (bf16[512,1024]{1,0:T(8,128)(2,1)S(1)}, bf16[512,1024]{1,0:T(8,128)(2,1)}, u32[]{:S(2)}) copy-start(bf16[512,1024]{1,0:T(8,128)(2,1)} %get-tuple-element.51) | copy-start | bytes 3145732

commit v5 on v4

--- a/solution.py
+++ b/solution.py
@@ -15,11 +15,14 @@
 BLOCK = 64
 CHUNK = 128
 TILE = 256
-UNIT = 128
+PIECE = 128
+UNIT = 64
 SUB = 32
-BOXES_X = 9
+LEAD = 2
+LAG = 2
+BOXES_X = 12
 BOXES_Z = 6
-LATE = 18
+LATE = 36
 MESH = pl.DeviceIdType.MESH
 F32 = jnp.float32
 BF = jnp.bfloat16
@@ -193,12 +196,12 @@
         if columns:
             here = pl.ds(pl.multiple_of(owner * rows_own, rows_own), rows_own)
             return buf.at[here, piece * TILE : (piece + 1) * TILE]
-        return buf.at[pl.ds(pl.multiple_of(owner * rows_own + piece * UNIT, UNIT), UNIT)]
+        return buf.at[pl.ds(pl.multiple_of(owner * rows_own + piece * PIECE, PIECE), PIECE)]
 
     class Gather:
         def __init__(self, source, buf, base, columns):
             self.source, self.buf, self.base, self.columns = source, buf, base, columns
-            self.pieces = source.shape[1] // TILE if columns else source.shape[0] // UNIT
+            self.pieces = source.shape[1] // TILE if columns else source.shape[0] // PIECE
 
         def copy(self, number, src, dst, target):
             return pltpu.make_async_remote_copy(
@@ -220,14 +223,14 @@
             if self.columns:
                 part = self.source.at[:, piece * TILE : (piece + 1) * TILE]
             else:
-                part = self.source.at[pl.ds(piece * UNIT, UNIT)]
+                part = self.source.at[pl.ds(piece * PIECE, PIECE)]
             return self.copy(1 + piece, part, slot(self.buf, owner, piece, self.columns), peer)
 
         def forward(self, owner, piece):
             part = slot(self.buf, owner, piece, self.columns)
             return self.copy(1 + self.pieces + piece, part, part, mate)
 
-    g_tok, g_cot = Gather(tok_in, tok, 0, False), Gather(cot_in, cot, 1 + 2 * (rows_own // UNIT), True)
+    g_tok, g_cot = Gather(tok_in, tok, 0, False), Gather(cot_in, cot, 1 + 2 * (rows_own // PIECE), True)
     g_tok.to_mate(me).start()
     for piece in range(g_tok.pieces):
         g_tok.to_peer(me, piece).start()
@@ -309,9 +312,9 @@
 
         late = lax.div(j, 4)
         early_at = jnp.where(j < 2, me, mate) * rows_own + lax.rem(j, 2) * TILE
-        row_a = pl.multiple_of(jnp.where(late == 0, early_at, peer * rows_own + (j - 4) * UNIT), UNIT)
-        row_b = pl.multiple_of(jnp.where(late == 0, early_at + UNIT, cross * rows_own + (j - 4) * UNIT), UNIT)
-        here = [pl.ds(row_a, UNIT), pl.ds(row_b, UNIT)]
+        row_a = pl.multiple_of(jnp.where(late == 0, early_at, peer * rows_own + (j - 4) * PIECE), PIECE)
+        row_b = pl.multiple_of(jnp.where(late == 0, early_at + PIECE, cross * rows_own + (j - 4) * PIECE), PIECE)
+        here = [pl.ds(row_a, PIECE), pl.ds(row_b, PIECE)]
 
         for at in here:
             pltpu.make_async_copy(tok.at[at], tok_kept.at[at], tok_sem.at[0]).start()
@@ -319,13 +322,13 @@
         first = (unit * gain_one + bias_one).astype(BF)
         second = (unit * gain_two + bias_two).astype(BF)
         for k, at in enumerate(here):
-            n_one[at, :] = first[k * UNIT : (k + 1) * UNIT]
-            n_two[at, :] = second[k * UNIT : (k + 1) * UNIT]
-        turn = [wide(pair, 0) for pair in zip(*(rotation(at, UNIT // BLOCK) for at in (row_a, row_b)))]
+            n_one[at, :] = first[k * PIECE : (k + 1) * PIECE]
+            n_two[at, :] = second[k * PIECE : (k + 1) * PIECE]
+        turn = [wide(pair, 0) for pair in zip(*(rotation(at, PIECE // BLOCK) for at in (row_a, row_b)))]
 
         def keep(write, value):
             for k, at in enumerate(here):
-                write(at, value[k * UNIT : (k + 1) * UNIT])
+                write(at, value[k * PIECE : (k + 1) * PIECE])
 
         def keep_field(s, value):
             def write(at, part):
@@ -442,11 +445,12 @@
         return carry
 
     def add_parts(base, first, count, sources):
-        for at in range(0, count, SUB):
-            total = base[pl.ds(first + at, SUB), :].astype(F32)
+        cut = min(SUB, count)
+        for at in range(0, count, cut):
+            total = base[pl.ds(first + at, cut), :].astype(F32)
             for source, place in sources:
-                total = total + source[pl.ds(place + at, SUB), :].astype(F32)
-            base[pl.ds(first + at, SUB), :] = total.astype(BF)
+                total = total + source[pl.ds(place + at, cut), :].astype(F32)
+            base[pl.ds(first + at, cut), :] = total.astype(BF)
 
     def bring(base, first, box, place, count):
         base[pl.ds(first, count), :] = box[pl.ds(place, count), :]
@@ -459,17 +463,18 @@
     def unit_of(n):
         return grads.at[pl.ds(pl.multiple_of(n * UNIT, UNIT), UNIT)]
 
-    def hop(n, kind, source, target, device):
+    def hop(box, kind, source, target, device):
         return pltpu.make_async_remote_copy(
             src_ref=source,
             dst_ref=target,
-            send_sem=ar_send.at[n, kind],
-            recv_sem=ar_recv.at[n, kind],
+            send_sem=ar_send.at[box, kind],
+            recv_sem=ar_recv.at[box, kind],
             device_id={"dp": device},
             device_id_type=MESH,
         )
 
     plain = units - 3 * width // UNIT
+    per_tile = TILE // UNIT
 
     class Copies:
         def __init__(self, n):
@@ -477,16 +482,16 @@
 
         def whole(self):
             first = pl.multiple_of(self.n * UNIT, UNIT)
-            return pltpu.make_async_copy(unit_of(self.n), grads_out.at[pl.ds(first, UNIT)], grad_sem.at[self.n])
+            return pltpu.make_async_copy(unit_of(self.n), grads_out.at[pl.ds(first, UNIT)], grad_sem.at[0])
 
         def piece(self, q):
             u = self.n - plain
-            at = 4 * lax.div(u, 2) + q
-            row = pl.multiple_of(lax.div(at, 3) * TILE + lax.rem(u, 2) * UNIT, UNIT)
+            at = 4 * lax.div(u, per_tile) + q
+            row = pl.multiple_of(lax.div(at, 3) * TILE + lax.rem(u, per_tile) * UNIT, UNIT)
             return pltpu.make_async_copy(
                 unit_of(self.n).at[:, q * width : (q + 1) * width],
                 qkv_out.at[lax.rem(at, 3), pl.ds(row, UNIT)],
-                grad_sem.at[self.n],
+                grad_sem.at[1],
             )
 
         def start(self):
@@ -496,14 +501,6 @@
             def _():
                 for q in range(4):
                     self.piece(q).start()
-
-        def wait(self):
-            pl.when(self.n < plain)(lambda: self.whole().wait())
-
-            @pl.when(self.n >= plain)
-            def _():
-                for q in range(4):
-                    self.piece(q).wait()
 
     def kind_of(n):
         return jnp.where(n < LATE, lax.rem(n, 2), 0)
@@ -519,11 +516,11 @@
         @pl.when(code < 4)
         def _():
             theirs = unit_of(n).at[pl.ds(rows_of(1 - along_x, half), half)]
-            hop(n, 0, theirs, recv_a.at[place, pl.ds(0, half)], across).start()
+            hop(place, 0, theirs, recv_a.at[place, pl.ds(0, half)], across).start()
 
         @pl.when(code == 4)
         def _():
-            hop(n, 0, unit_of(n), recv_b.at[place_b, pl.ds(0, UNIT)], inward).start()
+            hop(BOXES_X + place_b, 0, unit_of(n), recv_b.at[place_b, pl.ds(0, UNIT)], inward).start()
 
     def advance(n, stage):
         kind = jnp.where(n < 0, 2, jnp.where(n >= units, 2, kind_of(n)))
@@ -543,22 +540,22 @@
             return base.at[pl.ds(first, size)]
 
         def x_one():
-            return hop(n, 0, rows(theirs_at, half), box.at[pl.ds(0, half)], across)
+            return hop(place, 0, rows(theirs_at, half), box.at[pl.ds(0, half)], across)
 
         def z_one():
-            return hop(n, 1, rows(mine_at, half), box.at[pl.ds(half, half)], inward)
+            return hop(place, 1, rows(mine_at, half), box.at[pl.ds(half, half)], inward)
 
         def z_two():
-            return hop(n, 2, rows(other_at, quarter), box.at[pl.ds(2 * half, quarter)], inward)
+            return hop(place, 2, rows(other_at, quarter), box.at[pl.ds(2 * half, quarter)], inward)
 
         def z_swap():
-            return hop(n, 3, rows(own_at, quarter), box.at[pl.ds(swap_at, quarter)], inward)
+            return hop(place, 3, rows(own_at, quarter), box.at[pl.ds(swap_at, quarter)], inward)
 
         def out(kind, first, place_in):
-            return hop(n, kind, rows(first, quarter), box.at[pl.ds(half + place_in, quarter)], outward)
+            return hop(place, kind, rows(first, quarter), box.at[pl.ds(half + place_in, quarter)], outward)
 
         def x_two():
-            return hop(n, 6, rows(mine_at, half), box.at[pl.ds(last_at, half)], across)
+            return hop(place, 6, rows(mine_at, half), box.at[pl.ds(last_at, half)], across)
 
         swap_at, last_at = 2 * half + quarter, 3 * half
 
@@ -629,22 +626,22 @@
         own_part_at, other_part_at = rows_of(along_x, quarter), rows_of(1 - along_x, quarter)
 
         def z_in():
-            return hop(n, 0, base, box_b.at[pl.ds(0, UNIT)], inward)
+            return hop(BOXES_X + place_b, 0, base, box_b.at[pl.ds(0, UNIT)], inward)
 
         def z_mid():
-            return hop(n, 1, rows(theirs_z, half), box_b.at[pl.ds(UNIT, half)], inward)
+            return hop(BOXES_X + place_b, 1, rows(theirs_z, half), box_b.at[pl.ds(UNIT, half)], inward)
 
         def x_mid():
-            return hop(n, 2, rows(other_x, quarter), box_b.at[pl.ds(UNIT + half, quarter)], across)
+            return hop(BOXES_X + place_b, 2, rows(other_x, quarter), box_b.at[pl.ds(UNIT + half, quarter)], across)
 
         def x_swap():
-            return hop(n, 3, rows(own_x, quarter), box_b.at[pl.ds(swap_at, quarter)], across)
+            return hop(BOXES_X + place_b, 3, rows(own_x, quarter), box_b.at[pl.ds(swap_at, quarter)], across)
 
         def z_share():
-            return hop(n, 4, rows(mine_z, half), box_b.at[pl.ds(last_at, half)], inward)
+            return hop(BOXES_X + place_b, 4, rows(mine_z, half), box_b.at[pl.ds(last_at, half)], inward)
 
         def z_out(kind, first):
-            return hop(n, kind, rows(first, half), box_b.at[pl.ds(first, half)], outward)
+            return hop(BOXES_X + place_b, kind, rows(first, half), box_b.at[pl.ds(first, half)], outward)
 
         swap_at, last_at = UNIT + half + quarter, 2 * UNIT
 
@@ -712,7 +709,7 @@
             pl.when(kind < 2)(lambda: Copies(n).start())
 
     def at_ready(n):
-        return jnp.where(n < 2, 1, jnp.where(n < plain, 0, jnp.where(n < plain + 2, 1, 0)))
+        return jnp.where(n < LEAD, 1, jnp.where(n < plain, 0, jnp.where(n < plain + LEAD, 1, 0)))
 
     def ready(first, count):
         for n in (first + k for k in range(count)):
@@ -728,8 +725,8 @@
 
     def move(t):
         for stage in (6, 5, 4, 3, 2, 1):
-            advance(t - 2 * (stage - 1), stage)
-        later = t + 2
+            advance(t - LAG * (stage - 1), stage)
+        later = t + LEAD
 
         @pl.when(jnp.where(later >= units, 1, at_ready(later)) == 0)
         def _():
@@ -740,7 +737,14 @@
         def _():
             tick(first + lax.div(j, every))
 
-    ticks = units + 10
+    ticks = units + 5 * LAG
+
+    def run_ticks(first, last):
+        lax.fori_loop(first, last, pause, 0)
+
+    def pause(t, carry):
+        tick(t)
+        return carry
 
     def to_mate(which, number):
         return pltpu.make_async_remote_copy(
@@ -808,7 +812,6 @@
         grads[pl.ds(pl.multiple_of(n * UNIT, UNIT), value.shape[0]), :] = value
         ready(n, value.shape[0] // UNIT)
 
-    per_tile = TILE // UNIT
     first_out = hid.shape[1] // UNIT
     first_up = first_out + width // UNIT
 
@@ -832,26 +835,23 @@
         down(0)
         down(1)
     mix_some(0, pairs // 4)
-    tick(jnp.int32(0))
+    run_ticks(0, 1)
     arrive(2)
     mix_some(pairs // 4, pairs // 2)
+    run_ticks(1, 3)
     with jax.named_scope("grad_down"):
         down(2)
 
-    def pause(t, carry):
-        tick(t)
-        return carry
-
-    lax.fori_loop(1, 3, pause, 0)
+    run_ticks(3, 5)
     mix_some(pairs // 2, 3 * pairs // 4)
-    tick(jnp.int32(3))
+    run_ticks(5, 7)
     arrive(3)
     mix_some(3 * pairs // 4, pairs)
     with jax.named_scope("grad_down"):
         down(3)
-    tick(jnp.int32(4))
+    run_ticks(7, 9)
     keep_unit(first_out, dot(mixed[...], cot[...], TN).astype(BF))
-    tick(jnp.int32(5))
+    run_ticks(9, 11)
 
     column_tiles = [slice(at, at + TILE) for at in range(0, cot.shape[1], TILE)]
 
@@ -886,10 +886,7 @@
 
         pl.when(j == 1)(lambda: slope_copy(0, True).start())
         pl.when(j == 2)(lambda: slope_copy(1, True).start())
-
-        @pl.when(lax.div(j, 2) == 1)
-        def _():
-            tick(4 + j)
+        tick_at(j, 2, 11)
 
         return carry
 
@@ -901,7 +898,7 @@
     bring_up.start()
 
     def descend(p, carry):
-        here = [pl.ds(pl.multiple_of(owner * rows_own + p * UNIT, UNIT), UNIT) for owner in (peer, cross)]
+        here = [pl.ds(pl.multiple_of(owner * rows_own + p * PIECE, PIECE), PIECE) for owner in (peer, cross)]
         parity = lax.rem(p, 2)
         slope_copy(p, True).wait()
         turned = wide([cot[at, :] for at in here], 0)
@@ -909,8 +906,9 @@
             d_hidden = dot(turned, w_down[at : at + TILE, :], NT)
             d_up = (d_hidden * temp[parity, :, at : at + TILE]).astype(BF)
             for k, rows_at in enumerate(here):
-                hid[rows_at, at : at + TILE] = d_up[k * UNIT : (k + 1) * UNIT]
+                hid[rows_at, at : at + TILE] = d_up[k * PIECE : (k + 1) * PIECE]
         pl.when(p < 2)(lambda: slope_copy(p + 2, True).start())
+        tick_at(p, 2, 15)
         return carry
 
     with jax.named_scope("grad_gelu"):
@@ -920,7 +918,7 @@
     def upward(j, carry):
         at = pl.ds(pl.multiple_of(j * TILE, TILE), TILE)
         keep_unit(first_up + per_tile * j, dot(n_two[:, at], hid[...], TN).astype(BF))
-        tick_at(j, 2, 8)
+        run_ticks(17 + j, 18 + j)
         return carry
 
     with jax.named_scope("grad_up"):
@@ -1018,7 +1016,7 @@
             fqkv[here, s * width : (s + 1) * width] = rotate(back, turn, True).astype(BF)
         d_value = wide([d_value[c][:, :width] + d_value[c][:, width:] for c in both_chunks], 0)
         fqkv[here, 2 * width : 3 * width] = (d_value + wide([more[at][2] for at in range(4)], 0)).astype(BF)
-        tick(10 + step)
+        run_ticks(21 + lax.div(15 * step, chunks // 2), 21 + lax.div(15 * (step + 1), chunks // 2))
 
         return carry
 
@@ -1043,7 +1041,7 @@
             ready(plain + (j - 1) * per_tile, per_tile)
 
 
-    tick(jnp.int32(18))
+    run_ticks(36, 38)
 
     sums[...] = jnp.zeros_like(sums)
 
@@ -1110,7 +1108,7 @@
         def _():
             row_grads(j)(row_of(j), keep_temp(lax.rem(j, 2)))
 
-        tick(19 + j)
+        run_ticks(38 + 2 * j, 40 + 2 * j)
         return carry
 
     with jax.named_scope("row_grads"):
@@ -1185,37 +1183,23 @@
                 total = total + small_wide[member]
             small[...] = total
 
-    settle_at, late = 28, {27: 0, 29: 1, 32: 2}
+    small_step(0)
+    run_ticks(54, 55)
+    conclude(0)
+    small_step(1)
+    run_ticks(55, 56)
+    conclude(1)
+    run_ticks(56, 57)
+    small_step(2)
     if reduce_dp:
-
-        def rest(t, carry):
-            for at, k in late.items():
-                pl.when(t == at)(functools.partial(small_step, k))
-            for number in range(2):
-
-                @pl.when(t == settle_at + 2 * number)
-                def _():
-                    conclude(number)
-
-            tick(t)
-            return carry
-
-        lax.fori_loop(27, ticks, rest, 0)
-    else:
-        for k in range(2):
-            small_step(k)
-        for number in range(2):
-            conclude(number)
+        run_ticks(57, ticks)
     for h in range(heads):
         at = slice(h * HEAD_DIM, (h + 1) * HEAD_DIM)
         feat_out[0, h : h + 1, :] = small[4:5, at]
         feat_out[1, h : h + 1, :] = small[5:6, at]
 
-    def copied(n, carry):
-        Copies(n).wait()
-        return carry
-
-    lax.fori_loop(0, units, copied, 0)
+    pltpu.make_async_copy(grads.at[pl.ds(0, plain * UNIT)], grads_out, grad_sem.at[0]).wait()
+    pltpu.make_async_copy(w_qkv, qkv_out, grad_sem.at[1]).wait()
     for number in range(2):
         stored(number, input_grad.at[pl.ds(0, TILE)]).wait()
 
@@ -1227,12 +1211,18 @@
         g_cot.forward(peer, piece).wait_send()
 
 
-def widen(down_in, out_in, up_in, qkv_in, *outs):
-    down, out, up, qkv = outs
+def widen(down_in, out_in, up_in, qkv_in, small_in, feats_in, mixed_in, input_in, *outs):
+    down, out, up, qkv, *norms, scale, weight, mixed, input_grad = outs
     down[...] = down_in[...].astype(F32).T
     out[...] = out_in[...].astype(F32)
     up[...] = up_in[...].astype(F32)
     qkv[...] = qkv_in[...].astype(F32)
+    for number, norm in enumerate(norms):
+        norm[...] = small_in[number : number + 1, :]
+    scale[...] = feats_in[0]
+    weight[...] = feats_in[1]
+    mixed[...] = mixed_in[...]
+    input_grad[...] = input_in[...]
 
 
 def shards(
@@ -1308,17 +1298,17 @@
             pltpu.VMEM(w_out.shape, BF),
             pltpu.VMEM(w_up.shape, BF),
             pltpu.VMEM(w_down.shape, BF),
-            pltpu.SemaphoreType.DMA((2 + 2 * rows_own // UNIT,)),
-            pltpu.SemaphoreType.DMA((2 + 2 * rows_own // UNIT + 2 * model // TILE,)),
-            pltpu.SemaphoreType.DMA((2 + 2 * rows_own // UNIT + 2 * model // TILE,)),
+            pltpu.SemaphoreType.DMA((2 + 2 * rows_own // PIECE,)),
+            pltpu.SemaphoreType.DMA((2 + 2 * rows_own // PIECE + 2 * model // TILE,)),
+            pltpu.SemaphoreType.DMA((2 + 2 * rows_own // PIECE + 2 * model // TILE,)),
             pltpu.SemaphoreType.DMA((4,)),
-            pltpu.SemaphoreType.DMA((units, 7)),
-            pltpu.SemaphoreType.DMA((units, 7)),
+            pltpu.SemaphoreType.DMA((BOXES_X + BOXES_Z, 7)),
+            pltpu.SemaphoreType.DMA((BOXES_X + BOXES_Z, 7)),
             pltpu.SemaphoreType.DMA((2, 6)),
             pltpu.SemaphoreType.DMA((2, 6)),
             pltpu.SemaphoreType.DMA((10,)),
             pltpu.SemaphoreType.DMA((10,)),
-            pltpu.SemaphoreType.DMA((units,)),
+            pltpu.SemaphoreType.DMA((2,)),
             pltpu.SemaphoreType.DMA((2,)),
             pltpu.SemaphoreType.DMA((2,)),
             pltpu.SemaphoreType.DMA((2,)),
@@ -1329,14 +1319,18 @@
             collective_id=0, has_side_effects=True, vmem_limit_bytes=62 * 2**20
         ),
     )(lengths, tokens, cotangent, *norms, w_qkv, w_out, w_up, w_down, feature_scale, feature_weight, *consts)
-    norm_sums = small[0:4]
     if not reduce_dp:
-        grads, g_qkv, norm_sums, feats = lax.psum(
-            (*lax.optimization_barrier((grads.astype(F32), g_qkv.astype(F32))), norm_sums, feats), "dp"
+        grads, g_qkv, small, feats = lax.psum(
+            (*lax.optimization_barrier((grads.astype(F32), g_qkv.astype(F32))), small, feats), "dp"
         )
-    steps = 8
-    down_cut, out_cut, up_cut, row_cut = hidden // steps, width // steps, model // steps, model // steps
-    g_down, g_out, g_up, g_qkv = pl.pallas_call(
+    steps = 4
+    down_cut, out_cut, up_cut, row_cut, own_cut = (
+        size // steps for size in (hidden, width, model, model, rows_own)
+    )
+    rows_spec = pl.BlockSpec((own_cut, model), lambda i: (i, 0))
+    row_spec = pl.BlockSpec((1, model), lambda i: (0, 0))
+    feat_spec = pl.BlockSpec((heads, HEAD_DIM), lambda i: (0, 0))
+    g_down, g_out, g_up, g_qkv, *norm_sums, g_scale, g_weight, mixed_out, input_grad = pl.pallas_call(
         widen,
         grid=(steps,),
         out_shape=(
@@ -1344,34 +1338,41 @@
             shape((width, model), F32),
             shape((model, hidden), F32),
             shape((3, model, width), F32),
+            *[shape((1, model), F32)] * 4,
+            *[shape((heads, HEAD_DIM), F32)] * 2,
+            *[shape((rows_own, model), BF)] * 2,
         ),
         in_specs=[
             pl.BlockSpec((model, down_cut), lambda i: (0, i)),
             pl.BlockSpec((out_cut, model), lambda i: (hidden // out_cut + i, 0)),
             pl.BlockSpec((up_cut, hidden), lambda i: ((hidden + width) // up_cut + i, 0)),
             pl.BlockSpec((3, row_cut, width), lambda i: (0, i, 0)),
+            pl.BlockSpec((8, model), lambda i: (0, 0)),
+            pl.BlockSpec((2, heads, HEAD_DIM), lambda i: (0, 0, 0)),
+            rows_spec,
+            rows_spec,
         ],
         out_specs=(
             pl.BlockSpec((down_cut, model), lambda i: (i, 0)),
             pl.BlockSpec((out_cut, model), lambda i: (i, 0)),
             pl.BlockSpec((up_cut, hidden), lambda i: (i, 0)),
             pl.BlockSpec((3, row_cut, width), lambda i: (0, i, 0)),
+            *[row_spec] * 4,
+            *[feat_spec] * 2,
+            *[rows_spec] * 2,
         ),
-        compiler_params=pltpu.CompilerParams(vmem_limit_bytes=24 * 2**20),
-    )(grads, grads, grads, g_qkv)
+        compiler_params=pltpu.CompilerParams(vmem_limit_bytes=60 * 2**20),
+    )(grads, grads, grads, g_qkv, small, feats, mixed_out, input_grad)
     return (
         mixed_out,
         input_grad,
-        norm_sums[0],
-        norm_sums[1],
-        norm_sums[2],
-        norm_sums[3],
+        *[value.reshape(model) for value in norm_sums],
         g_qkv,
         g_out,
         g_up,
         g_down,
-        feats[0],
-        feats[1],
+        g_scale,
+        g_weight,
     )
 
 

time: 207 us -> 197 us (0.952)
  local copies, waits for them, and re-layouts: 8.47 us -> 0 us
    unnamed x10 -> x0, local copies, waits for them, and re-layouts: 5.69 us -> none
    pallas_call x1, Pallas kernels: 192 us -> 187 us  [shards(): pl.pallas_call(functools.partial(kernel, reduce_dp), out_shape=(shape((ro...]
    pallas_call x1, Pallas kernels: 5.77 us -> 9.39 us  [shards(): pl.pallas_call(widen, grid=(steps,), out_shape=(shape((hidden, model), F3...]
where the time goes in v5:
time: 197 us
  Pallas kernels  196 us (99%)
    pallas_call x1, Pallas kernels, shards(): pl.pallas_call(functools.partial(kernel, reduce_dp), out_shape=(shape((ro...  187 us
    pallas_call x1, Pallas kernels, shards(): pl.pallas_call(widen, grid=(steps,), out_shape=(shape((hidden, model), F3...  9.39 us

profile of v5, /device:TPU:0, one launch (start us, length us, event | category | flops | bytes accessed | tf_op | source)
XLA Modules:
  0.0 196.9 jit_solution(2597167512960238146)
XLA Ops:
  0.6 186.7 %shard_map.256 = (bf16[512,1024]{1,0:T(8,128)(2,1)}, bf16[512,1024]{1,0:T(8,128)(2,1)}, bf16[2304,1024]{1,0:T(8,128)(2,1)}, bf16[3,1024,256]{2,1,0:T(8,128)(2,1)...) custom-call(s32[1,3]{1,0:T(1,128)} %lengths.1, ...), custom_call_target="tpu_custom_call" | custom-call | tf_op jit(solution)/shard_map/pallas_call | solution.py:1257
  187.3 9.4 %shard_map.257 = (f32[1024,1024]{1,0:T(8,128)}, f32[256,1024]{1,0:T(8,128)}, f32[1024,1024]{1,0:T(8,128)}, f32[3,1024,256]{2,1,0:T(8,128)}, f32[1,1024]{1,0:T(1,...) custom-call(bf16[2304,1024]{1,0:T(8,128)(2,1)} %get-tuple-element.30, ...), custom_call_target="tpu_custom_call" | custom-call | tf_op jit(solution)/shard_map/pallas_call | solution.py:1333

commit v6 on v5

--- a/solution.py
+++ b/solution.py
@@ -20,9 +20,8 @@
 SUB = 32
 LEAD = 2
 LAG = 2
-BOXES_X = 12
+BOXES_X = 6
 BOXES_Z = 6
-LATE = 36
 MESH = pl.DeviceIdType.MESH
 F32 = jnp.float32
 BF = jnp.bfloat16
@@ -52,7 +51,7 @@
     dct = np.kron(np.eye(heads), dct).astype(np.float32)
     high = dct.astype(ml_dtypes.bfloat16)
     low = (dct - high.astype(np.float32)).astype(ml_dtypes.bfloat16)
-    halves = np.concatenate([high, high, low], 1)
+    halves = np.concatenate([high, low], 1)
     half = ROT // 2
     lane = np.arange(2 * HEAD_DIM) % HEAD_DIM
     rate = np.where(lane < ROT, 10000.0 ** (-(lane % half) * 2.0 / ROT), 0.0)
@@ -60,12 +59,12 @@
     of_block = np.arange(blocks)[:, None] * BLOCK * rate[None]
     signs = np.stack([np.where(lane < half, -1.0, 0.0), np.where((lane >= half) & (lane < ROT), 1.0, 0.0)] + [0.0 * lane] * 6)
     angles = np.concatenate([np.cos(in_block), np.sin(in_block), np.cos(of_block), np.sin(of_block), signs], 0)
-    diagonal = np.kron(np.eye(heads), np.ones((HEAD_DIM, HEAD_DIM)))
+    block_ones = np.kron(np.eye(heads), np.ones((HEAD_DIM, HEAD_DIM)))
     masks = np.kron(np.eye(heads), np.ones((CHUNK, HEAD_DIM)))
     return (
         halves,
         angles.astype(np.float32),
-        np.concatenate([diagonal, diagonal], 0).astype(ml_dtypes.bfloat16),
+        block_ones.astype(ml_dtypes.bfloat16),
         masks.astype(ml_dtypes.bfloat16),
     )
 
@@ -87,14 +86,13 @@
     feature_weight,
     dct,
     angles,
-    diag_two,
+    diagonal,
     masks,
     mixed_out,
     input_grad,
     grads_out,
     qkv_out,
     slopes,
-    own_part,
     tok_kept,
     small,
     feat_out,
@@ -102,6 +100,7 @@
     n_one,
     n_two,
     hid,
+    d_up,
     fqkv,
     spec,
     mixed,
@@ -282,14 +281,49 @@
         deviation = lax.rsqrt(jnp.mean(value * value, -1, keepdims=True) + 1e-05)
         return value * deviation, deviation
 
-    chip_row = pl.multiple_of(lax.div(me, 2) * 2 * rows_own, rows_own)
-
     def slope_copy(p, back=False):
         held = slopes.at[pl.ds(pl.multiple_of(p * TILE, TILE), TILE)]
         slot_of = temp.at[lax.rem(p, 2)]
         return pltpu.make_async_copy(*((held, slot_of) if back else (slot_of, held)), temp_sem.at[lax.rem(p, 2)])
 
+    def tile_rows(j):
+        late = lax.div(j, 4)
+        early_at = jnp.where(j < 2, me, mate) * rows_own + lax.rem(j, 2) * TILE
+        row_a = pl.multiple_of(jnp.where(late == 0, early_at, peer * rows_own + (j - 4) * PIECE), PIECE)
+        row_b = pl.multiple_of(jnp.where(late == 0, early_at + PIECE, cross * rows_own + (j - 4) * PIECE), PIECE)
+        return late, row_a, row_b, [pl.ds(row_a, PIECE), pl.ds(row_b, PIECE)]
+
+    def keep_rows(here, write, value):
+        for k, at in enumerate(here):
+            write(at, value[k * PIECE : (k + 1) * PIECE])
+
+    def attend(j, carry):
+        _, row_a, row_b, here = tile_rows(j)
+        first = wide([n_one[at, :] for at in here], 0)
+        turn = [wide(pair, 0) for pair in zip(*(rotation(at, PIECE // BLOCK) for at in (row_a, row_b)))]
+
+        def keep_field(s, value):
+            def write(at, part):
+                fqkv[at, s * width : (s + 1) * width] = part
+
+            keep_rows(here, write, value.astype(BF))
+
+        for s in range(2):
+            high, low = split(rotate(dot(first, w_qkv[s]), turn))
+            table = dct[:, 0:width]
+            spectrum = dot(high, table, NT) + dot(low, table, NT) + dot(high, dct[:, width:], NT)
+
+            def keep_spectrum(at, part):
+                spec[s, at, :] = part
+
+            keep_rows(here, keep_spectrum, spectrum)
+            keep_field(s, weight_row * jnp.exp(scale_row * spectrum))
+        keep_field(2, dot(first, w_qkv[2]))
+        return carry
+
     def project(j, carry):
+        pl.when(j >= 4)(lambda: attend(j - 4, None))
+
         @pl.when(j == 0)
         def _():
             g_tok.local().wait()
@@ -310,12 +344,7 @@
                 g_cot.to_peer(me, piece).start()
                 g_tok.forward(cross, piece).wait_recv()
 
-        late = lax.div(j, 4)
-        early_at = jnp.where(j < 2, me, mate) * rows_own + lax.rem(j, 2) * TILE
-        row_a = pl.multiple_of(jnp.where(late == 0, early_at, peer * rows_own + (j - 4) * PIECE), PIECE)
-        row_b = pl.multiple_of(jnp.where(late == 0, early_at + PIECE, cross * rows_own + (j - 4) * PIECE), PIECE)
-        here = [pl.ds(row_a, PIECE), pl.ds(row_b, PIECE)]
-
+        late, row_a, _, here = tile_rows(j)
         for at in here:
             pltpu.make_async_copy(tok.at[at], tok_kept.at[at], tok_sem.at[0]).start()
         unit, _ = unit_rows(wide([tok[at, :] for at in here], 0).astype(F32))
@@ -324,28 +353,6 @@
         for k, at in enumerate(here):
             n_one[at, :] = first[k * PIECE : (k + 1) * PIECE]
             n_two[at, :] = second[k * PIECE : (k + 1) * PIECE]
-        turn = [wide(pair, 0) for pair in zip(*(rotation(at, PIECE // BLOCK) for at in (row_a, row_b)))]
-
-        def keep(write, value):
-            for k, at in enumerate(here):
-                write(at, value[k * PIECE : (k + 1) * PIECE])
-
-        def keep_field(s, value):
-            def write(at, part):
-                fqkv[at, s * width : (s + 1) * width] = part
-
-            keep(write, value.astype(BF))
-
-        for s in range(2):
-            high, low = split(rotate(dot(first, w_qkv[s]), turn))
-            spectrum = dot(wide([high, low]), dct[:, 0 : 2 * width], NT) + dot(high, dct[:, 2 * width :], NT)
-
-            def keep_spectrum(at, part):
-                spec[s, at, :] = part
-
-            keep(keep_spectrum, spectrum)
-            keep_field(s, weight_row * jnp.exp(scale_row * spectrum))
-        keep_field(2, dot(first, w_qkv[2]))
         parity = lax.rem(j, 2)
         pl.when(j >= 6)(lambda: slope_copy(j - 6).wait())
         for at in range(0, w_up.shape[1], TILE):
@@ -355,7 +362,7 @@
             def keep_hidden(rows_at, part):
                 hid[rows_at, at : at + TILE] = part
 
-            keep(keep_hidden, (up * below).astype(BF))
+            keep_rows(here, keep_hidden, (up * below).astype(BF))
             temp[parity, :, at : at + TILE] = below + up * (
                 jnp.exp(-0.5 * up * up) * (1.0 / math.sqrt(2.0 * math.pi))
             )
@@ -363,10 +370,10 @@
         @pl.when(late == 0)
         def _():
             turned = wide([cot[at, :] for at in here], 0)
-            first_at = pl.multiple_of(rows + row_a - chip_row, TILE)
+            first_at = pl.multiple_of(row_a, TILE)
             for at in range(0, hid.shape[1], TILE):
                 d_hidden = dot(turned, w_down[at : at + TILE, :], NT)
-                grads[pl.ds(first_at, TILE), at : at + TILE] = (d_hidden * temp[parity, :, at : at + TILE]).astype(BF)
+                d_up[pl.ds(first_at, TILE), at : at + TILE] = (d_hidden * temp[parity, :, at : at + TILE]).astype(BF)
 
         pl.when(late == 1)(lambda: slope_copy(j - 4).start())
         return carry
@@ -377,6 +384,8 @@
         lax.fori_loop(0, rows // TILE, project, 0)
     for p in (2, 3):
         slope_copy(p).wait()
+    for p in range(2):
+        slope_copy(p, True).start()
 
     grid_t = lax.broadcasted_iota(jnp.int32, (CHUNK, CHUNK), 0)
     grid_s = lax.broadcasted_iota(jnp.int32, (CHUNK, CHUNK), 1)
@@ -407,7 +416,7 @@
     krow[...] = jnp.zeros_like(krow)
 
     def mix(pair, carry):
-        diag = diag_two[0:width, :].astype(F32)
+        diag = diagonal[...].astype(F32)
         here = chunk_rows(pair)
         query, key, value = ([fqkv[at, s * width : (s + 1) * width] for at in here] for s in range(3))
         scores = [split(dot(query[c], per_head(key[c]), NT) * causal) for c in both_chunks]
@@ -436,7 +445,7 @@
             parts = halves(query[c])
             more = wide([dot(parts[k], carried[2 * c + k]) for k in both_blocks], 0)
             high, low = split(wide([parts[k].astype(F32) * rows_in[2 * c + k] for k in both_blocks], 0))
-            inverse = 1.0 / (under[c] + dot(wide([high, low]), diag_two[...]))
+            inverse = 1.0 / (under[c] + dot(high, diagonal[...]) + dot(low, diagonal[...]))
             attended = (over[c] + more) * inverse
             att[here[c], :] = attended
             rden[here[c], :] = wide([inverse[:, h * HEAD_DIM : h * HEAD_DIM + HEAD_DIM // 2] for h in range(heads)])
@@ -503,11 +512,10 @@
                     self.piece(q).start()
 
     def kind_of(n):
-        return jnp.where(n < LATE, lax.rem(n, 2), 0)
+        return lax.rem(n, 2)
 
     def box_of(n):
-        first = jnp.where(n < LATE, lax.div(n, 2), n - LATE // 2)
-        return lax.rem(first, BOXES_X), lax.rem(lax.div(n, 2), BOXES_Z)
+        return lax.rem(lax.div(n, 2), BOXES_X), lax.rem(lax.div(n, 2), BOXES_Z)
 
     def begin(n):
         place, place_b = box_of(n)
@@ -746,10 +754,22 @@
         tick(t)
         return carry
 
-    def to_mate(which, number):
+    def landed(which, number):
+        if which:
+            return n_one.at[pl.ds(pl.multiple_of(number * TILE, TILE), TILE)]
+        return rs_in.at[number]
+
+    def late_landed(number):
+        return n_one.at[pl.ds(pl.multiple_of((6 + number) * TILE, TILE), TILE)]
+
+    def crossed(which, number):
+        at = pl.multiple_of((4 + number) * TILE, TILE)
+        return n_one.at[pl.ds(at, TILE)] if which else y_in.at[number]
+
+    def to_mate(which, number, late=False):
         return pltpu.make_async_remote_copy(
             src_ref=rs_out.at[lax.rem(number, 2)],
-            dst_ref=rs_in.at[number],
+            dst_ref=late_landed(number - 2) if late else landed(which, number),
             send_sem=rs_send.at[which, number],
             recv_sem=rs_recv.at[which, number],
             device_id={"tensor": mate},
@@ -758,8 +778,8 @@
 
     def to_peer(which, number):
         return pltpu.make_async_remote_copy(
-            src_ref=rs_in.at[number],
-            dst_ref=y_in.at[number],
+            src_ref=landed(which, number),
+            dst_ref=crossed(which, number),
             send_sem=rs_send.at[which, 4 + number],
             recv_sem=rs_recv.at[which, 4 + number],
             device_id={"tensor": peer},
@@ -780,29 +800,33 @@
                 rs_out[number, :, columns] = part.astype(BF)
 
             compute(row0, put)
-            to_mate(which, at).start()
+            if which:
+                to_mate(which, at).start()
+            else:
+                pl.when(j < 2)(lambda: to_mate(0, at).start())
+                pl.when(j >= 4)(lambda: to_mate(0, at, True).start())
 
         @pl.when(lax.div(j, 2) == 1)
         def _():
             to_mate(which, number).wait_recv()
 
+            here = landed(which, number)
+
             def put(columns, part):
-                rs_in[number, :, columns] = (rs_in[number, :, columns].astype(F32) + part).astype(BF)
+                here[:, columns] = (here[:, columns].astype(F32) + part).astype(BF)
 
             compute(row0, put)
             to_peer(which, number).start()
 
     def gathered(which, number):
-        to_mate(which, 2 + number).wait_recv()
+        to_mate(which, 2 + number, not which).wait_recv()
         to_peer(which, number).wait_recv()
 
-    def settle(which):
-        for number in range(2):
-            to_mate(which, 2 + number).wait_send()
-            to_peer(which, number).wait_send()
-
-    def stored(number, target):
-        return pltpu.make_async_copy(rs_out.at[number], target, result_sem.at[number])
+    def stored(which, number):
+        result = input_grad if which else mixed_out
+        here = rs_out.at[number] if which else late_landed(number)
+        target = result.at[pl.ds(pl.multiple_of(number * TILE, TILE), TILE)]
+        return pltpu.make_async_copy(here, target, result_sem.at[which, number])
 
     pltpu.make_async_copy(tok.at[pl.ds(0, rows)], tok_kept, tok_sem.at[0]).wait()
     for piece in range(g_tok.pieces):
@@ -829,29 +853,33 @@
             lax.fori_loop(first, last, mix, 0)
 
     pairs = chunks // 2
+    tiles = rows // TILE
     with jax.named_scope("grad_down"):
+        lax.fori_loop(tiles - 4, tiles - 2, attend, 0)
         arrive(0)
+        down(0)
+        lax.fori_loop(tiles - 2, tiles, attend, 0)
         arrive(1)
-        down(0)
+        run_ticks(0, 2)
         down(1)
     mix_some(0, pairs // 4)
-    run_ticks(0, 1)
+    run_ticks(2, 4)
     arrive(2)
     mix_some(pairs // 4, pairs // 2)
-    run_ticks(1, 3)
+    run_ticks(4, 5)
     with jax.named_scope("grad_down"):
         down(2)
-
-    run_ticks(3, 5)
+    run_ticks(5, 7)
     mix_some(pairs // 2, 3 * pairs // 4)
-    run_ticks(5, 7)
+    run_ticks(7, 8)
     arrive(3)
     mix_some(3 * pairs // 4, pairs)
+    run_ticks(8, 10)
     with jax.named_scope("grad_down"):
         down(3)
-    run_ticks(7, 9)
+    run_ticks(10, 12)
     keep_unit(first_out, dot(mixed[...], cot[...], TN).astype(BF))
-    run_ticks(9, 11)
+    run_ticks(12, 14)
 
     column_tiles = [slice(at, at + TILE) for at in range(0, cot.shape[1], TILE)]
 
@@ -867,35 +895,13 @@
 
         return put
 
-    def own_copy(number, back=False):
-        held = own_part.at[pl.ds(pl.multiple_of(number * TILE, TILE), TILE)]
-        if back:
-            return pltpu.make_async_copy(held, temp.at[number], temp_sem.at[number])
-        return pltpu.make_async_copy(temp.at[0], held, temp_sem.at[0])
-
     def produce(j, carry):
-        @pl.when(j >= 2)
-        def _():
-            scatter(j - 2, 0, branch)
-
-        @pl.when(j < 2)
-        def _():
-            branch(pl.multiple_of(me * rows_own + j * TILE, TILE), keep_temp(0))
-            own_copy(j).start()
-            own_copy(j).wait()
-
-        pl.when(j == 1)(lambda: slope_copy(0, True).start())
-        pl.when(j == 2)(lambda: slope_copy(1, True).start())
-        tick_at(j, 2, 11)
-
+        scatter(j, 0, branch)
+        run_ticks(14 + j, 15 + j)
         return carry
 
     with jax.named_scope("outputs"):
-        lax.fori_loop(0, 8, produce, 0)
-    bring_up = pltpu.make_async_copy(
-        grads.at[pl.ds(rows, 2 * rows_own)], hid.at[pl.ds(chip_row, 2 * rows_own)], tok_sem.at[0]
-    )
-    bring_up.start()
+        lax.fori_loop(0, 4, produce, 0)
 
     def descend(p, carry):
         here = [pl.ds(pl.multiple_of(owner * rows_own + p * PIECE, PIECE), PIECE) for owner in (peer, cross)]
@@ -904,21 +910,18 @@
         turned = wide([cot[at, :] for at in here], 0)
         for at in range(0, hid.shape[1], TILE):
             d_hidden = dot(turned, w_down[at : at + TILE, :], NT)
-            d_up = (d_hidden * temp[parity, :, at : at + TILE]).astype(BF)
+            value = (d_hidden * temp[parity, :, at : at + TILE]).astype(BF)
             for k, rows_at in enumerate(here):
-                hid[rows_at, at : at + TILE] = d_up[k * PIECE : (k + 1) * PIECE]
+                d_up[rows_at, at : at + TILE] = value[k * PIECE : (k + 1) * PIECE]
         pl.when(p < 2)(lambda: slope_copy(p + 2, True).start())
-        tick_at(p, 2, 15)
         return carry
 
     with jax.named_scope("grad_gelu"):
         lax.fori_loop(0, 4, descend, 0)
-    bring_up.wait()
-
     def upward(j, carry):
         at = pl.ds(pl.multiple_of(j * TILE, TILE), TILE)
-        keep_unit(first_up + per_tile * j, dot(n_two[:, at], hid[...], TN).astype(BF))
-        run_ticks(17 + j, 18 + j)
+        keep_unit(first_up + per_tile * j, dot(n_two[:, at], d_up[...], TN).astype(BF))
+        run_ticks(18 + j, 19 + j)
         return carry
 
     with jax.named_scope("grad_up"):
@@ -930,7 +933,7 @@
 
     def unmix(step, carry):
         pair = chunks // 2 - 1 - step
-        diag = diag_two[0:width, :].astype(F32)
+        diag = diagonal[...].astype(F32)
         row_pair = pl.multiple_of(pair * 2 * CHUNK, 2 * CHUNK)
         d_mixed = dot(cot[pl.ds(row_pair, 2 * CHUNK), :], w_out[...], NT)
         here = chunk_rows(pair)
@@ -942,9 +945,9 @@
                 [packed[:, h // 2 * HEAD_DIM // 2 : (h // 2 + 1) * HEAD_DIM // 2] for h in range(2 * heads)]
             )
             d_over.append(d_mixed[c * CHUNK : (c + 1) * CHUNK] * inverse)
-            under_parts.append(wide(split(d_over[c] * att[here[c], :])))
-        d_under = [-dot(under_parts[c], diag_two[...]) for c in both_chunks]
-        under_row = [-dot(wide([head_rows, head_rows]), under_parts[c], NT) for c in both_chunks]
+            under_parts.append(split(d_over[c] * att[here[c], :]))
+        d_under = [-dot(part[0], diagonal[...]) - dot(part[1], diagonal[...]) for part in under_parts]
+        under_row = [-dot(head_rows, under_parts[c][0], NT) - dot(head_rows, under_parts[c][1], NT) for c in both_chunks]
         over_split = [split(d_over[c]) for c in both_chunks]
         over_both = [wide(over_split[c]) for c in both_chunks]
         over_heads = [wide([per_head(part) for part in over_split[c]]) for c in both_chunks]
@@ -990,7 +993,7 @@
             query_k, key_k, value_k, both_k, under_k = (
                 halves(field[c])[k] for field in (query, key, value, over_both, d_under)
             )
-            carried = wide([states[block]] * heads, 0) * diag_two[0:width, :]
+            carried = wide([states[block]] * heads, 0) * diagonal[...]
             keep = joined(block + 1)
             later, later_row = later * keep, later_row * keep
             high, low = split(later)
@@ -1012,35 +1015,35 @@
             feat_sums[0:1, :] += jnp.sum(grad * spectrum, 0, keepdims=True)
             feat_sums[1:2, :] += jnp.sum(grad, 0, keepdims=True)
             high, low = split(grad * scale_row)
-            back = dot(high, dct[:, 0:width]) + dot(low, dct[:, 0:width]) + dot(high, dct[:, 2 * width :])
+            back = dot(high, dct[:, 0:width]) + dot(low, dct[:, 0:width]) + dot(high, dct[:, width:])
             fqkv[here, s * width : (s + 1) * width] = rotate(back, turn, True).astype(BF)
         d_value = wide([d_value[c][:, :width] + d_value[c][:, width:] for c in both_chunks], 0)
         fqkv[here, 2 * width : 3 * width] = (d_value + wide([more[at][2] for at in range(4)], 0)).astype(BF)
-        run_ticks(21 + lax.div(15 * step, chunks // 2), 21 + lax.div(15 * (step + 1), chunks // 2))
+        run_ticks(22 + lax.div(14 * step, chunks // 2), 22 + lax.div(14 * (step + 1), chunks // 2))
 
         return carry
 
     with jax.named_scope("mixer_back"):
         lax.fori_loop(0, chunks // 2, unmix, 0)
 
-    def own_tok(number):
-        return pltpu.make_async_copy(tok_in.at[pl.ds(number * TILE, TILE)], rs_out.at[number], result_sem.at[number])
-
-    settle(0)
-    for number in range(2):
-        own_copy(number, True).start()
-        own_tok(number).start()
-
-    for j in range(n_one.shape[1] // TILE):
-        tile = dot(n_one[:, j * TILE : (j + 1) * TILE], fqkv[...], TN).astype(BF)
+    def projected(j, carry):
+        tile = dot(n_one[:, pl.ds(pl.multiple_of(j * TILE, TILE), TILE)], fqkv[...], TN).astype(BF)
         for s in range(3):
             at = 3 * j + s
-            first = plain * UNIT + at // 4 * TILE
-            grads[first : first + TILE, at % 4 * width : (at % 4 + 1) * width] = tile[:, s * width : (s + 1) * width]
-        if j:
+            first = pl.multiple_of(plain * UNIT + lax.div(at, 4) * TILE, TILE)
+            columns = pl.ds(pl.multiple_of(lax.rem(at, 4) * width, width), width)
+            grads[pl.ds(first, TILE), columns] = tile[:, s * width : (s + 1) * width]
+
+        @pl.when(j >= 1)
+        def _():
             ready(plain + (j - 1) * per_tile, per_tile)
 
-
+        return carry
+
+    with jax.named_scope("grad_qkv"):
+        lax.fori_loop(0, n_one.shape[1] // TILE, projected, 0)
+    pl.semaphore_signal(free_mate, inc=1, device_id={"tensor": mate}, device_id_type=MESH)
+    pl.semaphore_signal(free_peer, inc=1, device_id={"tensor": peer}, device_id_type=MESH)
     run_ticks(36, 38)
 
     sums[...] = jnp.zeros_like(sums)
@@ -1060,7 +1063,7 @@
             here = pl.ds(row0, TILE)
             unit, _ = unit_rows(n_two[pl.ds(pl.multiple_of(lax.rem(j, 2) * TILE, TILE), TILE), :].astype(F32))
             fields = [fqkv[here, s * width : (s + 1) * width] for s in range(3)]
-            right = hid[here, :]
+            right = d_up[here, :]
             for columns in column_tiles:
                 one = sum(dot(fields[s], w_qkv[s, columns, :], NT) for s in range(3))
                 two = dot(right, w_up[columns, :], NT)
@@ -1071,30 +1074,37 @@
 
         return compute
 
-    def finish(number, carry):
-        own_copy(number, True).wait()
-        own_tok(number).wait()
+    tok_copy(0).start()
+
+    def own_tok(number):
+        here = n_two.at[pl.ds((2 + number) * TILE, TILE)]
+        return pltpu.make_async_copy(tok_in.at[pl.ds(number * TILE, TILE)], here, local_sem.at[number])
+
+    for number in range(2):
+        own_tok(number).start()
+
+    def finish(number):
         gathered(0, number)
-
-        def step(i, inner):
-            at = pl.ds(pl.multiple_of(i * SUB, SUB), SUB)
-            total = temp[number, at, :] + rs_in[2 + number, at, :].astype(F32) + y_in[number, at, :].astype(F32)
-            rs_out[number, at, :] = (total + rs_out[number, at, :].astype(F32)).astype(BF)
-            return inner
-
-        lax.fori_loop(0, TILE // SUB, step, 0)
-        stored(number, mixed_out.at[pl.ds(pl.multiple_of(number * TILE, TILE), TILE)]).start()
-        return carry
-
-    with jax.named_scope("finish"):
-        lax.fori_loop(0, 2, finish, 0)
-    pl.semaphore_signal(free_mate, inc=1, device_id={"tensor": mate}, device_id_type=MESH)
-    pl.semaphore_signal(free_peer, inc=1, device_id={"tensor": peer}, device_id_type=MESH)
-    tok_copy(0).start()
-    for number in range(2):
-        stored(number, mixed_out.at[pl.ds(0, TILE)]).wait()
+        tokens, result = n_two.at[pl.ds((2 + number) * TILE, TILE)], late_landed(number)
+
+        def put(columns, part):
+            total = part + result[:, columns].astype(F32) + y_in[number, :, columns].astype(F32)
+            result[:, columns] = (total + tokens[:, columns].astype(F32)).astype(BF)
+
+        branch(pl.multiple_of(me * rows_own + number * TILE, TILE), put)
+        stored(0, number).start()
+
     pl.semaphore_wait(free_mate, 1)
     pl.semaphore_wait(free_peer, 1)
+
+    def produce_late(j, carry):
+        scatter(j, 0, branch)
+        return carry
+
+    with jax.named_scope("outputs"):
+        lax.fori_loop(4, 6, produce_late, 0)
+    for number in range(2):
+        to_mate(0, 2 + number, True).wait_send()
 
     def inputs(j, carry):
         tok_copy(j).wait()
@@ -1113,27 +1123,24 @@
 
     with jax.named_scope("row_grads"):
         lax.fori_loop(0, 8, inputs, 0)
-    settle(1)
-    for number in range(2):
-        own_tok(number).start()
-
     def conclude(number):
-        own_tok(number).wait()
         gathered(1, number)
+        tokens = n_two.at[pl.ds((2 + number) * TILE, TILE)]
+        from_mate, from_peer = landed(1, 2 + number), crossed(1, number)
 
         def step(i, inner):
-            at = pl.ds(pl.multiple_of(i * SUB, SUB), SUB)
-            group_at = pl.multiple_of(me * rows_own + number * TILE + i * SUB, SUB)
-            unit, deviation = unit_rows(rs_out[number, at, :].astype(F32))
-            total = temp[number, at, :] + rs_in[2 + number, at, :].astype(F32) + y_in[number, at, :].astype(F32)
+            at = pl.ds(pl.multiple_of(i * PIECE, PIECE), PIECE)
+            group_at = pl.multiple_of(me * rows_own + number * TILE + i * PIECE, PIECE)
+            unit, deviation = unit_rows(tokens[at, :].astype(F32))
+            total = temp[number, at, :] + from_mate[at, :].astype(F32) + from_peer[at, :].astype(F32)
             along = jnp.mean(total * unit, -1, keepdims=True)
             total = total - jnp.mean(total, -1, keepdims=True) - unit * along
-            total = cot[pl.ds(group_at, SUB), :].astype(F32) + deviation * total
+            total = cot[pl.ds(group_at, PIECE), :].astype(F32) + deviation * total
             rs_out[number, at, :] = total.astype(BF)
             return inner
 
-        lax.fori_loop(0, TILE // SUB, step, 0)
-        stored(number, input_grad.at[pl.ds(number * TILE, TILE)]).start()
+        lax.fori_loop(0, TILE // PIECE, step, 0)
+        stored(1, number).start()
 
     small[...] = jnp.zeros_like(small)
     for number in range(4):
@@ -1183,16 +1190,21 @@
                 total = total + small_wide[member]
             small[...] = total
 
+    for number in range(2):
+        to_mate(1, 2 + number).wait_send()
+        own_tok(number).wait()
     small_step(0)
-    run_ticks(54, 55)
+    run_ticks(54, 56)
+    finish(0)
+    small_step(1)
+    run_ticks(56, 58)
+    finish(1)
     conclude(0)
-    small_step(1)
-    run_ticks(55, 56)
+    run_ticks(58, 60)
     conclude(1)
-    run_ticks(56, 57)
     small_step(2)
     if reduce_dp:
-        run_ticks(57, ticks)
+        run_ticks(60, ticks)
     for h in range(heads):
         at = slice(h * HEAD_DIM, (h + 1) * HEAD_DIM)
         feat_out[0, h : h + 1, :] = small[4:5, at]
@@ -1201,7 +1213,10 @@
     pltpu.make_async_copy(grads.at[pl.ds(0, plain * UNIT)], grads_out, grad_sem.at[0]).wait()
     pltpu.make_async_copy(w_qkv, qkv_out, grad_sem.at[1]).wait()
     for number in range(2):
-        stored(number, input_grad.at[pl.ds(0, TILE)]).wait()
+        to_peer(0, number).wait_send()
+        to_peer(1, number).wait_send()
+        for which in range(2):
+            stored(which, number).wait()
 
     for gather in (g_tok, g_cot):
         gather.to_mate(me).wait_send()
@@ -1254,7 +1269,7 @@
     shape = jax.ShapeDtypeStruct
     plain = 2 * hidden + width
     units = (plain + 3 * width) // UNIT
-    mixed_out, input_grad, grads, g_qkv, _, _, _, small, feats = pl.pallas_call(
+    mixed_out, input_grad, grads, g_qkv, _, _, small, feats = pl.pallas_call(
         functools.partial(kernel, reduce_dp),
         out_shape=(
             shape((rows_own, model), BF),
@@ -1262,17 +1277,17 @@
             shape((plain, model), BF),
             shape((3, model, width), BF),
             shape((rows // 2, hidden), F32),
-            shape((rows_own, model), F32),
             shape((rows, model), BF),
             shape((8, model), F32),
             shape((2, heads, HEAD_DIM), F32),
         ),
         in_specs=[smem, anywhere, anywhere] + [vmem] * 4 + [anywhere] * 4 + [vmem] * 6,
-        out_specs=(anywhere,) * 7 + (vmem, vmem),
+        out_specs=(anywhere,) * 6 + (vmem, vmem),
         scratch_shapes=[
             pltpu.VMEM((rows, model), BF),
             pltpu.VMEM((rows, model), BF),
             pltpu.VMEM((rows, model), BF),
+            pltpu.VMEM((rows, hidden), BF),
             pltpu.VMEM((rows, hidden), BF),
             pltpu.VMEM((rows, 3 * width), BF),
             pltpu.VMEM((2, rows, width), F32),
@@ -1287,7 +1302,7 @@
             pltpu.VMEM((BOXES_X, 2 * UNIT, model), BF),
             pltpu.VMEM((BOXES_Z, 5 * UNIT // 2, model), BF),
             pltpu.VMEM((2, TILE, model), BF),
-            pltpu.VMEM((4, TILE, model), BF),
+            pltpu.VMEM((2, TILE, model), BF),
             pltpu.VMEM((2, TILE, model), BF),
             pltpu.VMEM((2, TILE, model), F32),
             pltpu.VMEM((4, 8, model), F32),
@@ -1311,7 +1326,7 @@
             pltpu.SemaphoreType.DMA((2,)),
             pltpu.SemaphoreType.DMA((2,)),
             pltpu.SemaphoreType.DMA((2,)),
-            pltpu.SemaphoreType.DMA((2,)),
+            pltpu.SemaphoreType.DMA((2, 2)),
             pltpu.SemaphoreType.REGULAR,
             pltpu.SemaphoreType.REGULAR,
         ],

time: 197 us -> 197 us (level)
  no operation moved by 1% of the time
where the time goes in v6:
time: 197 us; the launch traced here: 196 us
  Pallas kernels  195 us (99%)
    pallas_call x1, Pallas kernels, shards(): pl.pallas_call(functools.partial(kernel, reduce_dp), out_shape=(shape((ro...  186 us
    pallas_call x1, Pallas kernels, shards(): pl.pallas_call(widen, grid=(steps,), out_shape=(shape((hidden, model), F3...  9.39 us

profile of v6, /device:TPU:0, one launch (start us, length us, event | category | flops | bytes accessed | tf_op | source)
XLA Modules:
  0.0 196.3 jit_solution(4796815920838869734)
XLA Ops:
  0.6 186.1 %shard_map.256 = (bf16[512,1024]{1,0:T(8,128)(2,1)}, bf16[512,1024]{1,0:T(8,128)(2,1)}, bf16[2304,1024]{1,0:T(8,128)(2,1)}, bf16[3,1024,256]{2,1,0:T(8,128)(2,1)...) custom-call(s32[1,3]{1,0:T(1,128)} %lengths.1, ...), custom_call_target="tpu_custom_call" | custom-call | tf_op jit(solution)/shard_map/pallas_call | solution.py:1272
  186.8 9.4 %shard_map.257 = (f32[1024,1024]{1,0:T(8,128)}, f32[256,1024]{1,0:T(8,128)}, f32[1024,1024]{1,0:T(8,128)}, f32[3,1024,256]{2,1,0:T(8,128)}, f32[1,1024]{1,0:T(1,...) custom-call(bf16[2304,1024]{1,0:T(8,128)(2,1)} %get-tuple-element.30, ...), custom_call_target="tpu_custom_call" | custom-call | tf_op jit(solution)/shard_map/pallas_call | solution.py:1348

commit v7 on v6

--- a/solution.py
+++ b/solution.py
@@ -167,7 +167,7 @@
 
     side = jnp.where(along_z < 2, 0, 1)
     inward = group + 2 - 4 * side
-    outward = group - 2 + 4 * side
+    outward = jnp.where(middle == 0, inward, group - 2 + 4 * side)
     units = grads.shape[0] // UNIT
 
     weight_copies = [
@@ -532,6 +532,7 @@
 
     def advance(n, stage):
         kind = jnp.where(n < 0, 2, jnp.where(n >= units, 2, kind_of(n)))
+        n = jnp.where(kind == 2, 0, n)
         code = 4 * kind + middle
         place, place_b = box_of(n)
 

time: 197 us -> 197 us (level)
  no operation moved by 1% of the time
where the time goes in v7:
time: 197 us
  Pallas kernels  196 us (99%)
    pallas_call x1, Pallas kernels, shards(): pl.pallas_call(functools.partial(kernel, reduce_dp), out_shape=(shape((ro...  187 us
    pallas_call x1, Pallas kernels, shards(): pl.pallas_call(widen, grid=(steps,), out_shape=(shape((hidden, model), F3...  9.39 us

profile of v7, /device:TPU:0, one launch (start us, length us, event | category | flops | bytes accessed | tf_op | source)
XLA Modules:
  0.0 196.8 jit_solution(14818308301539132274)
XLA Ops:
  0.6 186.5 %shard_map.256 = (bf16[512,1024]{1,0:T(8,128)(2,1)}, bf16[512,1024]{1,0:T(8,128)(2,1)}, bf16[2304,1024]{1,0:T(8,128)(2,1)}, bf16[3,1024,256]{2,1,0:T(8,128)(2,1)...) custom-call(s32[1,3]{1,0:T(1,128)} %lengths.1, ...), custom_call_target="tpu_custom_call" | custom-call | tf_op jit(solution)/shard_map/pallas_call | solution.py:1273
  187.2 9.4 %shard_map.257 = (f32[1024,1024]{1,0:T(8,128)}, f32[256,1024]{1,0:T(8,128)}, f32[1024,1024]{1,0:T(8,128)}, f32[3,1024,256]{2,1,0:T(8,128)}, f32[1,1024]{1,0:T(1,...) custom-call(bf16[2304,1024]{1,0:T(8,128)(2,1)} %get-tuple-element.30, ...), custom_call_target="tpu_custom_call" | custom-call | tf_op jit(solution)/shard_map/pallas_call | solution.py:1349
